TPU v7x, 32 devices: a whole 2x2x4 slice. The times are simulated.
32 devices in a mesh: grp: 1, dap: 32 (over z, y, x, core), ch: 1.
Axes of the slice: x: 2, y: 2, z: 4, core: 2. Of those that a mesh axis runs over, the one named last changes fastest.
Arguments:
- pair_act: bfloat16 [128, 128, 128], P(('grp', 'dap')), may hold values from -24 to 24
- out_grad: bfloat16 [128, 128, 128], P(('grp', 'dap'), 'ch'), may hold values from -6 to 6
- residue_mask: int32 [128], P('grp'), may hold values 0 or 1
- ln_in_gain: float32 [128], replicated, may hold values from 0.1 to 1.9
- ln_in_bias: float32 [128], replicated, may hold values from -3 to 3
- w_a_proj: bfloat16 [128, 128], P(None, 'ch'), may hold values from -4 to 4
- w_a_gate: bfloat16 [128, 128], P(None, 'ch'), may hold values from -0.5 to 0.5
- w_b_proj: bfloat16 [128, 128], P(None, 'ch'), may hold values from -0.5 to 0.5
- w_b_gate: bfloat16 [128, 128], P(None, 'ch'), may hold values from -0.5 to 0.5
- w_gate: bfloat16 [128, 128], replicated, may hold values from -0.5 to 0.5
- ln_out_gain: float32 [128], replicated, may hold values from 0.1 to 1.9
- ln_out_bias: float32 [128], replicated, may hold values from -4 to 4
- w_out: bfloat16 [128, 128], replicated, may hold values from -0.5 to 0.5
Outputs:
- pair_grad: bfloat16 [128, 128, 128], P(('grp', 'dap'), 'ch')
All inputs are finite; a program needn't handle non-finite values.
Results may differ from a plain program's by a relative error of at most 0.009.
Values may be sent and summed in bfloat16 or wider, within the bound.
No kernel may reach another device: no remote copies, remote signals or barrier semaphores. Data moves between devices by JAX's collectives and lax.ppermute only.
A program may use at most 128 MiB of HBM per device.

v0:
```python
import functools

import jax
import jax.numpy as jnp
from jax import lax
from jax.experimental import pallas as pl
from jax.experimental.pallas import tpu as pltpu
from jax.sharding import PartitionSpec as P

EPSILON = 1e-05


def normalise(values, reduce_dim):
    centre = values - jnp.mean(values, axis=reduce_dim, keepdims=True)
    inverse = lax.rsqrt(jnp.mean(centre * centre, axis=reduce_dim, keepdims=True) + EPSILON)
    return (centre * inverse, inverse)


def norm_backward(grad_hat, normed, inverse, reduce_dim):
    mean_grad = jnp.mean(grad_hat, axis=reduce_dim, keepdims=True)
    mean_proj = jnp.mean(grad_hat * normed, axis=reduce_dim, keepdims=True)
    return inverse * (grad_hat - mean_grad - normed * mean_proj)


def channel_shards(
    dap,
    ch,
    pair_act,
    out_grad,
    residue_mask,
    ln_in_gain,
    ln_in_bias,
    w_a_proj,
    w_a_gate,
    w_b_proj,
    w_b_gate,
    w_gate,
    ln_out_gain,
    ln_out_bias,
    w_out,
):
    own_rows, all_cols = pair_act.shape[:2]
    col_span = out_grad.shape[1]
    hidden_local = w_a_proj.shape[1]
    slice_h = hidden_local // dap
    row_first = lax.axis_index("dap") * own_rows
    col_first = lax.axis_index("ch") * col_span
    normed_in, rstd_in = normalise(pair_act.astype(jnp.float32), 2)
    pair_norm = (normed_in * ln_in_gain + ln_in_bias).astype(jnp.bfloat16)
    valid_all = residue_mask.astype(jnp.float32)
    valid_rows = lax.dynamic_slice_in_dim(valid_all, row_first, own_rows)
    row_mask = (valid_rows[:, None] * valid_all[None, :])[None]
    w_four = jnp.concatenate((w_a_proj, w_a_gate, w_b_proj, w_b_gate), axis=1)
    projected = jnp.einsum("ikc,cg->gik", pair_norm, w_four, preferred_element_type=jnp.float32)
    a_proj = projected[:hidden_local]
    a_sig = jax.nn.sigmoid(projected[hidden_local : 2 * hidden_local])
    b_proj = projected[2 * hidden_local : 3 * hidden_local]
    b_sig = jax.nn.sigmoid(projected[3 * hidden_local :])
    edge_a = (row_mask * a_sig * a_proj).astype(jnp.bfloat16)
    edge_b = (row_mask * b_sig * b_proj).astype(jnp.bfloat16)

    split = (dap, slice_h, own_rows, all_cols)
    edges = jnp.stack((edge_a.reshape(split), edge_b.reshape(split)), axis=1)
    edges = lax.all_to_all(edges, "dap", split_axis=0, concat_axis=0, tiled=True)
    edges = jnp.transpose(edges, (1, 2, 0, 3, 4)).reshape(2, slice_h, dap * own_rows, all_cols)
    a_all, b_all = edges[0], edges[1]
    tri = jnp.einsum("hik,hjk->hij", a_all, b_all, preferred_element_type=jnp.float32).astype(
        jnp.bfloat16
    )
    tri = tri.reshape(slice_h, dap, own_rows, ch, col_span)
    tri = jnp.transpose(tri, (1, 3, 0, 2, 4)).reshape(dap * ch, slice_h, own_rows, col_span)
    tri = lax.all_to_all(tri, ("dap", "ch"), split_axis=0, concat_axis=0, tiled=True)
    tri = tri.reshape(dap, ch, slice_h, own_rows, col_span)
    tri_full = jnp.transpose(tri, (1, 0, 2, 3, 4)).reshape(-1, own_rows, col_span)

    normed_out, rstd_out = normalise(tri_full.astype(jnp.float32), 0)
    gain_out = ln_out_gain.reshape(-1, 1, 1)
    bias_out = ln_out_bias.reshape(-1, 1, 1)
    tri_norm = (normed_out * gain_out + bias_out).astype(jnp.bfloat16)
    proj_out = jnp.einsum("hij,hc->ijc", tri_norm, w_out, preferred_element_type=jnp.float32)
    norm_cols = lax.dynamic_slice_in_dim(pair_norm, col_first, col_span, 1)
    gate_act = jax.nn.sigmoid(
        jnp.einsum("ijc,cd->ijd", norm_cols, w_gate, preferred_element_type=jnp.float32)
    )
    upstream = out_grad.astype(jnp.float32)
    d_proj = (upstream * gate_act).astype(jnp.bfloat16)
    d_gate = (upstream * proj_out * gate_act * (1.0 - gate_act)).astype(jnp.bfloat16)
    d_normed = (
        jnp.einsum("ijc,hc->hij", d_proj, w_out, preferred_element_type=jnp.float32) * gain_out
    )
    d_tri = norm_backward(d_normed, normed_out, rstd_out, 0).astype(jnp.bfloat16)

    d_tri = d_tri.reshape(ch, dap, slice_h, own_rows, col_span)
    d_tri = jnp.transpose(d_tri, (1, 0, 2, 3, 4)).reshape(dap * ch, slice_h, own_rows, col_span)
    d_tri = lax.all_to_all(d_tri, ("dap", "ch"), split_axis=0, concat_axis=0, tiled=True)
    d_tri = d_tri.reshape(dap, ch, slice_h, own_rows, col_span)
    d_tri = jnp.transpose(d_tri, (2, 0, 3, 1, 4)).reshape(slice_h, dap * own_rows, all_cols)
    d_edge_a = jnp.einsum("hij,hjk->hik", d_tri, b_all, preferred_element_type=jnp.float32)
    d_edge_b = jnp.einsum("hij,hik->hjk", d_tri, a_all, preferred_element_type=jnp.float32)
    d_edges = jnp.stack((d_edge_a, d_edge_b)).astype(jnp.bfloat16)
    d_edges = d_edges.reshape(2, slice_h, dap, own_rows, all_cols)
    d_edges = jnp.transpose(d_edges, (2, 0, 1, 3, 4))
    d_edges = lax.all_to_all(d_edges, "dap", split_axis=0, concat_axis=0, tiled=True)
    d_edges = jnp.transpose(d_edges, (1, 0, 2, 3, 4)).reshape(2, hidden_local, own_rows, all_cols)

    def split_grad(d_edge, sig_val, proj_val):
        masked = d_edge * row_mask
        return (
            (masked * sig_val).astype(jnp.bfloat16),
            (masked * proj_val * sig_val * (1.0 - sig_val)).astype(jnp.bfloat16),
        )

    d_four = jnp.concatenate(
        split_grad(d_edges[0].astype(jnp.float32), a_sig, a_proj)
        + split_grad(d_edges[1].astype(jnp.float32), b_sig, b_proj),
        axis=0,
    )
    d_hidden = jnp.einsum("gik,cg->ikc", d_four, w_four, preferred_element_type=jnp.float32)
    if ch > 1:
        d_hidden = lax.psum_scatter(
            d_hidden.astype(jnp.bfloat16), "ch", scatter_dimension=1, tiled=True
        ).astype(jnp.float32)
    d_pair_norm = d_hidden + jnp.einsum(
        "ijd,cd->ijc", d_gate, w_gate, preferred_element_type=jnp.float32
    )
    normed_cols = lax.dynamic_slice_in_dim(normed_in, col_first, col_span, 1)
    rstd_cols = lax.dynamic_slice_in_dim(rstd_in, col_first, col_span, 1)
    grad_hat = d_pair_norm * ln_in_gain
    return norm_backward(grad_hat, normed_cols, rstd_cols, 2).astype(jnp.bfloat16)


F32 = jnp.float32
BF16 = jnp.bfloat16
SUBLANES = 8


def dot(lhs, rhs, lhs_dim, rhs_dim):
    return lax.dot_general(
        lhs, rhs, (((lhs_dim,), (rhs_dim,)), ((), ())), preferred_element_type=F32
    )


def across(row, count):
    return jnp.transpose(jnp.broadcast_to(row, (count, row.shape[1])))


def normed_rows(act):
    centre = act - jnp.mean(act, axis=1, keepdims=True)
    return centre * lax.rsqrt(jnp.mean(centre * centre, axis=1, keepdims=True) + EPSILON)


def edges_kernel(me_ref, *refs):
    sources, (out_ref, *local), (wide, arrived) = refs[:9], refs[9:19], refs[19:]
    copies = [
        pltpu.make_async_copy(source, target, arrived.at[index])
        for index, (source, target) in enumerate(zip(sources, local))
    ]
    for copy in copies:
        copy.start()
    rows_ref, valid_ref, act_ref, gain_ref, bias_ref, *weights = local
    own, cols, _ = act_ref.shape
    devices, block, _ = out_ref.shape
    hidden = weights[0].shape[1]
    half = block // 2
    for copy in copies:
        copy.wait()
    valid = valid_ref[...].astype(F32)
    for r in range(own):
        normed = normed_rows(act_ref[r].astype(F32))
        pair_norm = (normed * gain_ref[...] + bias_ref[...]).astype(BF16)
        mask = valid * rows_ref[me_ref[0] * own + r].astype(F32)
        for side in range(2):
            proj = dot(weights[2 * side][...], pair_norm, 0, 1)
            sig = jax.nn.sigmoid(dot(weights[2 * side + 1][...], pair_norm, 0, 1))
            wide[side, pl.ds(r, hidden, stride=own), :] = mask * sig * proj
    for side in range(2):
        out_ref[:, side * half : (side + 1) * half, :] = (
            wide[side].reshape(devices, half, cols).astype(BF16)
        )


def gates_kernel(
    me_ref, rows_ref, valid_ref, act_ref, grad_ref, gain_ref, bias_ref, gain_out_ref,
    wap, wag, wbp, wbg, w_gate, w_out, factors, normed_t, rstd_t, gain_t, d_normed, slope,
):
    own, cols, _ = act_ref.shape
    hidden = wap.shape[1]
    valid = valid_ref[...].astype(F32)
    gain = across(gain_ref[...], cols)
    bias = across(bias_ref[...], cols)
    gain_out = across(gain_out_ref[...], cols)
    gain_t[...] = gain
    for r in range(own):
        act = jnp.transpose(act_ref[r].astype(F32))
        centre = act - jnp.mean(act, axis=0, keepdims=True)
        inverse = lax.rsqrt(jnp.mean(centre * centre, axis=0, keepdims=True) + EPSILON)
        normed = centre * inverse
        normed_t[r] = normed
        rstd_t[r] = inverse
        pair_norm = (normed * gain + bias).astype(BF16)
        mask = valid * rows_ref[me_ref[0] * own + r].astype(F32)
        for side, (w_proj, w_sig) in enumerate(((wap, wag), (wbp, wbg))):
            proj = dot(w_proj[...], pair_norm, 0, 0)
            sig = jax.nn.sigmoid(dot(w_sig[...], pair_norm, 0, 0))
            kept = mask * sig
            factors[2 * side, r] = kept
            factors[2 * side + 1, r] = kept * proj * (1.0 - sig)
        gate_act = jax.nn.sigmoid(dot(pair_norm, w_gate[...], 0, 0))
        d_proj = grad_ref[r].astype(F32) * gate_act
        slope[r] = d_proj * (1.0 - gate_act)
        d_normed[pl.ds(r, hidden, stride=own), :] = (
            dot(w_out[...], d_proj.astype(BF16), 1, 1) * gain_out
        )


def triangle_kernel(in_ref, out_ref, a_ref, b_ref, wide, back):
    devices, block, cols = in_ref.shape
    slice_h, rows, _ = a_ref.shape
    half = block // 2
    own = half // slice_h
    for side in range(2):
        wide[side] = (
            in_ref[:, side * half : (side + 1) * half, :].astype(F32).reshape(devices * half, cols)
        )
    for c in range(slice_h):
        for r in range(own):
            at = pl.ds(c * own + r, devices, stride=half)
            a_ref[c, r * devices : (r + 1) * devices, :] = wide[0, at, :].astype(BF16)
            back[pl.ds(r, devices, stride=own), :] = wide[1, at, :]
        b_ref[c] = back[...].astype(BF16)
        tri = dot(a_ref[c], b_ref[c], 1, 1)
        for r in range(own):
            wide[0, pl.ds(c * own + r, devices, stride=half), :] = tri[
                r * devices : (r + 1) * devices
            ]
    out_ref[...] = wide[0].reshape(devices, half, cols).astype(BF16)


def fold(values, own):
    total = jnp.sum(values, axis=0)
    rows = total
    for shift in range(own, SUBLANES, own):
        rows = rows + pltpu.roll(total, shift, 0)
    return rows[None]


def tri_normed(tri_ref, hidden, own):
    cols = tri_ref.shape[-1]
    tri = tri_ref[...].astype(F32).reshape(hidden * own // SUBLANES, SUBLANES, cols)
    centre = tri - fold(tri, own) / hidden
    inverse = lax.rsqrt(fold(centre * centre, own) / hidden + EPSILON)
    return centre * inverse, inverse


def norm_kernel(hidden, tri_ref, grad_ref, out_ref):
    devices, block, cols = tri_ref.shape
    own = devices * block // hidden
    normed, inverse = tri_normed(tri_ref, hidden, own)
    grad = grad_ref[...].reshape(normed.shape)
    mean_grad = fold(grad, own) / hidden
    mean_proj = fold(grad * normed, own) / hidden
    d_tri = inverse * (grad - mean_grad - normed * mean_proj)
    out_ref[...] = d_tri.reshape(devices, block, cols).astype(BF16)


def gate_grad_kernel(tri_ref, slope, gain_ref, bias_ref, w_out, w_gate, out_ref, wide):
    own, cols, _ = slope.shape
    hidden = w_out.shape[0]
    normed, _ = tri_normed(tri_ref, hidden, own)
    wide[...] = normed.reshape(hidden * own, cols)
    gain = across(gain_ref[...], cols)
    bias = across(bias_ref[...], cols)
    for r in range(own):
        tri_norm = (wide[pl.ds(r, hidden, stride=own), :] * gain + bias).astype(BF16)
        proj_out = dot(tri_norm, w_out[...], 0, 0)
        d_gate = (slope[r] * proj_out).astype(BF16)
        out_ref[r] = dot(w_gate[...], d_gate, 1, 1)


def edge_grad_kernel(in_ref, a_ref, b_ref, out_ref, wide, whole):
    devices, block, cols = in_ref.shape
    slice_h, rows, _ = a_ref.shape
    own = block // slice_h
    wide[0] = in_ref[...].astype(F32).reshape(devices * block, cols)
    for c in range(slice_h):
        at = [pl.ds(c * own + r, devices, stride=block) for r in range(own)]
        d_tri = jnp.concatenate([wide[0, at[r], :] for r in range(own)], axis=0).astype(BF16)
        d_a = dot(d_tri, b_ref[c], 1, 0)
        whole[...] = dot(d_tri, a_ref[c], 0, 0)
        for r in range(own):
            wide[1, at[r], :] = d_a[r * devices : (r + 1) * devices]
            wide[2, at[r], :] = whole[pl.ds(r, devices, stride=own), :]
    for side in range(2):
        out_ref[:, side * block : (side + 1) * block, :] = (
            wide[1 + side].reshape(devices, block, cols).astype(BF16)
        )


def input_grad_kernel(in_ref, factors, normed_t, rstd_t, gain_t, gate_part, wap, wag, wbp, wbg, out_ref, wide):
    own, cols, _ = out_ref.shape
    devices, block, _ = in_ref.shape
    hidden = wap.shape[1]
    half = block // 2
    for side in range(2):
        wide[side] = (
            in_ref[:, side * half : (side + 1) * half, :].astype(F32).reshape(devices * half, cols)
        )
    for r in range(own):
        total = gate_part[r]
        for side, (w_proj, w_sig) in enumerate(((wap, wag), (wbp, wbg))):
            d_edge = wide[side, pl.ds(r, hidden, stride=own), :]
            total = total + dot(w_proj[...], (d_edge * factors[2 * side, r]).astype(BF16), 1, 0)
            total = total + dot(w_sig[...], (d_edge * factors[2 * side + 1, r]).astype(BF16), 1, 0)
        grad_hat = total * gain_t[...]
        normed = normed_t[r]
        mean_grad = jnp.mean(grad_hat, axis=0, keepdims=True)
        mean_proj = jnp.mean(grad_hat * normed, axis=0, keepdims=True)
        grad = rstd_t[r] * (grad_hat - mean_grad - normed * mean_proj)
        out_ref[r] = jnp.transpose(grad).astype(BF16)


VMEM = pl.BlockSpec(memory_space=pltpu.VMEM)
SMEM = pl.BlockSpec(memory_space=pltpu.SMEM)
HBM = pl.BlockSpec(memory_space=pltpu.HBM)


def wide(*shape):
    return pltpu.VMEM(shape, F32)


def call(kernel, name, outs, args, scratch=(), scalars=0, flops=0, space=VMEM, limit=32 * 2**20):
    shapes = [jax.ShapeDtypeStruct(shape, dtype) for shape, dtype in outs]
    moved = sum(value.size * value.dtype.itemsize for value in list(args) + shapes)
    result = pl.pallas_call(
        kernel,
        name=name,
        out_shape=shapes,
        in_specs=[SMEM] * scalars + [space] * (len(args) - scalars),
        out_specs=[VMEM] * len(outs),
        scratch_shapes=scratch,
        cost_estimate=pl.CostEstimate(flops=flops, bytes_accessed=moved, transcendentals=0),
        compiler_params=pltpu.CompilerParams(vmem_limit_bytes=limit),
    )(*args)
    return result[0] if len(outs) == 1 else result


def kernel_shards(
    dap,
    pair_act,
    out_grad,
    residue_mask,
    ln_in_gain,
    ln_in_bias,
    w_a_proj,
    w_a_gate,
    w_b_proj,
    w_b_gate,
    w_gate,
    ln_out_gain,
    ln_out_bias,
    w_out,
):
    own, cols, chan = pair_act.shape
    hidden = w_a_proj.shape[1]
    slice_h = hidden // dap
    rows = dap * own
    block = slice_h * own
    me = lax.axis_index("dap").reshape(1)
    valid = residue_mask.reshape(1, -1)
    gain_in, bias_in, gain_out, bias_out = (
        value.reshape(1, -1) for value in (ln_in_gain, ln_in_bias, ln_out_gain, ln_out_bias)
    )
    w_edges = (w_a_proj, w_a_gate, w_b_proj, w_b_gate)
    product = 2 * own * cols * chan * hidden

    def exchange(value):
        return lax.all_to_all(value, "dap", split_axis=0, concat_axis=0, tiled=True)

    first = (residue_mask, valid, pair_act, gain_in, bias_in, *w_edges)
    edges = call(
        edges_kernel,
        "edges",
        [((dap, 2 * block, cols), BF16)],
        (me, *first),
        scratch=[
            (pltpu.VMEM if index else pltpu.SMEM)(value.shape, value.dtype)
            for index, value in enumerate(first)
        ]
        + [wide(2, hidden * own, cols), pltpu.SemaphoreType.DMA((len(first),))],
        scalars=1,
        flops=4 * product,
        space=HBM,
        limit=None,
    )
    edges = exchange(edges)
    factors, normed_t, rstd_t, gain_t, d_normed, slope = call(
        gates_kernel,
        "gates",
        [
            ((4, own, hidden, cols), F32),
            ((own, chan, cols), F32),
            ((own, 1, cols), F32),
            ((chan, cols), F32),
            ((hidden * own, cols), F32),
            ((own, cols, chan), F32),
        ],
        (me, residue_mask, valid, pair_act, out_grad, gain_in, bias_in, gain_out)
        + (*w_edges, w_gate, w_out),
        scalars=2,
        flops=6 * product,
    )
    tri, edge_a, edge_b = call(
        triangle_kernel,
        "triangle",
        [
            ((dap, block, cols), BF16),
            ((slice_h, rows, cols), BF16),
            ((slice_h, rows, cols), BF16),
        ],
        (edges,),
        scratch=[wide(2, dap * block, cols), wide(rows, cols)],
        flops=product,
    )
    tri = exchange(tri)
    d_tri = call(
        functools.partial(norm_kernel, hidden),
        "norm",
        [((dap, block, cols), BF16)],
        (tri, d_normed),
    )
    d_tri = exchange(d_tri)
    gate_part = call(
        gate_grad_kernel,
        "gate_grad",
        [((own, chan, cols), F32)],
        (tri, slope, gain_out, bias_out, w_out, w_gate),
        scratch=[wide(hidden * own, cols)],
        flops=2 * product,
    )
    d_edges = call(
        edge_grad_kernel,
        "edge_grad",
        [((dap, 2 * block, cols), BF16)],
        (d_tri, edge_a, edge_b),
        scratch=[wide(3, dap * block, cols), wide(rows, cols)],
        flops=2 * product,
    )
    d_edges = exchange(d_edges)
    return call(
        input_grad_kernel,
        "input_grad",
        [((own, cols, chan), BF16)],
        (d_edges, factors, normed_t, rstd_t, gain_t, gate_part, *w_edges),
        scratch=[wide(2, hidden * own, cols)],
        flops=4 * product,
    )


def fits_kernels(dap, ch, pair_act, w_proj):
    own, cols, chan = pair_act.shape
    hidden = w_proj.shape[1]
    block = hidden // dap * own
    return (
        ch == 1
        and hidden % dap == 0
        and own in (1, 2, 4, 8)
        and block % 16 == 0
        and dap % SUBLANES == 0
        and cols == dap * own
        and cols % 128 == chan % 128 == hidden % 128 == 0
    )


def solution(mesh):
    sizes = dict(mesh.shape)

    def program(*args):
        dap, ch = sizes["dap"], sizes["ch"]
        if fits_kernels(dap, ch, args[0], args[5]):
            return kernel_shards(dap, *args)
        return channel_shards(dap, ch, *args)

    in_specs = (
        P(("grp", "dap"), None, None),
        P(("grp", "dap"), "ch", None),
        P("grp"),
        P(),
        P(),
        P(None, "ch"),
        P(None, "ch"),
        P(None, "ch"),
        P(None, "ch"),
        P(),
        P(),
        P(),
        P(),
    )
    out_specs = P(("grp", "dap"), "ch", None)
    return jax.shard_map(
        program, mesh=mesh, in_specs=in_specs, out_specs=out_specs, check_vma=False
    )
```

profile of v0, /device:TPU:0, one launch (start us, length us, event | category | flops | bytes accessed | tf_op | source)
XLA Modules:
  0.0 58.2 jit_solution(13388239141684546636)
XLA Ops:
  0.0 2.6 %edges.1 = bf16[32,32,128]{2,1,0:T(8,128)(2,1)} custom-call(s32[1]{0:T(128)} %bitcast.me_ref, s32[128]{0:T(128)} %rows_ref.1, s32[1,128]{1,0:T(1,128)} %bitcast.6, bf16[4,128,128]{2,1,0:T(8,128)(2,1)} %act_ref.1, f32[1,128]{1,0:T(1,128)} %bitcast.8, f32[1,128]{1,0:T(1,128)} %bitcast.10, bf16[128,128]{1,0:T(8,128)(2,1)} %wap.3, bf16[128,128]{1,0:T(8,128)(2,1)} %wag.3, ...), custom_call_target="tpu_custom_call" | custom-call | flops 67108864 | bytes 526340 | tf_op jit(solution)/shard_map/edges/pallas_call | solution.py:334
  2.6 17.9 %all_to_all.20.in_ref = bf16[32,32,128]{2,1,0:T(8,128)(2,1)S(1)} all-to-all(bf16[32,32,128]{2,1,0:T(8,128)(2,1)} %edges.1), channel_id=1, replica_groups=mesh['grp'=1,'dap'=32,'ch'=1] {'dap'}, dimensions={0} | all-to-all | bytes 524288 | tf_op jit(solution)/shard_map/all_to_all | solution.py:377
  20.5 0.0 copy-start.5
  20.5 0.0 copy-start.6
  20.5 0.0 copy-start.7
  20.5 0.0 copy-start.11
  20.6 1.1 %triangle.1 = (bf16[32,16,128]{2,1,0:T(8,128)(2,1)}, bf16[4,128,128]{2,1,0:T(8,128)(2,1)S(1)}, bf16[4,128,128]{2,1,0:T(8,128)(2,1)S(1)}) custom-call(bf16[32,32,128]{2,1,0:T(8,128)(2,1)S(1)} %all_to_all.20.in_ref), custom_call_target="tpu_custom_call" | custom-call | flops 16777216 | bytes 655360 | tf_op jit(solution)/shard_map/triangle/pallas_call | solution.py:334
  21.6 0.0 copy-start
  21.6 0.0 copy-start.1
  21.6 0.0 copy-start.2
  21.6 0.0 copy-start.3
  21.6 0.0 copy-start.4
  21.6 2.7 %all-to-all-start.1 = ((bf16[32,16,128]{2,1,0:T(8,128)(2,1)}), bf16[32,16,128]{2,1,0:T(8,128)(2,1)S(1)}, u32[]{:S(2)}, u32[]{:S(2)}) async-start(bf16[32,16,128]{2,1,0:T(8,128)(2,1)} %get-tuple-element.14), calls=%async_computation.1 | async-start | bytes 262144 | tf_op jit(solution)/shard_map/all_to_all | solution.py:377
  24.4 0.0 copy-start.8
  24.4 0.0 copy-start.9
  24.4 0.0 copy-start.10
  24.4 0.0 copy-done.5
  24.4 0.0 copy-done.6
  24.4 0.0 copy-done.7
  24.4 0.0 copy-done.11
  24.5 0.0 copy-done
  24.5 0.0 copy-done.1
  24.5 0.0 copy-done.2
  24.5 0.0 copy-done.3
  24.5 0.0 copy-done.4
  24.5 0.5 copy-done.8
  25.0 0.0 copy-done.9
  25.1 0.0 copy-done.10
  25.1 1.7 %gates.1 = (f32[4,4,128,128]{3,2,1,0:T(8,128)S(1)}, f32[4,128,128]{2,1,0:T(8,128)S(1)}, f32[4,1,128]{2,1,0:T(1,128)S(1)}, f32[128,128]{1,0:T(8,128)S(1)}, f32[51...) custom-call(s32[1]{0:T(128)} %bitcast.me_ref, s32[128]{0:T(128)S(1)} %copy-done.8, s32[1,128]{1,0:T(1,128)S(1)} %bitcast.7, ...), custom_call_target="tpu_custom_call" | custom-call | flops 100663296 | bytes 2363908 | tf_op jit(solution)/shard_map/gates/pallas_call | solution.py:334
  26.7 5.9 %all-to-all-done.1.tri_ref = bf16[32,16,128]{2,1,0:T(8,128)(2,1)S(1)} async-done(((bf16[32,16,128]{2,1,0:T(8,128)(2,1)}), bf16[32,16,128]{2,1,0:T(8,128)(2,1)S(1)}, u32[]{:S(2)}, u32[]{:S(2)}) %all-to-all-start.1) | async-done | bytes 131104 | tf_op jit(solution)/shard_map/all_to_all | solution.py:377
  32.6 0.3 norm.1
  32.9 9.9 %all_to_all.21.in_ref = bf16[32,16,128]{2,1,0:T(8,128)(2,1)S(1)} all-to-all(bf16[32,16,128]{2,1,0:T(8,128)(2,1)S(1)} %norm.1), channel_id=1, replica_groups=mesh['grp'=1,'dap'=32,'ch'=1] {'dap'}, dimensions={0} | all-to-all | bytes 262144 | tf_op jit(solution)/shard_map/all_to_all | solution.py:377
  42.8 1.1 %edge_grad.1 = bf16[32,32,128]{2,1,0:T(8,128)(2,1)} custom-call(bf16[32,16,128]{2,1,0:T(8,128)(2,1)S(1)} %all_to_all.21.in_ref, bf16[4,128,128]{2,1,0:T(8,128)(2,1)S(1)} %get-tuple-element.16.a_ref, bf16[4,128,128]{2,1,0:T(8,128)(2,1)S(1)} %get-tuple-element.17.b_ref), custom_call_target="tpu_custom_call" | custom-call | flops 33554432 | bytes 655360 | tf_op jit(solution)/shard_map/edge_grad/pallas_call | solution.py:334
  43.9 2.6 %all-to-all-start.3 = ((bf16[32,32,128]{2,1,0:T(8,128)(2,1)}), bf16[32,32,128]{2,1,0:T(8,128)(2,1)S(1)}, u32[]{:S(2)}, u32[]{:S(2)}) async-start(bf16[32,32,128]{2,1,0:T(8,128)(2,1)} %edge_grad.1), calls=%async_computation.3 | async-start | bytes 524288 | tf_op jit(solution)/shard_map/all_to_all | solution.py:377
  46.5 0.0 copy-start.12
  46.5 0.6 %copy-done.12 = f32[128]{0:T(128)S(1)} copy-done((f32[128]{0:T(128)S(1)}, f32[128]{0:T(128)}, u32[]{:S(2)}) %copy-start.12) | copy-done | bytes 536
  47.1 0.7 %gate_grad.1.gate_part = f32[4,128,128]{2,1,0:T(8,128)S(1)} custom-call(bf16[32,16,128]{2,1,0:T(8,128)(2,1)S(1)} %all-to-all-done.1.tri_ref, f32[4,128,128]{2,1,0:T(8,128)S(1)} %get-tuple-element.22.slope, f32[1,128]{1,0:T(1,128)S(1)} %bitcast.13, f32[1,128]{1,0:T(1,128)S(1)} %bitcast.14, bf16[128,128]{1,0:T(8,128)(2,1)S(1)} %copy-done.6, ...), custom_call_target="tpu_custom_call" | custom-call | flops 33554432 | bytes 721920 | tf_op jit(solution)/shard_map/gate_grad/pallas_call | solution.py:334
  47.9 9.2 %all-to-all-done.3.in_ref = bf16[32,32,128]{2,1,0:T(8,128)(2,1)S(1)} async-done(((bf16[32,32,128]{2,1,0:T(8,128)(2,1)}), bf16[32,32,128]{2,1,0:T(8,128)(2,1)S(1)}, u32[]{:S(2)}, u32[]{:S(2)}) %all-to-all-start.3) | async-done | bytes 262176 | tf_op jit(solution)/shard_map/all_to_all | solution.py:377
  57.1 1.1 %input_grad.1 = bf16[4,128,128]{2,1,0:T(8,128)(2,1)} custom-call(bf16[32,32,128]{2,1,0:T(8,128)(2,1)S(1)} %all-to-all-done.3.in_ref, f32[4,4,128,128]{3,2,1,0:T(8,128)S(1)} %get-tuple-element.18.factors, f32[4,128,128]{2,1,0:T(8,128)S(1)} %get-tuple-element.19.normed_t, f32[4,1,128]{2,1,0:T(1,128)S(1)} %get-tuple-element.20.rstd_t, ...), custom_call_target="tpu_custom_call" | custom-call | flops 67108864 | bytes 2164736 | tf_op jit(solution)/shard_map/input_grad/pallas_call | solution.py:334
Async XLA Ops:
  20.5 3.9 %copy-start.5 = (bf16[128,128]{1,0:T(8,128)(2,1)S(1)}, bf16[128,128]{1,0:T(8,128)(2,1)}, u32[]{:S(2)}) copy-start(bf16[128,128]{1,0:T(8,128)(2,1)} %w_gate.3) | copy-start | bytes 98308
  20.5 3.9 %copy-start.6 = (bf16[128,128]{1,0:T(8,128)(2,1)S(1)}, bf16[128,128]{1,0:T(8,128)(2,1)}, u32[]{:S(2)}) copy-start(bf16[128,128]{1,0:T(8,128)(2,1)} %w_out.3) | copy-start | bytes 98308
  20.5 3.9 %copy-start.7 = (bf16[4,128,128]{2,1,0:T(8,128)(2,1)S(1)}, bf16[4,128,128]{2,1,0:T(8,128)(2,1)}, u32[]{:S(2)}) copy-start(bf16[4,128,128]{2,1,0:T(8,128)(2,1)} %grad_ref.1) | copy-start | bytes 393220
  20.5 3.9 %copy-start.11 = (f32[128]{0:T(128)S(1)}, f32[128]{0:T(128)}, u32[]{:S(2)}) copy-start(f32[128]{0:T(128)} %param.23) | copy-start | bytes 1540
  21.6 2.8 %copy-start = (bf16[4,128,128]{2,1,0:T(8,128)(2,1)S(1)}, bf16[4,128,128]{2,1,0:T(8,128)(2,1)}, u32[]{:S(2)}) copy-start(bf16[4,128,128]{2,1,0:T(8,128)(2,1)} %act_ref.1) | copy-start | bytes 393220
  21.6 2.8 %copy-start.1 = (bf16[128,128]{1,0:T(8,128)(2,1)S(1)}, bf16[128,128]{1,0:T(8,128)(2,1)}, u32[]{:S(2)}) copy-start(bf16[128,128]{1,0:T(8,128)(2,1)} %wap.3) | copy-start | bytes 98308
  21.6 2.9 %copy-start.2 = (bf16[128,128]{1,0:T(8,128)(2,1)S(1)}, bf16[128,128]{1,0:T(8,128)(2,1)}, u32[]{:S(2)}) copy-start(bf16[128,128]{1,0:T(8,128)(2,1)} %wag.3) | copy-start | bytes 98308
  21.6 2.9 %copy-start.3 = (bf16[128,128]{1,0:T(8,128)(2,1)S(1)}, bf16[128,128]{1,0:T(8,128)(2,1)}, u32[]{:S(2)}) copy-start(bf16[128,128]{1,0:T(8,128)(2,1)} %wbp.3) | copy-start | bytes 98308
  21.6 2.9 %copy-start.4 = (bf16[128,128]{1,0:T(8,128)(2,1)S(1)}, bf16[128,128]{1,0:T(8,128)(2,1)}, u32[]{:S(2)}) copy-start(bf16[128,128]{1,0:T(8,128)(2,1)} %wbg.3) | copy-start | bytes 98308
  21.6 11.0 %all-to-all-start.1 = ((bf16[32,16,128]{2,1,0:T(8,128)(2,1)}), bf16[32,16,128]{2,1,0:T(8,128)(2,1)S(1)}, u32[]{:S(2)}, u32[]{:S(2)}) async-start(bf16[32,16,128]{2,1,0:T(8,128)(2,1)} %get-tuple-element.14), calls=%async_computation.1 | async-start | bytes 262144 | tf_op jit(solution)/shard_map/all_to_all | solution.py:377
  24.4 0.7 %copy-start.8 = (s32[128]{0:T(128)S(1)}, s32[128]{0:T(128)}, u32[]{:S(2)}) copy-start(s32[128]{0:T(128)} %rows_ref.1) | copy-start | bytes 1540
  24.4 0.7 %copy-start.9 = (f32[128]{0:T(128)S(1)}, f32[128]{0:T(128)}, u32[]{:S(2)}) copy-start(f32[128]{0:T(128)} %param.16) | copy-start | bytes 1540
  24.4 0.7 %copy-start.10 = (f32[128]{0:T(128)S(1)}, f32[128]{0:T(128)}, u32[]{:S(2)}) copy-start(f32[128]{0:T(128)} %param.17) | copy-start | bytes 1540
  43.9 13.2 %all-to-all-start.3 = ((bf16[32,32,128]{2,1,0:T(8,128)(2,1)}), bf16[32,32,128]{2,1,0:T(8,128)(2,1)S(1)}, u32[]{:S(2)}, u32[]{:S(2)}) async-start(bf16[32,32,128]{2,1,0:T(8,128)(2,1)} %edge_grad.1), calls=%async_computation.3 | async-start | bytes 524288 | tf_op jit(solution)/shard_map/all_to_all | solution.py:377
  46.5 0.7 %copy-start.12 = (f32[128]{0:T(128)S(1)}, f32[128]{0:T(128)}, u32[]{:S(2)}) copy-start(f32[128]{0:T(128)} %param.24) | copy-start | bytes 1540
where the time goes:
time: 58.6 us; the launch traced here: 58.2 us
  blocking collectives  27.8 us (47%)
  waiting for transfers between devices  15.1 us (26%)
  Pallas kernels  8.52 us (15%)
  starting transfers between devices  5.31 us (9%)
  local copies, waits for them, and re-layouts  1.26 us (2%)
    all_to_all x2, blocking collectives, exchange(): return lax.all_to_all(value, 'dap', split_axis=0, concat_axis=0, tiled=True)  27.8 us
    all_to_all x2, waiting for transfers between devices, exchange(): return lax.all_to_all(value, 'dap', split_axis=0, concat_axis=0, tiled=True)  15.1 us
    pallas_call x7, Pallas kernels, call(): pl.pallas_call(kernel, name=name, out_shape=shapes, in_specs=[SMEM] * sca...  8.52 us
    all_to_all x2, starting transfers between devices, exchange(): return lax.all_to_all(value, 'dap', split_axis=0, concat_axis=0, tiled=True)  5.31 us
    unnamed x26, local copies, waits for them, and re-layouts  1.26 us
  transfers between devices with their start and end apart: 2, of which 2 were waited for; matrix products, arithmetic and copies ran while one was open for 0% of the time, Pallas kernels for 4%

commit v1 on v0

--- a/solution.py
+++ b/solution.py
@@ -157,23 +157,26 @@
     ]
     for copy in copies:
         copy.start()
-    rows_ref, valid_ref, act_ref, gain_ref, bias_ref, *weights = local
-    own, cols, _ = act_ref.shape
+    act_ref, gain_ref, bias_ref, rows_ref, valid_ref, *weights = local
+    own, cols, chan = act_ref.shape
     devices, block, _ = out_ref.shape
     hidden = weights[0].shape[1]
     half = block // 2
-    for copy in copies:
+    for copy in copies[:3]:
+        copy.wait()
+    normed = normed_rows(act_ref[...].reshape(own * cols, chan).astype(F32))
+    pair_norm = (normed * gain_ref[...] + bias_ref[...]).astype(BF16)
+    for copy in copies[3:]:
         copy.wait()
     valid = valid_ref[...].astype(F32)
-    for r in range(own):
-        normed = normed_rows(act_ref[r].astype(F32))
-        pair_norm = (normed * gain_ref[...] + bias_ref[...]).astype(BF16)
-        mask = valid * rows_ref[me_ref[0] * own + r].astype(F32)
-        for side in range(2):
-            proj = dot(weights[2 * side][...], pair_norm, 0, 1)
-            sig = jax.nn.sigmoid(dot(weights[2 * side + 1][...], pair_norm, 0, 1))
-            wide[side, pl.ds(r, hidden, stride=own), :] = mask * sig * proj
+    mask = jnp.concatenate(
+        [valid * rows_ref[me_ref[0] * own + r].astype(F32) for r in range(own)], axis=1
+    )
     for side in range(2):
+        proj = dot(weights[2 * side][...], pair_norm, 0, 1)
+        edge = mask * jax.nn.sigmoid(dot(weights[2 * side + 1][...], pair_norm, 0, 1)) * proj
+        for r in range(own):
+            wide[side, pl.ds(r, hidden, stride=own), :] = edge[:, r * cols : (r + 1) * cols]
         out_ref[:, side * half : (side + 1) * half, :] = (
             wide[side].reshape(devices, half, cols).astype(BF16)
         )
@@ -195,16 +198,17 @@
         centre = act - jnp.mean(act, axis=0, keepdims=True)
         inverse = lax.rsqrt(jnp.mean(centre * centre, axis=0, keepdims=True) + EPSILON)
         normed = centre * inverse
-        normed_t[r] = normed
-        rstd_t[r] = inverse
+        lanes = pl.ds(r * cols, cols)
+        normed_t[:, lanes] = normed
+        rstd_t[:, lanes] = inverse
         pair_norm = (normed * gain + bias).astype(BF16)
         mask = valid * rows_ref[me_ref[0] * own + r].astype(F32)
         for side, (w_proj, w_sig) in enumerate(((wap, wag), (wbp, wbg))):
             proj = dot(w_proj[...], pair_norm, 0, 0)
             sig = jax.nn.sigmoid(dot(w_sig[...], pair_norm, 0, 0))
             kept = mask * sig
-            factors[2 * side, r] = kept
-            factors[2 * side + 1, r] = kept * proj * (1.0 - sig)
+            factors[2 * side, :, lanes] = kept
+            factors[2 * side + 1, :, lanes] = kept * proj * (1.0 - sig)
         gate_act = jax.nn.sigmoid(dot(pair_norm, w_gate[...], 0, 0))
         d_proj = grad_ref[r].astype(F32) * gate_act
         slope[r] = d_proj * (1.0 - gate_act)
@@ -213,27 +217,52 @@
         )
 
 
-def triangle_kernel(in_ref, out_ref, a_ref, b_ref, wide, back):
-    devices, block, cols = in_ref.shape
-    slice_h, rows, _ = a_ref.shape
-    half = block // 2
-    own = half // slice_h
-    for side in range(2):
-        wide[side] = (
-            in_ref[:, side * half : (side + 1) * half, :].astype(F32).reshape(devices * half, cols)
-        )
-    for c in range(slice_h):
-        for r in range(own):
-            at = pl.ds(c * own + r, devices, stride=half)
-            a_ref[c, r * devices : (r + 1) * devices, :] = wide[0, at, :].astype(BF16)
-            back[pl.ds(r, devices, stride=own), :] = wide[1, at, :]
-        b_ref[c] = back[...].astype(BF16)
-        tri = dot(a_ref[c], b_ref[c], 1, 1)
-        for r in range(own):
-            wide[0, pl.ds(c * own + r, devices, stride=half), :] = tri[
-                r * devices : (r + 1) * devices
-            ]
-    out_ref[...] = wide[0].reshape(devices, half, cols).astype(BF16)
+def low_rows(shape):
+    return lax.broadcasted_iota(jnp.int32, shape, 1) < SUBLANES // 2
+
+
+def swap(values):
+    return pltpu.roll(values, SUBLANES // 2, 1)
+
+
+def split_channels(blocks, own):
+    devices, block, cols = blocks.shape
+    tiles = blocks.reshape(devices // 2, 2, block // SUBLANES, SUBLANES, cols)
+    parts = []
+    for tile in range(block // SUBLANES):
+        even, odd = tiles[:, 0, tile], tiles[:, 1, tile]
+        low = low_rows(even.shape)
+        parts.append(jnp.where(low, even, swap(odd)))
+        parts.append(jnp.where(low, swap(even), odd))
+    return [part.reshape(devices * own, cols) for part in parts]
+
+
+def merge_channels(parts, own):
+    rows, cols = parts[0].shape
+    devices = rows // own
+    tiles = [part.reshape(devices // 2, SUBLANES, cols) for part in parts]
+    low = low_rows(tiles[0].shape)
+    even, odd = [], []
+    for first, second in zip(tiles[::2], tiles[1::2]):
+        even.append(jnp.where(low, first, swap(second)))
+        odd.append(jnp.where(low, swap(first), second))
+    both = [jnp.concatenate(side, axis=1) for side in (even, odd)]
+    block = len(parts) * own
+    return jnp.stack(both, axis=1).reshape(devices, block, cols)
+
+
+def triangle_kernel(own, in_ref, _, out_ref, a_ref, b_ref):
+    half = out_ref.shape[1]
+    sides = [
+        split_channels(in_ref[:, side * half : (side + 1) * half, :].astype(F32), own)
+        for side in range(2)
+    ]
+    tri = []
+    for c, (edge_a, edge_b) in enumerate(zip(*sides)):
+        a_ref[c] = edge_a.astype(BF16)
+        b_ref[c] = edge_b.astype(BF16)
+        tri.append(dot(a_ref[c], b_ref[c], 1, 1))
+    out_ref[...] = merge_channels(tri, own).astype(BF16)
 
 
 def fold(values, own):
@@ -274,25 +303,19 @@
         tri_norm = (wide[pl.ds(r, hidden, stride=own), :] * gain + bias).astype(BF16)
         proj_out = dot(tri_norm, w_out[...], 0, 0)
         d_gate = (slope[r] * proj_out).astype(BF16)
-        out_ref[r] = dot(w_gate[...], d_gate, 1, 1)
-
-
-def edge_grad_kernel(in_ref, a_ref, b_ref, out_ref, wide, whole):
-    devices, block, cols = in_ref.shape
-    slice_h, rows, _ = a_ref.shape
-    own = block // slice_h
-    wide[0] = in_ref[...].astype(F32).reshape(devices * block, cols)
-    for c in range(slice_h):
-        at = [pl.ds(c * own + r, devices, stride=block) for r in range(own)]
-        d_tri = jnp.concatenate([wide[0, at[r], :] for r in range(own)], axis=0).astype(BF16)
-        d_a = dot(d_tri, b_ref[c], 1, 0)
-        whole[...] = dot(d_tri, a_ref[c], 0, 0)
-        for r in range(own):
-            wide[1, at[r], :] = d_a[r * devices : (r + 1) * devices]
-            wide[2, at[r], :] = whole[pl.ds(r, devices, stride=own), :]
+        out_ref[:, r * cols : (r + 1) * cols] = dot(w_gate[...], d_gate, 1, 1)
+
+
+def edge_grad_kernel(own, in_ref, a_ref, b_ref, out_ref):
+    block = in_ref.shape[1]
+    grads = ([], [])
+    for c, part in enumerate(split_channels(in_ref[...].astype(F32), own)):
+        d_tri = part.astype(BF16)
+        grads[0].append(dot(d_tri, b_ref[c], 1, 0))
+        grads[1].append(dot(d_tri, a_ref[c], 0, 0))
     for side in range(2):
         out_ref[:, side * block : (side + 1) * block, :] = (
-            wide[1 + side].reshape(devices, block, cols).astype(BF16)
+            merge_channels(grads[side], own).astype(BF16)
         )
 
 
@@ -305,18 +328,20 @@
         wide[side] = (
             in_ref[:, side * half : (side + 1) * half, :].astype(F32).reshape(devices * half, cols)
         )
+    total = gate_part[...]
+    for side, weights in enumerate(((wap, wag), (wbp, wbg))):
+        d_edge = jnp.concatenate(
+            [wide[side, pl.ds(r, hidden, stride=own), :] for r in range(own)], axis=1
+        )
+        for at, weight in enumerate(weights):
+            total = total + dot(weight[...], (d_edge * factors[2 * side + at]).astype(BF16), 1, 0)
+    grad_hat = total * jnp.concatenate([gain_t[...]] * own, axis=1)
+    normed = normed_t[...]
+    mean_grad = jnp.mean(grad_hat, axis=0, keepdims=True)
+    mean_proj = jnp.mean(grad_hat * normed, axis=0, keepdims=True)
+    grad = rstd_t[...] * (grad_hat - mean_grad - normed * mean_proj)
     for r in range(own):
-        total = gate_part[r]
-        for side, (w_proj, w_sig) in enumerate(((wap, wag), (wbp, wbg))):
-            d_edge = wide[side, pl.ds(r, hidden, stride=own), :]
-            total = total + dot(w_proj[...], (d_edge * factors[2 * side, r]).astype(BF16), 1, 0)
-            total = total + dot(w_sig[...], (d_edge * factors[2 * side + 1, r]).astype(BF16), 1, 0)
-        grad_hat = total * gain_t[...]
-        normed = normed_t[r]
-        mean_grad = jnp.mean(grad_hat, axis=0, keepdims=True)
-        mean_proj = jnp.mean(grad_hat * normed, axis=0, keepdims=True)
-        grad = rstd_t[r] * (grad_hat - mean_grad - normed * mean_proj)
-        out_ref[r] = jnp.transpose(grad).astype(BF16)
+        out_ref[r] = jnp.transpose(grad[:, r * cols : (r + 1) * cols]).astype(BF16)
 
 
 VMEM = pl.BlockSpec(memory_space=pltpu.VMEM)
@@ -328,14 +353,14 @@
     return pltpu.VMEM(shape, F32)
 
 
-def call(kernel, name, outs, args, scratch=(), scalars=0, flops=0, space=VMEM, limit=32 * 2**20):
+def call(kernel, name, outs, args, scratch=(), scalars=0, flops=0, spaces=None, limit=32 * 2**20):
     shapes = [jax.ShapeDtypeStruct(shape, dtype) for shape, dtype in outs]
     moved = sum(value.size * value.dtype.itemsize for value in list(args) + shapes)
     result = pl.pallas_call(
         kernel,
         name=name,
         out_shape=shapes,
-        in_specs=[SMEM] * scalars + [space] * (len(args) - scalars),
+        in_specs=[SMEM] * scalars + (spaces or [VMEM] * (len(args) - scalars)),
         out_specs=[VMEM] * len(outs),
         scratch_shapes=scratch,
         cost_estimate=pl.CostEstimate(flops=flops, bytes_accessed=moved, transcendentals=0),
@@ -376,20 +401,20 @@
     def exchange(value):
         return lax.all_to_all(value, "dap", split_axis=0, concat_axis=0, tiled=True)
 
-    first = (residue_mask, valid, pair_act, gain_in, bias_in, *w_edges)
+    first = (pair_act, gain_in, bias_in, residue_mask, valid, *w_edges)
     edges = call(
         edges_kernel,
         "edges",
         [((dap, 2 * block, cols), BF16)],
         (me, *first),
         scratch=[
-            (pltpu.VMEM if index else pltpu.SMEM)(value.shape, value.dtype)
-            for index, value in enumerate(first)
+            (pltpu.SMEM if value is residue_mask else pltpu.VMEM)(value.shape, value.dtype)
+            for value in first
         ]
         + [wide(2, hidden * own, cols), pltpu.SemaphoreType.DMA((len(first),))],
         scalars=1,
         flops=4 * product,
-        space=HBM,
+        spaces=[HBM] * len(first),
         limit=None,
     )
     edges = exchange(edges)
@@ -397,9 +422,9 @@
         gates_kernel,
         "gates",
         [
-            ((4, own, hidden, cols), F32),
-            ((own, chan, cols), F32),
-            ((own, 1, cols), F32),
+            ((4, hidden, own * cols), F32),
+            ((chan, own * cols), F32),
+            ((1, own * cols), F32),
             ((chan, cols), F32),
             ((hidden * own, cols), F32),
             ((own, cols, chan), F32),
@@ -410,16 +435,16 @@
         flops=6 * product,
     )
     tri, edge_a, edge_b = call(
-        triangle_kernel,
+        functools.partial(triangle_kernel, own),
         "triangle",
         [
             ((dap, block, cols), BF16),
             ((slice_h, rows, cols), BF16),
             ((slice_h, rows, cols), BF16),
         ],
-        (edges,),
-        scratch=[wide(2, dap * block, cols), wide(rows, cols)],
+        (edges, d_normed),
         flops=product,
+        spaces=[VMEM, pl.BlockSpec(memory_space=pl.ANY)],
     )
     tri = exchange(tri)
     d_tri = call(
@@ -432,17 +457,16 @@
     gate_part = call(
         gate_grad_kernel,
         "gate_grad",
-        [((own, chan, cols), F32)],
+        [((chan, own * cols), F32)],
         (tri, slope, gain_out, bias_out, w_out, w_gate),
         scratch=[wide(hidden * own, cols)],
         flops=2 * product,
     )
     d_edges = call(
-        edge_grad_kernel,
+        functools.partial(edge_grad_kernel, own),
         "edge_grad",
         [((dap, 2 * block, cols), BF16)],
         (d_tri, edge_a, edge_b),
-        scratch=[wide(3, dap * block, cols), wide(rows, cols)],
         flops=2 * product,
     )
     d_edges = exchange(d_edges)
@@ -463,7 +487,7 @@
     return (
         ch == 1
         and hidden % dap == 0
-        and own in (1, 2, 4, 8)
+        and own == SUBLANES // 2
         and block % 16 == 0
         and dap % SUBLANES == 0
         and cols == dap * own

time: 58.6 us -> 56.9 us (0.971)
  blocking collectives: 27.8 us -> 20.4 us
  starting transfers between devices: 5.31 us -> 9.89 us
  waiting for transfers between devices: 15.1 us -> 17.4 us
  Pallas kernels: 8.52 us -> 7.29 us
    all_to_all x2, blocking collectives: 27.8 us -> 20.4 us  [exchange(): return lax.all_to_all(value, 'dap', split_axis=0, concat_axis=0, tiled=True)]
    all_to_all x2, starting transfers between devices: 5.31 us -> 9.89 us  [exchange(): return lax.all_to_all(value, 'dap', split_axis=0, concat_axis=0, tiled=True)]
    all_to_all x2, waiting for transfers between devices: 15.1 us -> 17.4 us  [exchange(): return lax.all_to_all(value, 'dap', split_axis=0, concat_axis=0, tiled=True)]
    pallas_call x7, Pallas kernels: 8.52 us -> 7.29 us  [call(): pl.pallas_call(kernel, name=name, out_shape=shapes, in_specs=[SMEM] * sca...]
where the time goes in v1:
time: 56.9 us; the launch traced here: 56.6 us
  blocking collectives  20.4 us (36%)
  waiting for transfers between devices  17.4 us (31%)
  starting transfers between devices  9.89 us (17%)
  Pallas kernels  7.29 us (13%)
  local copies, waits for them, and re-layouts  1.28 us (2%)
    all_to_all x2, blocking collectives, exchange(): return lax.all_to_all(value, 'dap', split_axis=0, concat_axis=0, tiled=True)  20.4 us
    all_to_all x2, waiting for transfers between devices, exchange(): return lax.all_to_all(value, 'dap', split_axis=0, concat_axis=0, tiled=True)  17.4 us
    all_to_all x2, starting transfers between devices, exchange(): return lax.all_to_all(value, 'dap', split_axis=0, concat_axis=0, tiled=True)  9.89 us
    pallas_call x7, Pallas kernels, call(): pl.pallas_call(kernel, name=name, out_shape=shapes, in_specs=[SMEM] * sca...  7.29 us
    unnamed x26, local copies, waits for them, and re-layouts  1.28 us
  transfers between devices with their start and end apart: 2, of which 2 were waited for; matrix products, arithmetic and copies ran while one was open for 0% of the time, Pallas kernels for 4%

profile of v1, /device:TPU:0, one launch (start us, length us, event | category | flops | bytes accessed | tf_op | source)
XLA Modules:
  0.0 56.6 jit_solution(12427414065535903652)
XLA Ops:
  0.0 2.3 %edges.1 = bf16[32,32,128]{2,1,0:T(8,128)(2,1)} custom-call(s32[1]{0:T(128)} %bitcast.me_ref, bf16[4,128,128]{2,1,0:T(8,128)(2,1)} %act_ref.1, f32[1,128]{1,0:T(1,128)} %bitcast.8, f32[1,128]{1,0:T(1,128)} %bitcast.10, s32[128]{0:T(128)} %rows_ref.1, s32[1,128]{1,0:T(1,128)} %bitcast.6, bf16[128,128]{1,0:T(8,128)(2,1)} %wap.3, bf16[128,128]{1,0:T(8,128)(2,1)} %wag.3, ...), custom_call_target="tpu_custom_call" | custom-call | flops 67108864 | bytes 526340 | tf_op jit(solution)/shard_map/edges/pallas_call | solution.py:359
  2.3 0.0 copy-start
  2.3 0.0 copy-start.1
  2.3 0.0 copy-start.2
  2.3 0.0 copy-start.3
  2.4 0.0 copy-start.4
  2.4 0.0 copy-start.5
  2.4 0.0 copy-start.6
  2.4 0.0 copy-start.7
  2.4 0.0 copy-start.11
  2.4 7.3 %all-to-all-start = ((bf16[32,32,128]{2,1,0:T(8,128)(2,1)}), bf16[32,32,128]{2,1,0:T(8,128)(2,1)S(1)}, u32[]{:S(2)}, u32[]{:S(2)}) async-start(bf16[32,32,128]{2,1,0:T(8,128)(2,1)} %edges.1), calls=%async_computation | async-start | bytes 524288 | tf_op jit(solution)/shard_map/all_to_all | solution.py:402
  9.7 0.0 copy-start.8
  9.7 0.0 copy-start.9
  9.8 0.0 copy-start.10
  9.8 0.0 copy-done
  9.8 0.0 copy-done.1
  9.8 0.0 copy-done.2
  9.8 0.0 copy-done.3
  9.8 0.0 copy-done.4
  9.8 0.0 copy-done.5
  9.8 0.0 copy-done.6
  9.8 0.0 copy-done.7
  9.8 0.0 copy-done.11
  9.9 0.5 copy-done.8
  10.4 0.0 copy-done.9
  10.4 0.0 copy-done.10
  10.4 1.7 %gates.1 = (f32[4,128,512]{2,1,0:T(8,128)S(1)}, f32[128,512]{1,0:T(8,128)S(1)}, f32[1,512]{1,0:T(1,128)S(1)}, f32[128,128]{1,0:T(8,128)S(1)}, f32[512,128]{1,0:T(8,128)S(1)}, /*index=5*/f32[4,128,128]{2,1,0:T(8,128)S(1)}) custom-call(s32[1]{0:T(128)} %bitcast.me_ref, s32[128]{0:T(128)S(1)} %copy-done.8, s32[1,128]{1,0:T(1,128)S(1)} %bitcast.7, ...), custom_call_target="tpu_custom_call" | custom-call | flops 100663296 | bytes 2363908 | tf_op jit(solution)/shard_map/gates/pallas_call | solution.py:359
  12.1 8.2 %all-to-all-done.in_ref = bf16[32,32,128]{2,1,0:T(8,128)(2,1)S(1)} async-done(((bf16[32,32,128]{2,1,0:T(8,128)(2,1)}), bf16[32,32,128]{2,1,0:T(8,128)(2,1)S(1)}, u32[]{:S(2)}, u32[]{:S(2)}) %all-to-all-start) | async-done | bytes 262176 | tf_op jit(solution)/shard_map/all_to_all | solution.py:402
  20.3 0.2 triangle.1
  20.6 10.4 %all_to_all.20.tri_ref = bf16[32,16,128]{2,1,0:T(8,128)(2,1)S(1)} all-to-all(bf16[32,16,128]{2,1,0:T(8,128)(2,1)S(1)} %get-tuple-element.15), channel_id=1, replica_groups=mesh['grp'=1,'dap'=32,'ch'=1] {'dap'}, dimensions={0} | all-to-all | bytes 262144 | tf_op jit(solution)/shard_map/all_to_all | solution.py:402
  31.0 0.3 norm.1
  31.3 10.0 %all_to_all.21.in_ref = bf16[32,16,128]{2,1,0:T(8,128)(2,1)S(1)} all-to-all(bf16[32,16,128]{2,1,0:T(8,128)(2,1)S(1)} %norm.1), channel_id=1, replica_groups=mesh['grp'=1,'dap'=32,'ch'=1] {'dap'}, dimensions={0} | all-to-all | bytes 262144 | tf_op jit(solution)/shard_map/all_to_all | solution.py:402
  41.3 1.0 %edge_grad.1 = bf16[32,32,128]{2,1,0:T(8,128)(2,1)} custom-call(bf16[32,16,128]{2,1,0:T(8,128)(2,1)S(1)} %all_to_all.21.in_ref, bf16[4,128,128]{2,1,0:T(8,128)(2,1)S(1)} %get-tuple-element.16.a_ref, bf16[4,128,128]{2,1,0:T(8,128)(2,1)S(1)} %get-tuple-element.17.b_ref), custom_call_target="tpu_custom_call" | custom-call | flops 33554432 | bytes 655360 | tf_op jit(solution)/shard_map/edge_grad/pallas_call | solution.py:359
  42.2 2.6 %all-to-all-start.3 = ((bf16[32,32,128]{2,1,0:T(8,128)(2,1)}), bf16[32,32,128]{2,1,0:T(8,128)(2,1)S(1)}, u32[]{:S(2)}, u32[]{:S(2)}) async-start(bf16[32,32,128]{2,1,0:T(8,128)(2,1)} %edge_grad.1), calls=%async_computation.3 | async-start | bytes 524288 | tf_op jit(solution)/shard_map/all_to_all | solution.py:402
  44.8 0.0 copy-start.12
  44.8 0.6 %copy-done.12 = f32[128]{0:T(128)S(1)} copy-done((f32[128]{0:T(128)S(1)}, f32[128]{0:T(128)}, u32[]{:S(2)}) %copy-start.12) | copy-done | bytes 536
  45.5 0.7 %gate_grad.1.gate_part = f32[128,512]{1,0:T(8,128)S(1)} custom-call(bf16[32,16,128]{2,1,0:T(8,128)(2,1)S(1)} %all_to_all.20.tri_ref, f32[4,128,128]{2,1,0:T(8,128)S(1)} %get-tuple-element.22.slope, f32[1,128]{1,0:T(1,128)S(1)} %bitcast.13, f32[1,128]{1,0:T(1,128)S(1)} %bitcast.14, bf16[128,128]{1,0:T(8,128)(2,1)S(1)} %copy-done.6, bf16[128,128]{1,0:T(8,128)(2,1)S(1)} %copy-done.5), custom_call_target="tpu_custom_call" | custom-call | flops 33554432 | bytes 721920 | tf_op jit(solution)/shard_map/gate_grad/pallas_call | solution.py:359
  46.2 9.2 %all-to-all-done.3.in_ref = bf16[32,32,128]{2,1,0:T(8,128)(2,1)S(1)} async-done(((bf16[32,32,128]{2,1,0:T(8,128)(2,1)}), bf16[32,32,128]{2,1,0:T(8,128)(2,1)S(1)}, u32[]{:S(2)}, u32[]{:S(2)}) %all-to-all-start.3) | async-done | bytes 262176 | tf_op jit(solution)/shard_map/all_to_all | solution.py:402
  55.4 1.1 %input_grad.1 = bf16[4,128,128]{2,1,0:T(8,128)(2,1)} custom-call(bf16[32,32,128]{2,1,0:T(8,128)(2,1)S(1)} %all-to-all-done.3.in_ref, f32[4,128,512]{2,1,0:T(8,128)S(1)} %get-tuple-element.18.factors, f32[128,512]{1,0:T(8,128)S(1)} %get-tuple-element.19.normed_t, f32[1,512]{1,0:T(1,128)S(1)} %get-tuple-element.20.rstd_t, ...), custom_call_target="tpu_custom_call" | custom-call | flops 67108864 | bytes 2164736 | tf_op jit(solution)/shard_map/input_grad/pallas_call | solution.py:359
Async XLA Ops:
  2.3 7.5 %copy-start = (bf16[4,128,128]{2,1,0:T(8,128)(2,1)S(1)}, bf16[4,128,128]{2,1,0:T(8,128)(2,1)}, u32[]{:S(2)}) copy-start(bf16[4,128,128]{2,1,0:T(8,128)(2,1)} %act_ref.1) | copy-start | bytes 393220
  2.3 7.5 %copy-start.1 = (bf16[128,128]{1,0:T(8,128)(2,1)S(1)}, bf16[128,128]{1,0:T(8,128)(2,1)}, u32[]{:S(2)}) copy-start(bf16[128,128]{1,0:T(8,128)(2,1)} %wap.3) | copy-start | bytes 98308
  2.3 7.5 %copy-start.2 = (bf16[128,128]{1,0:T(8,128)(2,1)S(1)}, bf16[128,128]{1,0:T(8,128)(2,1)}, u32[]{:S(2)}) copy-start(bf16[128,128]{1,0:T(8,128)(2,1)} %wag.3) | copy-start | bytes 98308
  2.3 7.5 %copy-start.3 = (bf16[128,128]{1,0:T(8,128)(2,1)S(1)}, bf16[128,128]{1,0:T(8,128)(2,1)}, u32[]{:S(2)}) copy-start(bf16[128,128]{1,0:T(8,128)(2,1)} %wbp.3) | copy-start | bytes 98308
  2.4 7.5 %copy-start.4 = (bf16[128,128]{1,0:T(8,128)(2,1)S(1)}, bf16[128,128]{1,0:T(8,128)(2,1)}, u32[]{:S(2)}) copy-start(bf16[128,128]{1,0:T(8,128)(2,1)} %wbg.3) | copy-start | bytes 98308
  2.4 7.4 %copy-start.5 = (bf16[128,128]{1,0:T(8,128)(2,1)S(1)}, bf16[128,128]{1,0:T(8,128)(2,1)}, u32[]{:S(2)}) copy-start(bf16[128,128]{1,0:T(8,128)(2,1)} %w_gate.3) | copy-start | bytes 98308
  2.4 7.4 %copy-start.6 = (bf16[128,128]{1,0:T(8,128)(2,1)S(1)}, bf16[128,128]{1,0:T(8,128)(2,1)}, u32[]{:S(2)}) copy-start(bf16[128,128]{1,0:T(8,128)(2,1)} %w_out.3) | copy-start | bytes 98308
  2.4 7.4 %copy-start.7 = (bf16[4,128,128]{2,1,0:T(8,128)(2,1)S(1)}, bf16[4,128,128]{2,1,0:T(8,128)(2,1)}, u32[]{:S(2)}) copy-start(bf16[4,128,128]{2,1,0:T(8,128)(2,1)} %grad_ref.1) | copy-start | bytes 393220
  2.4 7.4 %copy-start.11 = (f32[128]{0:T(128)S(1)}, f32[128]{0:T(128)}, u32[]{:S(2)}) copy-start(f32[128]{0:T(128)} %param.23) | copy-start | bytes 1540
  2.4 17.9 %all-to-all-start = ((bf16[32,32,128]{2,1,0:T(8,128)(2,1)}), bf16[32,32,128]{2,1,0:T(8,128)(2,1)S(1)}, u32[]{:S(2)}, u32[]{:S(2)}) async-start(bf16[32,32,128]{2,1,0:T(8,128)(2,1)} %edges.1), calls=%async_computation | async-start | bytes 524288 | tf_op jit(solution)/shard_map/all_to_all | solution.py:402
  9.7 0.7 %copy-start.8 = (s32[128]{0:T(128)S(1)}, s32[128]{0:T(128)}, u32[]{:S(2)}) copy-start(s32[128]{0:T(128)} %rows_ref.1) | copy-start | bytes 1540
  9.7 0.7 %copy-start.9 = (f32[128]{0:T(128)S(1)}, f32[128]{0:T(128)}, u32[]{:S(2)}) copy-start(f32[128]{0:T(128)} %param.16) | copy-start | bytes 1540
  9.8 0.7 %copy-start.10 = (f32[128]{0:T(128)S(1)}, f32[128]{0:T(128)}, u32[]{:S(2)}) copy-start(f32[128]{0:T(128)} %param.17) | copy-start | bytes 1540
  42.2 13.2 %all-to-all-start.3 = ((bf16[32,32,128]{2,1,0:T(8,128)(2,1)}), bf16[32,32,128]{2,1,0:T(8,128)(2,1)S(1)}, u32[]{:S(2)}, u32[]{:S(2)}) async-start(bf16[32,32,128]{2,1,0:T(8,128)(2,1)} %edge_grad.1), calls=%async_computation.3 | async-start | bytes 524288 | tf_op jit(solution)/shard_map/all_to_all | solution.py:402
  44.8 0.7 %copy-start.12 = (f32[128]{0:T(128)S(1)}, f32[128]{0:T(128)}, u32[]{:S(2)}) copy-start(f32[128]{0:T(128)} %param.24) | copy-start | bytes 1540

commit v2 on v1

--- a/solution.py
+++ b/solution.py
@@ -149,8 +149,44 @@
     return centre * lax.rsqrt(jnp.mean(centre * centre, axis=1, keepdims=True) + EPSILON)
 
 
+def exchange_bit(first, second, weight):
+    sublane = lax.broadcasted_iota(jnp.int32, first.shape, 1)
+    low = sublane & weight == 0
+    return (
+        jnp.where(low, first, pltpu.roll(second, weight, 1)),
+        jnp.where(low, pltpu.roll(first, SUBLANES - weight, 1), second),
+    )
+
+
+def split_channels(blocks, own):
+    devices, block, cols = blocks.shape
+    tiles = blocks.reshape(devices // 2, 2, block // SUBLANES, SUBLANES, cols)
+    parts = []
+    for tile in range(block // SUBLANES):
+        parts.extend(exchange_bit(tiles[:, 0, tile], tiles[:, 1, tile], own))
+    return [part.reshape(devices * own, cols) for part in parts]
+
+
+def merge_channels(parts, own):
+    rows, cols = parts[0].shape
+    devices = rows // own
+    tiles = [part.reshape(devices // 2, SUBLANES, cols) for part in parts]
+    pairs = [exchange_bit(*pair, own) for pair in zip(tiles[::2], tiles[1::2])]
+    both = [jnp.concatenate(side, axis=1) for side in zip(*pairs)]
+    block = len(parts) * own
+    return jnp.stack(both, axis=1).reshape(devices, block, cols)
+
+
+def trade(parts):
+    rows, cols = parts[0].shape
+    a, b, c, d = (part.reshape(rows // SUBLANES, SUBLANES, cols) for part in parts)
+    (a, b), (c, d) = exchange_bit(a, b, 1), exchange_bit(c, d, 1)
+    (a, c), (b, d) = exchange_bit(a, c, 2), exchange_bit(b, d, 2)
+    return [part.reshape(rows, cols) for part in (a, b, c, d)]
+
+
 def edges_kernel(me_ref, *refs):
-    sources, (out_ref, *local), (wide, arrived) = refs[:9], refs[9:19], refs[19:]
+    sources, (out_ref, *local), arrived = refs[:9], refs[9:19], refs[19]
     copies = [
         pltpu.make_async_copy(source, target, arrived.at[index])
         for index, (source, target) in enumerate(zip(sources, local))
@@ -159,9 +195,7 @@
         copy.start()
     act_ref, gain_ref, bias_ref, rows_ref, valid_ref, *weights = local
     own, cols, chan = act_ref.shape
-    devices, block, _ = out_ref.shape
-    hidden = weights[0].shape[1]
-    half = block // 2
+    half = out_ref.shape[1] // 2
     for copy in copies[:3]:
         copy.wait()
     normed = normed_rows(act_ref[...].reshape(own * cols, chan).astype(F32))
@@ -175,11 +209,8 @@
     for side in range(2):
         proj = dot(weights[2 * side][...], pair_norm, 0, 1)
         edge = mask * jax.nn.sigmoid(dot(weights[2 * side + 1][...], pair_norm, 0, 1)) * proj
-        for r in range(own):
-            wide[side, pl.ds(r, hidden, stride=own), :] = edge[:, r * cols : (r + 1) * cols]
-        out_ref[:, side * half : (side + 1) * half, :] = (
-            wide[side].reshape(devices, half, cols).astype(BF16)
-        )
+        parts = trade([edge[:, r * cols : (r + 1) * cols] for r in range(own)])
+        out_ref[:, side * half : (side + 1) * half, :] = merge_channels(parts, own).astype(BF16)
 
 
 def gates_kernel(
@@ -209,46 +240,12 @@
             kept = mask * sig
             factors[2 * side, :, lanes] = kept
             factors[2 * side + 1, :, lanes] = kept * proj * (1.0 - sig)
-        gate_act = jax.nn.sigmoid(dot(pair_norm, w_gate[...], 0, 0))
-        d_proj = grad_ref[r].astype(F32) * gate_act
-        slope[r] = d_proj * (1.0 - gate_act)
+        gate_act = jax.nn.sigmoid(dot(w_gate[...], pair_norm, 0, 0))
+        d_proj = jnp.transpose(grad_ref[r].astype(F32)) * gate_act
+        slope[:, lanes] = d_proj * (1.0 - gate_act)
         d_normed[pl.ds(r, hidden, stride=own), :] = (
-            dot(w_out[...], d_proj.astype(BF16), 1, 1) * gain_out
+            dot(w_out[...], d_proj.astype(BF16), 1, 0) * gain_out
         )
-
-
-def low_rows(shape):
-    return lax.broadcasted_iota(jnp.int32, shape, 1) < SUBLANES // 2
-
-
-def swap(values):
-    return pltpu.roll(values, SUBLANES // 2, 1)
-
-
-def split_channels(blocks, own):
-    devices, block, cols = blocks.shape
-    tiles = blocks.reshape(devices // 2, 2, block // SUBLANES, SUBLANES, cols)
-    parts = []
-    for tile in range(block // SUBLANES):
-        even, odd = tiles[:, 0, tile], tiles[:, 1, tile]
-        low = low_rows(even.shape)
-        parts.append(jnp.where(low, even, swap(odd)))
-        parts.append(jnp.where(low, swap(even), odd))
-    return [part.reshape(devices * own, cols) for part in parts]
-
-
-def merge_channels(parts, own):
-    rows, cols = parts[0].shape
-    devices = rows // own
-    tiles = [part.reshape(devices // 2, SUBLANES, cols) for part in parts]
-    low = low_rows(tiles[0].shape)
-    even, odd = [], []
-    for first, second in zip(tiles[::2], tiles[1::2]):
-        even.append(jnp.where(low, first, swap(second)))
-        odd.append(jnp.where(low, swap(first), second))
-    both = [jnp.concatenate(side, axis=1) for side in (even, odd)]
-    block = len(parts) * own
-    return jnp.stack(both, axis=1).reshape(devices, block, cols)
 
 
 def triangle_kernel(own, in_ref, _, out_ref, a_ref, b_ref):
@@ -281,29 +278,21 @@
     return centre * inverse, inverse
 
 
-def norm_kernel(hidden, tri_ref, grad_ref, out_ref):
+def norm_kernel(own, tri_ref, grad_ref, slope, gain_ref, bias_ref, w_out, w_gate, out_ref, part_ref):
     devices, block, cols = tri_ref.shape
-    own = devices * block // hidden
+    hidden = w_out.shape[0]
     normed, inverse = tri_normed(tri_ref, hidden, own)
     grad = grad_ref[...].reshape(normed.shape)
     mean_grad = fold(grad, own) / hidden
     mean_proj = fold(grad * normed, own) / hidden
     d_tri = inverse * (grad - mean_grad - normed * mean_proj)
     out_ref[...] = d_tri.reshape(devices, block, cols).astype(BF16)
-
-
-def gate_grad_kernel(tri_ref, slope, gain_ref, bias_ref, w_out, w_gate, out_ref, wide):
-    own, cols, _ = slope.shape
-    hidden = w_out.shape[0]
-    normed, _ = tri_normed(tri_ref, hidden, own)
-    wide[...] = normed.reshape(hidden * own, cols)
     gain = across(gain_ref[...], cols)
     bias = across(bias_ref[...], cols)
-    for r in range(own):
-        tri_norm = (wide[pl.ds(r, hidden, stride=own), :] * gain + bias).astype(BF16)
-        proj_out = dot(tri_norm, w_out[...], 0, 0)
-        d_gate = (slope[r] * proj_out).astype(BF16)
-        out_ref[:, r * cols : (r + 1) * cols] = dot(w_gate[...], d_gate, 1, 1)
+    parts = trade(split_channels(normed.reshape(devices, block, cols), own))
+    tri_norm = jnp.concatenate([(part * gain + bias).astype(BF16) for part in parts], axis=1)
+    d_gate = (slope[...] * dot(w_out[...], tri_norm, 0, 0)).astype(BF16)
+    part_ref[...] = dot(w_gate[...], d_gate, 1, 0)
 
 
 def edge_grad_kernel(own, in_ref, a_ref, b_ref, out_ref):
@@ -319,20 +308,13 @@
         )
 
 
-def input_grad_kernel(in_ref, factors, normed_t, rstd_t, gain_t, gate_part, wap, wag, wbp, wbg, out_ref, wide):
+def input_grad_kernel(in_ref, factors, normed_t, rstd_t, gain_t, gate_part, wap, wag, wbp, wbg, out_ref):
     own, cols, _ = out_ref.shape
-    devices, block, _ = in_ref.shape
-    hidden = wap.shape[1]
-    half = block // 2
-    for side in range(2):
-        wide[side] = (
-            in_ref[:, side * half : (side + 1) * half, :].astype(F32).reshape(devices * half, cols)
-        )
+    half = in_ref.shape[1] // 2
     total = gate_part[...]
     for side, weights in enumerate(((wap, wag), (wbp, wbg))):
-        d_edge = jnp.concatenate(
-            [wide[side, pl.ds(r, hidden, stride=own), :] for r in range(own)], axis=1
-        )
+        blocks = in_ref[:, side * half : (side + 1) * half, :].astype(F32)
+        d_edge = jnp.concatenate(trade(split_channels(blocks, own)), axis=1)
         for at, weight in enumerate(weights):
             total = total + dot(weight[...], (d_edge * factors[2 * side + at]).astype(BF16), 1, 0)
     grad_hat = total * jnp.concatenate([gain_t[...]] * own, axis=1)
@@ -347,10 +329,6 @@
 VMEM = pl.BlockSpec(memory_space=pltpu.VMEM)
 SMEM = pl.BlockSpec(memory_space=pltpu.SMEM)
 HBM = pl.BlockSpec(memory_space=pltpu.HBM)
-
-
-def wide(*shape):
-    return pltpu.VMEM(shape, F32)
 
 
 def call(kernel, name, outs, args, scratch=(), scalars=0, flops=0, spaces=None, limit=32 * 2**20):
@@ -411,7 +389,7 @@
             (pltpu.SMEM if value is residue_mask else pltpu.VMEM)(value.shape, value.dtype)
             for value in first
         ]
-        + [wide(2, hidden * own, cols), pltpu.SemaphoreType.DMA((len(first),))],
+        + [pltpu.SemaphoreType.DMA((len(first),))],
         scalars=1,
         flops=4 * product,
         spaces=[HBM] * len(first),
@@ -427,7 +405,7 @@
             ((1, own * cols), F32),
             ((chan, cols), F32),
             ((hidden * own, cols), F32),
-            ((own, cols, chan), F32),
+            ((chan, own * cols), F32),
         ],
         (me, residue_mask, valid, pair_act, out_grad, gain_in, bias_in, gain_out)
         + (*w_edges, w_gate, w_out),
@@ -447,21 +425,14 @@
         spaces=[VMEM, pl.BlockSpec(memory_space=pl.ANY)],
     )
     tri = exchange(tri)
-    d_tri = call(
-        functools.partial(norm_kernel, hidden),
+    d_tri, gate_part = call(
+        functools.partial(norm_kernel, own),
         "norm",
-        [((dap, block, cols), BF16)],
-        (tri, d_normed),
+        [((dap, block, cols), BF16), ((chan, own * cols), F32)],
+        (tri, d_normed, slope, gain_out, bias_out, w_out, w_gate),
+        flops=2 * product,
     )
     d_tri = exchange(d_tri)
-    gate_part = call(
-        gate_grad_kernel,
-        "gate_grad",
-        [((chan, own * cols), F32)],
-        (tri, slope, gain_out, bias_out, w_out, w_gate),
-        scratch=[wide(hidden * own, cols)],
-        flops=2 * product,
-    )
     d_edges = call(
         functools.partial(edge_grad_kernel, own),
         "edge_grad",
@@ -475,7 +446,6 @@
         "input_grad",
         [((own, cols, chan), BF16)],
         (d_edges, factors, normed_t, rstd_t, gain_t, gate_part, *w_edges),
-        scratch=[wide(2, hidden * own, cols)],
         flops=4 * product,
     )
 
@@ -488,7 +458,7 @@
         ch == 1
         and hidden % dap == 0
         and own == SUBLANES // 2
-        and block % 16 == 0
+        and block == own * own
         and dap % SUBLANES == 0
         and cols == dap * own
         and cols % 128 == chan % 128 == hidden % 128 == 0

time: 56.9 us -> 56.4 us (level)
  blocking collectives: 20.4 us -> 32.8 us
  waiting for transfers between devices: 17.4 us -> 8.68 us
  starting transfers between devices: 9.89 us -> 7.3 us
  Pallas kernels: 7.29 us -> 5.81 us
    all_to_all x2 -> x3, blocking collectives: 20.4 us -> 32.8 us  [exchange(): return lax.all_to_all(value, 'dap', split_axis=0, concat_axis=0, tiled=True)]
    all_to_all x2 -> x1, waiting for transfers between devices: 17.4 us -> 8.68 us  [exchange(): return lax.all_to_all(value, 'dap', split_axis=0, concat_axis=0, tiled=True)]
    all_to_all x2 -> x1, starting transfers between devices: 9.89 us -> 7.3 us  [exchange(): return lax.all_to_all(value, 'dap', split_axis=0, concat_axis=0, tiled=True)]
    pallas_call x7 -> x6, Pallas kernels: 7.29 us -> 5.81 us  [call(): pl.pallas_call(kernel, name=name, out_shape=shapes, in_specs=[SMEM] * sca...]
  transfers between devices with their start and end apart: 2 -> 1, of which waited for: 2 -> 1; matrix products, arithmetic and copies ran while one was open for 0% -> 0% of each run, Pallas kernels for 4% -> 2%
where the time goes in v2:
time: 56.4 us; the launch traced here: 56.1 us
  blocking collectives  32.8 us (58%)
  waiting for transfers between devices  8.68 us (15%)
  starting transfers between devices  7.3 us (13%)
  Pallas kernels  5.81 us (10%)
  local copies, waits for them, and re-layouts  1.29 us (2%)
    all_to_all x3, blocking collectives, exchange(): return lax.all_to_all(value, 'dap', split_axis=0, concat_axis=0, tiled=True)  32.8 us
    all_to_all x1, waiting for transfers between devices, exchange(): return lax.all_to_all(value, 'dap', split_axis=0, concat_axis=0, tiled=True)  8.68 us
    all_to_all x1, starting transfers between devices, exchange(): return lax.all_to_all(value, 'dap', split_axis=0, concat_axis=0, tiled=True)  7.3 us
    pallas_call x6, Pallas kernels, call(): pl.pallas_call(kernel, name=name, out_shape=shapes, in_specs=[SMEM] * sca...  5.81 us
    unnamed x26, local copies, waits for them, and re-layouts  1.29 us
  transfers between devices with their start and end apart: 1, of which 1 were waited for; matrix products, arithmetic and copies ran while one was open for 0% of the time, Pallas kernels for 2%

profile of v2, /device:TPU:0, one launch (start us, length us, event | category | flops | bytes accessed | tf_op | source)
XLA Modules:
  0.0 56.1 jit_solution(7892587744693065031)
XLA Ops:
  0.0 2.3 %edges.1 = bf16[32,32,128]{2,1,0:T(8,128)(2,1)} custom-call(s32[1]{0:T(128)} %bitcast.me_ref, bf16[4,128,128]{2,1,0:T(8,128)(2,1)} %act_ref.1, f32[1,128]{1,0:T(1,128)} %bitcast.8, f32[1,128]{1,0:T(1,128)} %bitcast.10, s32[128]{0:T(128)} %rows_ref.1, s32[1,128]{1,0:T(1,128)} %bitcast.6, bf16[128,128]{1,0:T(8,128)(2,1)} %wap.3, bf16[128,128]{1,0:T(8,128)(2,1)} %wag.3, ...), custom_call_target="tpu_custom_call" | custom-call | flops 67108864 | bytes 526340 | tf_op jit(solution)/shard_map/edges/pallas_call | solution.py:337
  2.4 0.0 copy-start
  2.4 0.0 copy-start.1
  2.4 0.0 copy-start.2
  2.4 0.0 copy-start.3
  2.4 0.0 copy-start.4
  2.4 0.0 copy-start.5
  2.4 0.0 copy-start.6
  2.4 0.0 copy-start.7
  2.5 0.0 copy-start.11
  2.5 7.3 %all-to-all-start = ((bf16[32,32,128]{2,1,0:T(8,128)(2,1)}), bf16[32,32,128]{2,1,0:T(8,128)(2,1)S(1)}, u32[]{:S(2)}, u32[]{:S(2)}) async-start(bf16[32,32,128]{2,1,0:T(8,128)(2,1)} %edges.1), calls=%async_computation | async-start | bytes 524288 | tf_op jit(solution)/shard_map/all_to_all | solution.py:380
  9.8 0.0 copy-start.8
  9.8 0.0 copy-start.9
  9.8 0.0 copy-start.10
  9.8 0.0 copy-done
  9.8 0.0 copy-done.1
  9.8 0.0 copy-done.2
  9.8 0.0 copy-done.3
  9.9 0.0 copy-done.4
  9.9 0.0 copy-done.5
  9.9 0.0 copy-done.6
  9.9 0.0 copy-done.7
  9.9 0.0 copy-done.11
  9.9 0.5 copy-done.8
  10.4 0.0 copy-done.9
  10.4 0.0 copy-done.10
  10.5 1.2 %gates.1 = (f32[4,128,512]{2,1,0:T(8,128)S(1)}, f32[128,512]{1,0:T(8,128)S(1)}, f32[1,512]{1,0:T(1,128)S(1)}, f32[128,128]{1,0:T(8,128)S(1)}, f32[512,128]{1,0:T(8,128)S(1)}, /*index=5*/f32[128,512]{1,0:T(8,128)S(1)}) custom-call(s32[1]{0:T(128)} %bitcast.me_ref, s32[128]{0:T(128)S(1)} %copy-done.8, s32[1,128]{1,0:T(1,128)S(1)} %bitcast.7, ...), custom_call_target="tpu_custom_call" | custom-call | flops 100663296 | bytes 2363908 | tf_op jit(solution)/shard_map/gates/pallas_call | solution.py:337
  11.7 8.7 %all-to-all-done.in_ref = bf16[32,32,128]{2,1,0:T(8,128)(2,1)S(1)} async-done(((bf16[32,32,128]{2,1,0:T(8,128)(2,1)}), bf16[32,32,128]{2,1,0:T(8,128)(2,1)S(1)}, u32[]{:S(2)}, u32[]{:S(2)}) %all-to-all-start) | async-done | bytes 262176 | tf_op jit(solution)/shard_map/all_to_all | solution.py:380
  20.4 0.2 triangle.1
  20.6 10.4 %all_to_all.20.tri_ref = bf16[32,16,128]{2,1,0:T(8,128)(2,1)S(1)} all-to-all(bf16[32,16,128]{2,1,0:T(8,128)(2,1)S(1)} %get-tuple-element.17), channel_id=1, replica_groups=mesh['grp'=1,'dap'=32,'ch'=1] {'dap'}, dimensions={0} | all-to-all | bytes 262144 | tf_op jit(solution)/shard_map/all_to_all | solution.py:380
  31.1 0.0 copy-start.12
  31.1 0.7 %copy-done.12 = f32[128]{0:T(128)S(1)} copy-done((f32[128]{0:T(128)S(1)}, f32[128]{0:T(128)}, u32[]{:S(2)}) %copy-start.12) | copy-done | bytes 536
  31.7 0.6 %norm.1 = (bf16[32,16,128]{2,1,0:T(8,128)(2,1)S(1)}, f32[128,512]{1,0:T(8,128)S(1)}) custom-call(bf16[32,16,128]{2,1,0:T(8,128)(2,1)S(1)} %all_to_all.20.tri_ref, f32[512,128]{1,0:T(8,128)S(1)} %get-tuple-element.16._.grad_ref, f32[128,512]{1,0:T(8,128)S(1)} %get-tuple-element.18.slope, f32[1,128]{1,0:T(1,128)S(1)} %bitcast.13, f32[1,128]{1,0:T(1,128)S(1)} %bitcast.14, ...), custom_call_target="tpu_custom_call" | custom-call | flops 33554432 | bytes 1115136 | tf_op jit(solution)/shard_map/norm/pallas_call | solution.py:337
  32.3 10.0 %all_to_all.21.in_ref = bf16[32,16,128]{2,1,0:T(8,128)(2,1)S(1)} all-to-all(bf16[32,16,128]{2,1,0:T(8,128)(2,1)S(1)} %get-tuple-element.19), channel_id=1, replica_groups=mesh['grp'=1,'dap'=32,'ch'=1] {'dap'}, dimensions={0} | all-to-all | bytes 262144 | tf_op jit(solution)/shard_map/all_to_all | solution.py:380
  42.3 0.2 edge_grad.1
  42.6 12.4 %all_to_all.22.in_ref = bf16[32,32,128]{2,1,0:T(8,128)(2,1)S(1)} all-to-all(bf16[32,32,128]{2,1,0:T(8,128)(2,1)S(1)} %edge_grad.1), channel_id=1, replica_groups=mesh['grp'=1,'dap'=32,'ch'=1] {'dap'}, dimensions={0} | all-to-all | bytes 524288 | tf_op jit(solution)/shard_map/all_to_all | solution.py:380
  55.0 1.2 %input_grad.1 = bf16[4,128,128]{2,1,0:T(8,128)(2,1)} custom-call(bf16[32,32,128]{2,1,0:T(8,128)(2,1)S(1)} %all_to_all.22.in_ref, f32[4,128,512]{2,1,0:T(8,128)S(1)} %get-tuple-element.22.factors, f32[128,512]{1,0:T(8,128)S(1)} %get-tuple-element.23.normed_t, f32[1,512]{1,0:T(1,128)S(1)} %get-tuple-element.24.rstd_t, ...), custom_call_target="tpu_custom_call" | custom-call | flops 67108864 | bytes 2164736 | tf_op jit(solution)/shard_map/input_grad/pallas_call | solution.py:337
Async XLA Ops:
  2.4 7.5 %copy-start = (bf16[4,128,128]{2,1,0:T(8,128)(2,1)S(1)}, bf16[4,128,128]{2,1,0:T(8,128)(2,1)}, u32[]{:S(2)}) copy-start(bf16[4,128,128]{2,1,0:T(8,128)(2,1)} %act_ref.1) | copy-start | bytes 393220
  2.4 7.5 %copy-start.1 = (bf16[128,128]{1,0:T(8,128)(2,1)S(1)}, bf16[128,128]{1,0:T(8,128)(2,1)}, u32[]{:S(2)}) copy-start(bf16[128,128]{1,0:T(8,128)(2,1)} %wap.3) | copy-start | bytes 98308
  2.4 7.5 %copy-start.2 = (bf16[128,128]{1,0:T(8,128)(2,1)S(1)}, bf16[128,128]{1,0:T(8,128)(2,1)}, u32[]{:S(2)}) copy-start(bf16[128,128]{1,0:T(8,128)(2,1)} %wag.3) | copy-start | bytes 98308
  2.4 7.5 %copy-start.3 = (bf16[128,128]{1,0:T(8,128)(2,1)S(1)}, bf16[128,128]{1,0:T(8,128)(2,1)}, u32[]{:S(2)}) copy-start(bf16[128,128]{1,0:T(8,128)(2,1)} %wbp.3) | copy-start | bytes 98308
  2.4 7.4 %copy-start.4 = (bf16[128,128]{1,0:T(8,128)(2,1)S(1)}, bf16[128,128]{1,0:T(8,128)(2,1)}, u32[]{:S(2)}) copy-start(bf16[128,128]{1,0:T(8,128)(2,1)} %wbg.3) | copy-start | bytes 98308
  2.4 7.4 %copy-start.5 = (bf16[128,128]{1,0:T(8,128)(2,1)S(1)}, bf16[128,128]{1,0:T(8,128)(2,1)}, u32[]{:S(2)}) copy-start(bf16[128,128]{1,0:T(8,128)(2,1)} %w_gate.3) | copy-start | bytes 98308
  2.4 7.4 %copy-start.6 = (bf16[128,128]{1,0:T(8,128)(2,1)S(1)}, bf16[128,128]{1,0:T(8,128)(2,1)}, u32[]{:S(2)}) copy-start(bf16[128,128]{1,0:T(8,128)(2,1)} %w_out.3) | copy-start | bytes 98308
  2.4 7.4 %copy-start.7 = (bf16[4,128,128]{2,1,0:T(8,128)(2,1)S(1)}, bf16[4,128,128]{2,1,0:T(8,128)(2,1)}, u32[]{:S(2)}) copy-start(bf16[4,128,128]{2,1,0:T(8,128)(2,1)} %grad_ref.1) | copy-start | bytes 393220
  2.5 7.4 %copy-start.11 = (f32[128]{0:T(128)S(1)}, f32[128]{0:T(128)}, u32[]{:S(2)}) copy-start(f32[128]{0:T(128)} %param.23) | copy-start | bytes 1540
  2.5 17.9 %all-to-all-start = ((bf16[32,32,128]{2,1,0:T(8,128)(2,1)}), bf16[32,32,128]{2,1,0:T(8,128)(2,1)S(1)}, u32[]{:S(2)}, u32[]{:S(2)}) async-start(bf16[32,32,128]{2,1,0:T(8,128)(2,1)} %edges.1), calls=%async_computation | async-start | bytes 524288 | tf_op jit(solution)/shard_map/all_to_all | solution.py:380
  9.8 0.7 %copy-start.8 = (s32[128]{0:T(128)S(1)}, s32[128]{0:T(128)}, u32[]{:S(2)}) copy-start(s32[128]{0:T(128)} %rows_ref.1) | copy-start | bytes 1540
  9.8 0.7 %copy-start.9 = (f32[128]{0:T(128)S(1)}, f32[128]{0:T(128)}, u32[]{:S(2)}) copy-start(f32[128]{0:T(128)} %param.16) | copy-start | bytes 1540
  9.8 0.7 %copy-start.10 = (f32[128]{0:T(128)S(1)}, f32[128]{0:T(128)}, u32[]{:S(2)}) copy-start(f32[128]{0:T(128)} %param.17) | copy-start | bytes 1540
  31.1 0.7 %copy-start.12 = (f32[128]{0:T(128)S(1)}, f32[128]{0:T(128)}, u32[]{:S(2)}) copy-start(f32[128]{0:T(128)} %param.24) | copy-start | bytes 1540

commit v3 on v2

--- a/solution.py
+++ b/solution.py
@@ -214,8 +214,9 @@
 
 
 def gates_kernel(
-    me_ref, rows_ref, valid_ref, act_ref, grad_ref, gain_ref, bias_ref, gain_out_ref,
-    wap, wag, wbp, wbg, w_gate, w_out, factors, normed_t, rstd_t, gain_t, d_normed, slope,
+    me_ref, rows_ref, valid_ref, act_ref, grad_ref, gain_ref, bias_ref, gain_out_ref, bias_out_ref,
+    wap, wag, wbp, wbg, w_gate, w_out,
+    factors, normed_t, rstd_t, gain_t, d_normed, slope, gain_out_t, bias_out_t,
 ):
     own, cols, _ = act_ref.shape
     hidden = wap.shape[1]
@@ -224,6 +225,8 @@
     bias = across(bias_ref[...], cols)
     gain_out = across(gain_out_ref[...], cols)
     gain_t[...] = gain
+    gain_out_t[...] = gain_out
+    bias_out_t[...] = across(bias_out_ref[...], cols)
     for r in range(own):
         act = jnp.transpose(act_ref[r].astype(F32))
         centre = act - jnp.mean(act, axis=0, keepdims=True)
@@ -278,7 +281,7 @@
     return centre * inverse, inverse
 
 
-def norm_kernel(own, tri_ref, grad_ref, slope, gain_ref, bias_ref, w_out, w_gate, out_ref, part_ref):
+def norm_kernel(own, tri_ref, grad_ref, slope, gain, bias, w_out, w_gate, out_ref, part_ref):
     devices, block, cols = tri_ref.shape
     hidden = w_out.shape[0]
     normed, inverse = tri_normed(tri_ref, hidden, own)
@@ -287,10 +290,8 @@
     mean_proj = fold(grad * normed, own) / hidden
     d_tri = inverse * (grad - mean_grad - normed * mean_proj)
     out_ref[...] = d_tri.reshape(devices, block, cols).astype(BF16)
-    gain = across(gain_ref[...], cols)
-    bias = across(bias_ref[...], cols)
     parts = trade(split_channels(normed.reshape(devices, block, cols), own))
-    tri_norm = jnp.concatenate([(part * gain + bias).astype(BF16) for part in parts], axis=1)
+    tri_norm = jnp.concatenate([(part * gain[...] + bias[...]).astype(BF16) for part in parts], axis=1)
     d_gate = (slope[...] * dot(w_out[...], tri_norm, 0, 0)).astype(BF16)
     part_ref[...] = dot(w_gate[...], d_gate, 1, 0)
 
@@ -396,7 +397,7 @@
         limit=None,
     )
     edges = exchange(edges)
-    factors, normed_t, rstd_t, gain_t, d_normed, slope = call(
+    factors, normed_t, rstd_t, gain_t, d_normed, slope, gain_out_t, bias_out_t = call(
         gates_kernel,
         "gates",
         [
@@ -406,9 +407,11 @@
             ((chan, cols), F32),
             ((hidden * own, cols), F32),
             ((chan, own * cols), F32),
+            ((hidden, cols), F32),
+            ((hidden, cols), F32),
         ],
         (me, residue_mask, valid, pair_act, out_grad, gain_in, bias_in, gain_out)
-        + (*w_edges, w_gate, w_out),
+        + (bias_out, *w_edges, w_gate, w_out),
         scalars=2,
         flops=6 * product,
     )
@@ -429,7 +432,7 @@
         functools.partial(norm_kernel, own),
         "norm",
         [((dap, block, cols), BF16), ((chan, own * cols), F32)],
-        (tri, d_normed, slope, gain_out, bias_out, w_out, w_gate),
+        (tri, d_normed, slope, gain_out_t, bias_out_t, w_out, w_gate),
         flops=2 * product,
     )
     d_tri = exchange(d_tri)

time: 56.4 us -> 55.8 us (0.989)
  local copies, waits for them, and re-layouts: 1.29 us -> 0.63 us
    unnamed x26, local copies, waits for them, and re-layouts: 1.29 us -> 0.63 us
where the time goes in v3:
time: 55.8 us; the launch traced here: 55.5 us
  blocking collectives  32.8 us (59%)
  waiting for transfers between devices  8.68 us (16%)
  starting transfers between devices  7.3 us (13%)
  Pallas kernels  5.85 us (10%)
  local copies, waits for them, and re-layouts  0.63 us (1%)
    all_to_all x3, blocking collectives, exchange(): return lax.all_to_all(value, 'dap', split_axis=0, concat_axis=0, tiled=True)  32.8 us
    all_to_all x1, waiting for transfers between devices, exchange(): return lax.all_to_all(value, 'dap', split_axis=0, concat_axis=0, tiled=True)  8.68 us
    all_to_all x1, starting transfers between devices, exchange(): return lax.all_to_all(value, 'dap', split_axis=0, concat_axis=0, tiled=True)  7.3 us
    pallas_call x6, Pallas kernels, call(): pl.pallas_call(kernel, name=name, out_shape=shapes, in_specs=[SMEM] * sca...  5.85 us
  transfers between devices with their start and end apart: 1, of which 1 were waited for; matrix products, arithmetic and copies ran while one was open for 0% of the time, Pallas kernels for 2%

profile of v3, /device:TPU:0, one launch (start us, length us, event | category | flops | bytes accessed | tf_op | source)
XLA Modules:
  0.0 55.5 jit_solution(3200390909827568504)
XLA Ops:
  0.0 2.3 %edges.1 = bf16[32,32,128]{2,1,0:T(8,128)(2,1)} custom-call(s32[1]{0:T(128)} %bitcast.me_ref, bf16[4,128,128]{2,1,0:T(8,128)(2,1)} %act_ref.1, f32[1,128]{1,0:T(1,128)} %bitcast.8, f32[1,128]{1,0:T(1,128)} %bitcast.10, s32[128]{0:T(128)} %rows_ref.1, s32[1,128]{1,0:T(1,128)} %bitcast.6, bf16[128,128]{1,0:T(8,128)(2,1)} %wap.3, bf16[128,128]{1,0:T(8,128)(2,1)} %wag.3, ...), custom_call_target="tpu_custom_call" | custom-call | flops 67108864 | bytes 526340 | tf_op jit(solution)/shard_map/edges/pallas_call | solution.py:338
  2.4 0.0 copy-start
  2.4 0.0 copy-start.1
  2.4 0.0 copy-start.2
  2.4 0.0 copy-start.3
  2.4 0.0 copy-start.4
  2.4 0.0 copy-start.5
  2.4 0.0 copy-start.6
  2.4 0.0 copy-start.7
  2.5 0.0 copy-start.11
  2.5 0.0 copy-start.12
  2.5 7.3 %all-to-all-start = ((bf16[32,32,128]{2,1,0:T(8,128)(2,1)}), bf16[32,32,128]{2,1,0:T(8,128)(2,1)S(1)}, u32[]{:S(2)}, u32[]{:S(2)}) async-start(bf16[32,32,128]{2,1,0:T(8,128)(2,1)} %edges.1), calls=%async_computation | async-start | bytes 524288 | tf_op jit(solution)/shard_map/all_to_all | solution.py:381
  9.8 0.0 copy-start.8
  9.8 0.0 copy-start.9
  9.8 0.0 copy-start.10
  9.8 0.0 copy-done
  9.8 0.0 copy-done.1
  9.8 0.0 copy-done.2
  9.9 0.0 copy-done.3
  9.9 0.0 copy-done.4
  9.9 0.0 copy-done.5
  9.9 0.0 copy-done.6
  9.9 0.0 copy-done.7
  9.9 0.0 copy-done.11
  9.9 0.0 copy-done.12
  9.9 0.5 copy-done.8
  10.4 0.0 copy-done.9
  10.5 0.0 copy-done.10
  10.5 1.2 %gates.1 = (f32[4,128,512]{2,1,0:T(8,128)S(1)}, f32[128,512]{1,0:T(8,128)S(1)}, f32[1,512]{1,0:T(1,128)S(1)}, f32[128,128]{1,0:T(8,128)S(1)}, f32[512,128]{1,0:T...) custom-call(s32[1]{0:T(128)} %bitcast.me_ref, s32[128]{0:T(128)S(1)} %copy-done.8, ...), custom_call_target="tpu_custom_call" | custom-call | flops 100663296 | bytes 2495492 | tf_op jit(solution)/shard_map/gates/pallas_call | solution.py:338
  11.7 8.7 %all-to-all-done.in_ref = bf16[32,32,128]{2,1,0:T(8,128)(2,1)S(1)} async-done(((bf16[32,32,128]{2,1,0:T(8,128)(2,1)}), bf16[32,32,128]{2,1,0:T(8,128)(2,1)S(1)}, u32[]{:S(2)}, u32[]{:S(2)}) %all-to-all-start) | async-done | bytes 262176 | tf_op jit(solution)/shard_map/all_to_all | solution.py:381
  20.4 0.2 triangle.1
  20.6 10.4 %all_to_all.20.tri_ref = bf16[32,16,128]{2,1,0:T(8,128)(2,1)S(1)} all-to-all(bf16[32,16,128]{2,1,0:T(8,128)(2,1)S(1)} %get-tuple-element.19), channel_id=1, replica_groups=mesh['grp'=1,'dap'=32,'ch'=1] {'dap'}, dimensions={0} | all-to-all | bytes 262144 | tf_op jit(solution)/shard_map/all_to_all | solution.py:381
  31.1 0.6 %norm.1 = (bf16[32,16,128]{2,1,0:T(8,128)(2,1)S(1)}, f32[128,512]{1,0:T(8,128)S(1)}) custom-call(bf16[32,16,128]{2,1,0:T(8,128)(2,1)S(1)} %all_to_all.20.tri_ref, f32[512,128]{1,0:T(8,128)S(1)} %get-tuple-element.18._.grad_ref, f32[128,512]{1,0:T(8,128)S(1)} %get-tuple-element.20.slope, f32[128,128]{1,0:T(8,128)S(1)} %get-tuple-element.21.gain, ...), custom_call_target="tpu_custom_call" | custom-call | flops 33554432 | bytes 1245184 | tf_op jit(solution)/shard_map/norm/pallas_call | solution.py:338
  31.7 10.0 %all_to_all.21.in_ref = bf16[32,16,128]{2,1,0:T(8,128)(2,1)S(1)} all-to-all(bf16[32,16,128]{2,1,0:T(8,128)(2,1)S(1)} %get-tuple-element.23), channel_id=1, replica_groups=mesh['grp'=1,'dap'=32,'ch'=1] {'dap'}, dimensions={0} | all-to-all | bytes 262144 | tf_op jit(solution)/shard_map/all_to_all | solution.py:381
  41.7 0.2 edge_grad.1
  42.0 12.4 %all_to_all.22.in_ref = bf16[32,32,128]{2,1,0:T(8,128)(2,1)S(1)} all-to-all(bf16[32,32,128]{2,1,0:T(8,128)(2,1)S(1)} %edge_grad.1), channel_id=1, replica_groups=mesh['grp'=1,'dap'=32,'ch'=1] {'dap'}, dimensions={0} | all-to-all | bytes 524288 | tf_op jit(solution)/shard_map/all_to_all | solution.py:381
  54.3 1.2 %input_grad.1 = bf16[4,128,128]{2,1,0:T(8,128)(2,1)} custom-call(bf16[32,32,128]{2,1,0:T(8,128)(2,1)S(1)} %all_to_all.22.in_ref, f32[4,128,512]{2,1,0:T(8,128)S(1)} %get-tuple-element.26.factors, f32[128,512]{1,0:T(8,128)S(1)} %get-tuple-element.27.normed_t, f32[1,512]{1,0:T(1,128)S(1)} %get-tuple-element.28.rstd_t, ...), custom_call_target="tpu_custom_call" | custom-call | flops 67108864 | bytes 2164736 | tf_op jit(solution)/shard_map/input_grad/pallas_call | solution.py:338
Async XLA Ops:
  2.4 7.5 %copy-start = (bf16[4,128,128]{2,1,0:T(8,128)(2,1)S(1)}, bf16[4,128,128]{2,1,0:T(8,128)(2,1)}, u32[]{:S(2)}) copy-start(bf16[4,128,128]{2,1,0:T(8,128)(2,1)} %act_ref.1) | copy-start | bytes 393220
  2.4 7.5 %copy-start.1 = (bf16[128,128]{1,0:T(8,128)(2,1)S(1)}, bf16[128,128]{1,0:T(8,128)(2,1)}, u32[]{:S(2)}) copy-start(bf16[128,128]{1,0:T(8,128)(2,1)} %wap.3) | copy-start | bytes 98308
  2.4 7.5 %copy-start.2 = (bf16[128,128]{1,0:T(8,128)(2,1)S(1)}, bf16[128,128]{1,0:T(8,128)(2,1)}, u32[]{:S(2)}) copy-start(bf16[128,128]{1,0:T(8,128)(2,1)} %wag.3) | copy-start | bytes 98308
  2.4 7.5 %copy-start.3 = (bf16[128,128]{1,0:T(8,128)(2,1)S(1)}, bf16[128,128]{1,0:T(8,128)(2,1)}, u32[]{:S(2)}) copy-start(bf16[128,128]{1,0:T(8,128)(2,1)} %wbp.3) | copy-start | bytes 98308
  2.4 7.5 %copy-start.4 = (bf16[128,128]{1,0:T(8,128)(2,1)S(1)}, bf16[128,128]{1,0:T(8,128)(2,1)}, u32[]{:S(2)}) copy-start(bf16[128,128]{1,0:T(8,128)(2,1)} %wbg.3) | copy-start | bytes 98308
  2.4 7.5 %copy-start.5 = (bf16[4,128,128]{2,1,0:T(8,128)(2,1)S(1)}, bf16[4,128,128]{2,1,0:T(8,128)(2,1)}, u32[]{:S(2)}) copy-start(bf16[4,128,128]{2,1,0:T(8,128)(2,1)} %grad_ref.1) | copy-start | bytes 393220
  2.4 7.5 %copy-start.6 = (bf16[128,128]{1,0:T(8,128)(2,1)S(1)}, bf16[128,128]{1,0:T(8,128)(2,1)}, u32[]{:S(2)}) copy-start(bf16[128,128]{1,0:T(8,128)(2,1)} %w_gate.3) | copy-start | bytes 98308
  2.4 7.5 %copy-start.7 = (bf16[128,128]{1,0:T(8,128)(2,1)S(1)}, bf16[128,128]{1,0:T(8,128)(2,1)}, u32[]{:S(2)}) copy-start(bf16[128,128]{1,0:T(8,128)(2,1)} %w_out.3) | copy-start | bytes 98308
  2.5 7.5 %copy-start.11 = (f32[128]{0:T(128)S(1)}, f32[128]{0:T(128)}, u32[]{:S(2)}) copy-start(f32[128]{0:T(128)} %param.23) | copy-start | bytes 1540
  2.5 7.4 %copy-start.12 = (f32[128]{0:T(128)S(1)}, f32[128]{0:T(128)}, u32[]{:S(2)}) copy-start(f32[128]{0:T(128)} %param.24) | copy-start | bytes 1540
  2.5 17.9 %all-to-all-start = ((bf16[32,32,128]{2,1,0:T(8,128)(2,1)}), bf16[32,32,128]{2,1,0:T(8,128)(2,1)S(1)}, u32[]{:S(2)}, u32[]{:S(2)}) async-start(bf16[32,32,128]{2,1,0:T(8,128)(2,1)} %edges.1), calls=%async_computation | async-start | bytes 524288 | tf_op jit(solution)/shard_map/all_to_all | solution.py:381
  9.8 0.7 %copy-start.8 = (s32[128]{0:T(128)S(1)}, s32[128]{0:T(128)}, u32[]{:S(2)}) copy-start(s32[128]{0:T(128)} %rows_ref.1) | copy-start | bytes 1540
  9.8 0.7 %copy-start.9 = (f32[128]{0:T(128)S(1)}, f32[128]{0:T(128)}, u32[]{:S(2)}) copy-start(f32[128]{0:T(128)} %param.16) | copy-start | bytes 1540
  9.8 0.7 %copy-start.10 = (f32[128]{0:T(128)S(1)}, f32[128]{0:T(128)}, u32[]{:S(2)}) copy-start(f32[128]{0:T(128)} %param.17) | copy-start | bytes 1540

commit v4 on v3

--- a/solution.py
+++ b/solution.py
@@ -132,6 +132,7 @@
 F32 = jnp.float32
 BF16 = jnp.bfloat16
 SUBLANES = 8
+LEVELS = 4
 
 
 def dot(lhs, rhs, lhs_dim, rhs_dim):
@@ -156,6 +157,16 @@
         jnp.where(low, first, pltpu.roll(second, weight, 1)),
         jnp.where(low, pltpu.roll(first, SUBLANES - weight, 1), second),
     )
+
+
+def mesh_order(blocks):
+    count, *rest = blocks.shape
+    return jnp.swapaxes(blocks.reshape(count // LEVELS, LEVELS, *rest), 0, 1).reshape(blocks.shape)
+
+
+def list_order(blocks):
+    count, *rest = blocks.shape
+    return jnp.swapaxes(blocks.reshape(LEVELS, count // LEVELS, *rest), 0, 1).reshape(blocks.shape)
 
 
 def split_channels(blocks, own):
@@ -254,7 +265,9 @@
 def triangle_kernel(own, in_ref, _, out_ref, a_ref, b_ref):
     half = out_ref.shape[1]
     sides = [
-        split_channels(in_ref[:, side * half : (side + 1) * half, :].astype(F32), own)
+        split_channels(
+            mesh_order(in_ref[:, side * half : (side + 1) * half, :].astype(F32)), own
+        )
         for side in range(2)
     ]
     tri = []
@@ -262,7 +275,7 @@
         a_ref[c] = edge_a.astype(BF16)
         b_ref[c] = edge_b.astype(BF16)
         tri.append(dot(a_ref[c], b_ref[c], 1, 1))
-    out_ref[...] = merge_channels(tri, own).astype(BF16)
+    out_ref[...] = list_order(merge_channels(tri, own)).astype(BF16)
 
 
 def fold(values, own):
@@ -299,13 +312,13 @@
 def edge_grad_kernel(own, in_ref, a_ref, b_ref, out_ref):
     block = in_ref.shape[1]
     grads = ([], [])
-    for c, part in enumerate(split_channels(in_ref[...].astype(F32), own)):
+    for c, part in enumerate(split_channels(mesh_order(in_ref[...].astype(F32)), own)):
         d_tri = part.astype(BF16)
         grads[0].append(dot(d_tri, b_ref[c], 1, 0))
         grads[1].append(dot(d_tri, a_ref[c], 0, 0))
     for side in range(2):
         out_ref[:, side * block : (side + 1) * block, :] = (
-            merge_channels(grads[side], own).astype(BF16)
+            list_order(merge_channels(grads[side], own)).astype(BF16)
         )
 
 
@@ -377,8 +390,12 @@
     w_edges = (w_a_proj, w_a_gate, w_b_proj, w_b_gate)
     product = 2 * own * cols * chan * hidden
 
+    listed = [quarter * (dap // LEVELS) + at for at in range(dap // LEVELS) for quarter in range(LEVELS)]
+
     def exchange(value):
-        return lax.all_to_all(value, "dap", split_axis=0, concat_axis=0, tiled=True)
+        return lax.all_to_all(
+            value, "dap", split_axis=0, concat_axis=0, axis_index_groups=[listed], tiled=True
+        )
 
     first = (pair_act, gain_in, bias_in, residue_mask, valid, *w_edges)
     edges = call(

time: 55.8 us -> 55.5 us (level)
  no operation moved by 1% of the time
where the time goes in v4:
time: 55.5 us; the launch traced here: 55.2 us
  blocking collectives  33 us (59%)
  waiting for transfers between devices  8.27 us (15%)
  starting transfers between devices  7.3 us (13%)
  Pallas kernels  5.85 us (11%)
  local copies, waits for them, and re-layouts  0.63 us (1%)
    all_to_all x3, blocking collectives, exchange(): lax.all_to_all(value, 'dap', split_axis=0, concat_axis=0, axis_index_grou...  33 us
    all_to_all x1, waiting for transfers between devices, exchange(): lax.all_to_all(value, 'dap', split_axis=0, concat_axis=0, axis_index_grou...  8.27 us
    all_to_all x1, starting transfers between devices, exchange(): lax.all_to_all(value, 'dap', split_axis=0, concat_axis=0, axis_index_grou...  7.3 us
    pallas_call x6, Pallas kernels, call(): pl.pallas_call(kernel, name=name, out_shape=shapes, in_specs=[SMEM] * sca...  5.85 us
  transfers between devices with their start and end apart: 1, of which 1 were waited for; matrix products, arithmetic and copies ran while one was open for 0% of the time, Pallas kernels for 2%

profile of v4, /device:TPU:0, one launch (start us, length us, event | category | flops | bytes accessed | tf_op | source)
XLA Modules:
  0.0 55.2 jit_solution(11151723738146919271)
XLA Ops:
  0.0 2.3 %edges.1 = bf16[32,32,128]{2,1,0:T(8,128)(2,1)} custom-call(s32[1]{0:T(128)} %bitcast.me_ref, bf16[4,128,128]{2,1,0:T(8,128)(2,1)} %act_ref.1, f32[1,128]{1,0:T(1,128)} %bitcast.8, f32[1,128]{1,0:T(1,128)} %bitcast.10, s32[128]{0:T(128)} %rows_ref.1, s32[1,128]{1,0:T(1,128)} %bitcast.6, bf16[128,128]{1,0:T(8,128)(2,1)} %wap.3, bf16[128,128]{1,0:T(8,128)(2,1)} %wag.3, ...), custom_call_target="tpu_custom_call" | custom-call | flops 67108864 | bytes 526340 | tf_op jit(solution)/shard_map/edges/pallas_call | solution.py:351
  2.4 0.0 copy-start
  2.4 0.0 copy-start.1
  2.4 0.0 copy-start.2
  2.4 0.0 copy-start.3
  2.4 0.0 copy-start.4
  2.4 0.0 copy-start.5
  2.4 0.0 copy-start.6
  2.4 0.0 copy-start.7
  2.5 0.0 copy-start.11
  2.5 0.0 copy-start.12
  2.5 7.3 %all-to-all-start = ((bf16[32,32,128]{2,1,0:T(8,128)(2,1)}), bf16[32,32,128]{2,1,0:T(8,128)(2,1)S(1)}, u32[]{:S(2)}, u32[]{:S(2)}) async-start(bf16[32,32,128]{2,1,0:T(8,128)(2,1)} %edges.1), calls=%async_computation | async-start | bytes 524288 | tf_op jit(solution)/shard_map/all_to_all | solution.py:396
  9.8 0.0 copy-start.8
  9.8 0.0 copy-start.9
  9.8 0.0 copy-start.10
  9.8 0.0 copy-done
  9.8 0.0 copy-done.1
  9.8 0.0 copy-done.2
  9.9 0.0 copy-done.3
  9.9 0.0 copy-done.4
  9.9 0.0 copy-done.5
  9.9 0.0 copy-done.6
  9.9 0.0 copy-done.7
  9.9 0.0 copy-done.11
  9.9 0.0 copy-done.12
  9.9 0.5 copy-done.8
  10.4 0.0 copy-done.9
  10.5 0.0 copy-done.10
  10.5 1.2 %gates.1 = (f32[4,128,512]{2,1,0:T(8,128)S(1)}, f32[128,512]{1,0:T(8,128)S(1)}, f32[1,512]{1,0:T(1,128)S(1)}, f32[128,128]{1,0:T(8,128)S(1)}, f32[512,128]{1,0:T...) custom-call(s32[1]{0:T(128)} %bitcast.me_ref, s32[128]{0:T(128)S(1)} %copy-done.8, ...), custom_call_target="tpu_custom_call" | custom-call | flops 100663296 | bytes 2495492 | tf_op jit(solution)/shard_map/gates/pallas_call | solution.py:351
  11.7 8.3 %all-to-all-done.in_ref = bf16[32,32,128]{2,1,0:T(8,128)(2,1)S(1)} async-done(((bf16[32,32,128]{2,1,0:T(8,128)(2,1)}), bf16[32,32,128]{2,1,0:T(8,128)(2,1)S(1)}, u32[]{:S(2)}, u32[]{:S(2)}) %all-to-all-start) | async-done | bytes 262176 | tf_op jit(solution)/shard_map/all_to_all | solution.py:396
  20.0 0.2 triangle.1
  20.2 10.9 %all_to_all.20.tri_ref = bf16[32,16,128]{2,1,0:T(8,128)(2,1)S(1)} all-to-all(bf16[32,16,128]{2,1,0:T(8,128)(2,1)S(1)} %get-tuple-element.19), channel_id=1, replica_groups={{0,8,16,24,1,9,17,25,2,10,18,26,3,11,19,27,4,12,20,28,5,13,21,29,6,14,2..., dimensions={0} | all-to-all | bytes 262144 | tf_op jit(solution)/shard_map/all_to_all | solution.py:396
  31.2 0.6 %norm.1 = (bf16[32,16,128]{2,1,0:T(8,128)(2,1)S(1)}, f32[128,512]{1,0:T(8,128)S(1)}) custom-call(bf16[32,16,128]{2,1,0:T(8,128)(2,1)S(1)} %all_to_all.20.tri_ref, f32[512,128]{1,0:T(8,128)S(1)} %get-tuple-element.18._.grad_ref, f32[128,512]{1,0:T(8,128)S(1)} %get-tuple-element.20.slope, f32[128,128]{1,0:T(8,128)S(1)} %get-tuple-element.21.gain, ...), custom_call_target="tpu_custom_call" | custom-call | flops 33554432 | bytes 1245184 | tf_op jit(solution)/shard_map/norm/pallas_call | solution.py:351
  31.8 10.1 %all_to_all.21.in_ref = bf16[32,16,128]{2,1,0:T(8,128)(2,1)S(1)} all-to-all(bf16[32,16,128]{2,1,0:T(8,128)(2,1)S(1)} %get-tuple-element.23), channel_id=1, replica_groups={{0,8,16,24,1,9,17,25,2,10,18,26,3,11,19,27,4,12,20,28,5,13,21,29,6,14,2..., dimensions={0} | all-to-all | bytes 262144 | tf_op jit(solution)/shard_map/all_to_all | solution.py:396
  41.9 0.2 edge_grad.1
  42.2 11.9 %all_to_all.22.in_ref = bf16[32,32,128]{2,1,0:T(8,128)(2,1)S(1)} all-to-all(bf16[32,32,128]{2,1,0:T(8,128)(2,1)S(1)} %edge_grad.1), channel_id=1, replica_groups={{0,8,16,24,1,9,17,25,2,10,18,26,3,11,19,27,4,12,20,28,5,13,21,29,6,14,2..., dimensions={0} | all-to-all | bytes 524288 | tf_op jit(solution)/shard_map/all_to_all | solution.py:396
  54.1 1.2 %input_grad.1 = bf16[4,128,128]{2,1,0:T(8,128)(2,1)} custom-call(bf16[32,32,128]{2,1,0:T(8,128)(2,1)S(1)} %all_to_all.22.in_ref, f32[4,128,512]{2,1,0:T(8,128)S(1)} %get-tuple-element.26.factors, f32[128,512]{1,0:T(8,128)S(1)} %get-tuple-element.27.normed_t, f32[1,512]{1,0:T(1,128)S(1)} %get-tuple-element.28.rstd_t, ...), custom_call_target="tpu_custom_call" | custom-call | flops 67108864 | bytes 2164736 | tf_op jit(solution)/shard_map/input_grad/pallas_call | solution.py:351
Async XLA Ops:
  2.4 7.5 %copy-start = (bf16[4,128,128]{2,1,0:T(8,128)(2,1)S(1)}, bf16[4,128,128]{2,1,0:T(8,128)(2,1)}, u32[]{:S(2)}) copy-start(bf16[4,128,128]{2,1,0:T(8,128)(2,1)} %act_ref.1) | copy-start | bytes 393220
  2.4 7.5 %copy-start.1 = (bf16[128,128]{1,0:T(8,128)(2,1)S(1)}, bf16[128,128]{1,0:T(8,128)(2,1)}, u32[]{:S(2)}) copy-start(bf16[128,128]{1,0:T(8,128)(2,1)} %wap.3) | copy-start | bytes 98308
  2.4 7.5 %copy-start.2 = (bf16[128,128]{1,0:T(8,128)(2,1)S(1)}, bf16[128,128]{1,0:T(8,128)(2,1)}, u32[]{:S(2)}) copy-start(bf16[128,128]{1,0:T(8,128)(2,1)} %wag.3) | copy-start | bytes 98308
  2.4 7.5 %copy-start.3 = (bf16[128,128]{1,0:T(8,128)(2,1)S(1)}, bf16[128,128]{1,0:T(8,128)(2,1)}, u32[]{:S(2)}) copy-start(bf16[128,128]{1,0:T(8,128)(2,1)} %wbp.3) | copy-start | bytes 98308
  2.4 7.5 %copy-start.4 = (bf16[128,128]{1,0:T(8,128)(2,1)S(1)}, bf16[128,128]{1,0:T(8,128)(2,1)}, u32[]{:S(2)}) copy-start(bf16[128,128]{1,0:T(8,128)(2,1)} %wbg.3) | copy-start | bytes 98308
  2.4 7.5 %copy-start.5 = (bf16[4,128,128]{2,1,0:T(8,128)(2,1)S(1)}, bf16[4,128,128]{2,1,0:T(8,128)(2,1)}, u32[]{:S(2)}) copy-start(bf16[4,128,128]{2,1,0:T(8,128)(2,1)} %grad_ref.1) | copy-start | bytes 393220
  2.4 7.5 %copy-start.6 = (bf16[128,128]{1,0:T(8,128)(2,1)S(1)}, bf16[128,128]{1,0:T(8,128)(2,1)}, u32[]{:S(2)}) copy-start(bf16[128,128]{1,0:T(8,128)(2,1)} %w_gate.3) | copy-start | bytes 98308
  2.4 7.5 %copy-start.7 = (bf16[128,128]{1,0:T(8,128)(2,1)S(1)}, bf16[128,128]{1,0:T(8,128)(2,1)}, u32[]{:S(2)}) copy-start(bf16[128,128]{1,0:T(8,128)(2,1)} %w_out.3) | copy-start | bytes 98308
  2.5 7.5 %copy-start.11 = (f32[128]{0:T(128)S(1)}, f32[128]{0:T(128)}, u32[]{:S(2)}) copy-start(f32[128]{0:T(128)} %param.23) | copy-start | bytes 1540
  2.5 7.4 %copy-start.12 = (f32[128]{0:T(128)S(1)}, f32[128]{0:T(128)}, u32[]{:S(2)}) copy-start(f32[128]{0:T(128)} %param.24) | copy-start | bytes 1540
  2.5 17.5 %all-to-all-start = ((bf16[32,32,128]{2,1,0:T(8,128)(2,1)}), bf16[32,32,128]{2,1,0:T(8,128)(2,1)S(1)}, u32[]{:S(2)}, u32[]{:S(2)}) async-start(bf16[32,32,128]{2,1,0:T(8,128)(2,1)} %edges.1), calls=%async_computation | async-start | bytes 524288 | tf_op jit(solution)/shard_map/all_to_all | solution.py:396
  9.8 0.7 %copy-start.8 = (s32[128]{0:T(128)S(1)}, s32[128]{0:T(128)}, u32[]{:S(2)}) copy-start(s32[128]{0:T(128)} %rows_ref.1) | copy-start | bytes 1540
  9.8 0.7 %copy-start.9 = (f32[128]{0:T(128)S(1)}, f32[128]{0:T(128)}, u32[]{:S(2)}) copy-start(f32[128]{0:T(128)} %param.16) | copy-start | bytes 1540
  9.8 0.7 %copy-start.10 = (f32[128]{0:T(128)S(1)}, f32[128]{0:T(128)}, u32[]{:S(2)}) copy-start(f32[128]{0:T(128)} %param.17) | copy-start | bytes 1540

commit v5 on v4

--- a/solution.py
+++ b/solution.py
@@ -145,11 +145,6 @@
     return jnp.transpose(jnp.broadcast_to(row, (count, row.shape[1])))
 
 
-def normed_rows(act):
-    centre = act - jnp.mean(act, axis=1, keepdims=True)
-    return centre * lax.rsqrt(jnp.mean(centre * centre, axis=1, keepdims=True) + EPSILON)
-
-
 def exchange_bit(first, second, weight):
     sublane = lax.broadcasted_iota(jnp.int32, first.shape, 1)
     low = sublane & weight == 0
@@ -197,7 +192,7 @@
 
 
 def edges_kernel(me_ref, *refs):
-    sources, (out_ref, *local), arrived = refs[:9], refs[9:19], refs[19]
+    sources, (out_ref, *local), (blocks, arrived, left) = refs[:9], refs[9:19], refs[19:]
     copies = [
         pltpu.make_async_copy(source, target, arrived.at[index])
         for index, (source, target) in enumerate(zip(sources, local))
@@ -209,19 +204,32 @@
     half = out_ref.shape[1] // 2
     for copy in copies[:3]:
         copy.wait()
-    normed = normed_rows(act_ref[...].reshape(own * cols, chan).astype(F32))
-    pair_norm = (normed * gain_ref[...] + bias_ref[...]).astype(BF16)
+    act = jnp.concatenate([jnp.transpose(act_ref[r].astype(F32)) for r in range(own)], axis=1)
+    gain = across(gain_ref[...], cols)
+    bias = across(bias_ref[...], cols)
+    centre = act - jnp.mean(act, axis=0, keepdims=True)
+    inverse = lax.rsqrt(jnp.mean(centre * centre, axis=0, keepdims=True) + EPSILON)
+    wide_gain, wide_bias = (jnp.concatenate([value] * own, axis=1) for value in (gain, bias))
+    pair_norm = (centre * inverse * wide_gain + wide_bias).astype(BF16)
     for copy in copies[3:]:
         copy.wait()
     valid = valid_ref[...].astype(F32)
     mask = jnp.concatenate(
         [valid * rows_ref[me_ref[0] * own + r].astype(F32) for r in range(own)], axis=1
     )
+    sent = []
     for side in range(2):
-        proj = dot(weights[2 * side][...], pair_norm, 0, 1)
-        edge = mask * jax.nn.sigmoid(dot(weights[2 * side + 1][...], pair_norm, 0, 1)) * proj
+        proj = dot(weights[2 * side][...], pair_norm, 0, 0)
+        edge = mask * jax.nn.sigmoid(dot(weights[2 * side + 1][...], pair_norm, 0, 0)) * proj
         parts = trade([edge[:, r * cols : (r + 1) * cols] for r in range(own)])
-        out_ref[:, side * half : (side + 1) * half, :] = merge_channels(parts, own).astype(BF16)
+        blocks[side] = merge_channels(parts, own).astype(BF16)
+        copy = pltpu.make_async_copy(
+            blocks.at[side], out_ref.at[:, side * half : (side + 1) * half, :], left.at[side]
+        )
+        copy.start()
+        sent.append(copy)
+    for copy in sent:
+        copy.wait()
 
 
 def gates_kernel(
@@ -345,7 +353,7 @@
 HBM = pl.BlockSpec(memory_space=pltpu.HBM)
 
 
-def call(kernel, name, outs, args, scratch=(), scalars=0, flops=0, spaces=None, limit=32 * 2**20):
+def call(kernel, name, outs, args, scratch=(), scalars=0, flops=0, spaces=None, to=VMEM, limit=32 * 2**20):
     shapes = [jax.ShapeDtypeStruct(shape, dtype) for shape, dtype in outs]
     moved = sum(value.size * value.dtype.itemsize for value in list(args) + shapes)
     result = pl.pallas_call(
@@ -353,7 +361,7 @@
         name=name,
         out_shape=shapes,
         in_specs=[SMEM] * scalars + (spaces or [VMEM] * (len(args) - scalars)),
-        out_specs=[VMEM] * len(outs),
+        out_specs=[to] * len(outs),
         scratch_shapes=scratch,
         cost_estimate=pl.CostEstimate(flops=flops, bytes_accessed=moved, transcendentals=0),
         compiler_params=pltpu.CompilerParams(vmem_limit_bytes=limit),
@@ -407,9 +415,11 @@
             (pltpu.SMEM if value is residue_mask else pltpu.VMEM)(value.shape, value.dtype)
             for value in first
         ]
-        + [pltpu.SemaphoreType.DMA((len(first),))],
+        + [pltpu.VMEM((2, dap, block, cols), BF16)]
+        + [pltpu.SemaphoreType.DMA((len(first),)), pltpu.SemaphoreType.DMA((2,))],
         scalars=1,
         flops=4 * product,
+        to=HBM,
         spaces=[HBM] * len(first),
         limit=None,
     )

time: 55.5 us -> 55.4 us (level)
  no operation moved by 1% of the time
where the time goes in v5:
time: 55.4 us; the launch traced here: 55.2 us
  blocking collectives  33 us (60%)
  waiting for transfers between devices  8.27 us (15%)
  starting transfers between devices  7.31 us (13%)
  Pallas kernels  5.79 us (10%)
  local copies, waits for them, and re-layouts  0.63 us (1%)
    all_to_all x3, blocking collectives, exchange(): lax.all_to_all(value, 'dap', split_axis=0, concat_axis=0, axis_index_grou...  33 us
    all_to_all x1, waiting for transfers between devices, exchange(): lax.all_to_all(value, 'dap', split_axis=0, concat_axis=0, axis_index_grou...  8.27 us
    all_to_all x1, starting transfers between devices, exchange(): lax.all_to_all(value, 'dap', split_axis=0, concat_axis=0, axis_index_grou...  7.31 us
    pallas_call x6, Pallas kernels, call(): pl.pallas_call(kernel, name=name, out_shape=shapes, in_specs=[SMEM] * sca...  5.79 us
  transfers between devices with their start and end apart: 1, of which 1 were waited for; matrix products, arithmetic and copies ran while one was open for 0% of the time, Pallas kernels for 2%

profile of v5, /device:TPU:0, one launch (start us, length us, event | category | flops | bytes accessed | tf_op | source)
XLA Modules:
  0.0 55.2 jit_solution(17143261347736165958)
XLA Ops:
  0.0 2.3 %edges.1 = bf16[32,32,128]{2,1,0:T(8,128)(2,1)} custom-call(s32[1]{0:T(128)} %bitcast.me_ref, bf16[4,128,128]{2,1,0:T(8,128)(2,1)} %act_ref.1, f32[1,128]{1,0:T(1,128)} %bitcast.8, f32[1,128]{1,0:T(1,128)} %bitcast.10, s32[128]{0:T(128)} %rows_ref.1, s32[1,128]{1,0:T(1,128)} %bitcast.6, bf16[128,128]{1,0:T(8,128)(2,1)} %wap.3, bf16[128,128]{1,0:T(8,128)(2,1)} %wag.3, ...), custom_call_target="tpu_custom_call" | custom-call | flops 67108864 | bytes 526340 | tf_op jit(solution)/shard_map/edges/pallas_call | solution.py:359
  2.3 0.0 copy-start
  2.3 0.0 copy-start.1
  2.3 0.0 copy-start.2
  2.3 0.0 copy-start.3
  2.3 0.0 copy-start.4
  2.4 0.0 copy-start.5
  2.4 0.0 copy-start.6
  2.4 0.0 copy-start.7
  2.4 0.0 copy-start.11
  2.4 0.0 copy-start.12
  2.4 7.3 %all-to-all-start = ((bf16[32,32,128]{2,1,0:T(8,128)(2,1)}), bf16[32,32,128]{2,1,0:T(8,128)(2,1)S(1)}, u32[]{:S(2)}, u32[]{:S(2)}) async-start(bf16[32,32,128]{2,1,0:T(8,128)(2,1)} %edges.1), calls=%async_computation | async-start | bytes 524288 | tf_op jit(solution)/shard_map/all_to_all | solution.py:404
  9.7 0.0 copy-start.8
  9.7 0.0 copy-start.9
  9.8 0.0 copy-start.10
  9.8 0.0 copy-done
  9.8 0.0 copy-done.1
  9.8 0.0 copy-done.2
  9.8 0.0 copy-done.3
  9.8 0.0 copy-done.4
  9.8 0.0 copy-done.5
  9.8 0.0 copy-done.6
  9.8 0.0 copy-done.7
  9.8 0.0 copy-done.11
  9.9 0.0 copy-done.12
  9.9 0.5 copy-done.8
  10.4 0.0 copy-done.9
  10.4 0.0 copy-done.10
  10.4 1.2 %gates.1 = (f32[4,128,512]{2,1,0:T(8,128)S(1)}, f32[128,512]{1,0:T(8,128)S(1)}, f32[1,512]{1,0:T(1,128)S(1)}, f32[128,128]{1,0:T(8,128)S(1)}, f32[512,128]{1,0:T...) custom-call(s32[1]{0:T(128)} %bitcast.me_ref, s32[128]{0:T(128)S(1)} %copy-done.8, ...), custom_call_target="tpu_custom_call" | custom-call | flops 100663296 | bytes 2495492 | tf_op jit(solution)/shard_map/gates/pallas_call | solution.py:359
  11.7 8.3 %all-to-all-done.in_ref = bf16[32,32,128]{2,1,0:T(8,128)(2,1)S(1)} async-done(((bf16[32,32,128]{2,1,0:T(8,128)(2,1)}), bf16[32,32,128]{2,1,0:T(8,128)(2,1)S(1)}, u32[]{:S(2)}, u32[]{:S(2)}) %all-to-all-start) | async-done | bytes 262176 | tf_op jit(solution)/shard_map/all_to_all | solution.py:404
  19.9 0.2 triangle.1
  20.2 10.9 %all_to_all.20.tri_ref = bf16[32,16,128]{2,1,0:T(8,128)(2,1)S(1)} all-to-all(bf16[32,16,128]{2,1,0:T(8,128)(2,1)S(1)} %get-tuple-element.19), channel_id=1, replica_groups={{0,8,16,24,1,9,17,25,2,10,18,26,3,11,19,27,4,12,20,28,5,13,21,29,6,14,2..., dimensions={0} | all-to-all | bytes 262144 | tf_op jit(solution)/shard_map/all_to_all | solution.py:404
  31.1 0.6 %norm.1 = (bf16[32,16,128]{2,1,0:T(8,128)(2,1)S(1)}, f32[128,512]{1,0:T(8,128)S(1)}) custom-call(bf16[32,16,128]{2,1,0:T(8,128)(2,1)S(1)} %all_to_all.20.tri_ref, f32[512,128]{1,0:T(8,128)S(1)} %get-tuple-element.18._.grad_ref, f32[128,512]{1,0:T(8,128)S(1)} %get-tuple-element.20.slope, f32[128,128]{1,0:T(8,128)S(1)} %get-tuple-element.21.gain, ...), custom_call_target="tpu_custom_call" | custom-call | flops 33554432 | bytes 1245184 | tf_op jit(solution)/shard_map/norm/pallas_call | solution.py:359
  31.7 10.1 %all_to_all.21.in_ref = bf16[32,16,128]{2,1,0:T(8,128)(2,1)S(1)} all-to-all(bf16[32,16,128]{2,1,0:T(8,128)(2,1)S(1)} %get-tuple-element.23), channel_id=1, replica_groups={{0,8,16,24,1,9,17,25,2,10,18,26,3,11,19,27,4,12,20,28,5,13,21,29,6,14,2..., dimensions={0} | all-to-all | bytes 262144 | tf_op jit(solution)/shard_map/all_to_all | solution.py:404
  41.9 0.2 edge_grad.1
  42.1 11.9 %all_to_all.22.in_ref = bf16[32,32,128]{2,1,0:T(8,128)(2,1)S(1)} all-to-all(bf16[32,32,128]{2,1,0:T(8,128)(2,1)S(1)} %edge_grad.1), channel_id=1, replica_groups={{0,8,16,24,1,9,17,25,2,10,18,26,3,11,19,27,4,12,20,28,5,13,21,29,6,14,2..., dimensions={0} | all-to-all | bytes 524288 | tf_op jit(solution)/shard_map/all_to_all | solution.py:404
  54.0 1.2 %input_grad.1 = bf16[4,128,128]{2,1,0:T(8,128)(2,1)} custom-call(bf16[32,32,128]{2,1,0:T(8,128)(2,1)S(1)} %all_to_all.22.in_ref, f32[4,128,512]{2,1,0:T(8,128)S(1)} %get-tuple-element.26.factors, f32[128,512]{1,0:T(8,128)S(1)} %get-tuple-element.27.normed_t, f32[1,512]{1,0:T(1,128)S(1)} %get-tuple-element.28.rstd_t, ...), custom_call_target="tpu_custom_call" | custom-call | flops 67108864 | bytes 2164736 | tf_op jit(solution)/shard_map/input_grad/pallas_call | solution.py:359
Async XLA Ops:
  2.3 7.5 %copy-start = (bf16[4,128,128]{2,1,0:T(8,128)(2,1)S(1)}, bf16[4,128,128]{2,1,0:T(8,128)(2,1)}, u32[]{:S(2)}) copy-start(bf16[4,128,128]{2,1,0:T(8,128)(2,1)} %act_ref.1) | copy-start | bytes 393220
  2.3 7.5 %copy-start.1 = (bf16[128,128]{1,0:T(8,128)(2,1)S(1)}, bf16[128,128]{1,0:T(8,128)(2,1)}, u32[]{:S(2)}) copy-start(bf16[128,128]{1,0:T(8,128)(2,1)} %wap.3) | copy-start | bytes 98308
  2.3 7.5 %copy-start.2 = (bf16[128,128]{1,0:T(8,128)(2,1)S(1)}, bf16[128,128]{1,0:T(8,128)(2,1)}, u32[]{:S(2)}) copy-start(bf16[128,128]{1,0:T(8,128)(2,1)} %wag.3) | copy-start | bytes 98308
  2.3 7.5 %copy-start.3 = (bf16[128,128]{1,0:T(8,128)(2,1)S(1)}, bf16[128,128]{1,0:T(8,128)(2,1)}, u32[]{:S(2)}) copy-start(bf16[128,128]{1,0:T(8,128)(2,1)} %wbp.3) | copy-start | bytes 98308
  2.3 7.5 %copy-start.4 = (bf16[128,128]{1,0:T(8,128)(2,1)S(1)}, bf16[128,128]{1,0:T(8,128)(2,1)}, u32[]{:S(2)}) copy-start(bf16[128,128]{1,0:T(8,128)(2,1)} %wbg.3) | copy-start | bytes 98308
  2.4 7.5 %copy-start.5 = (bf16[4,128,128]{2,1,0:T(8,128)(2,1)S(1)}, bf16[4,128,128]{2,1,0:T(8,128)(2,1)}, u32[]{:S(2)}) copy-start(bf16[4,128,128]{2,1,0:T(8,128)(2,1)} %grad_ref.1) | copy-start | bytes 393220
  2.4 7.5 %copy-start.6 = (bf16[128,128]{1,0:T(8,128)(2,1)S(1)}, bf16[128,128]{1,0:T(8,128)(2,1)}, u32[]{:S(2)}) copy-start(bf16[128,128]{1,0:T(8,128)(2,1)} %w_gate.3) | copy-start | bytes 98308
  2.4 7.5 %copy-start.7 = (bf16[128,128]{1,0:T(8,128)(2,1)S(1)}, bf16[128,128]{1,0:T(8,128)(2,1)}, u32[]{:S(2)}) copy-start(bf16[128,128]{1,0:T(8,128)(2,1)} %w_out.3) | copy-start | bytes 98308
  2.4 7.5 %copy-start.11 = (f32[128]{0:T(128)S(1)}, f32[128]{0:T(128)}, u32[]{:S(2)}) copy-start(f32[128]{0:T(128)} %param.23) | copy-start | bytes 1540
  2.4 7.5 %copy-start.12 = (f32[128]{0:T(128)S(1)}, f32[128]{0:T(128)}, u32[]{:S(2)}) copy-start(f32[128]{0:T(128)} %param.24) | copy-start | bytes 1540
  2.4 17.5 %all-to-all-start = ((bf16[32,32,128]{2,1,0:T(8,128)(2,1)}), bf16[32,32,128]{2,1,0:T(8,128)(2,1)S(1)}, u32[]{:S(2)}, u32[]{:S(2)}) async-start(bf16[32,32,128]{2,1,0:T(8,128)(2,1)} %edges.1), calls=%async_computation | async-start | bytes 524288 | tf_op jit(solution)/shard_map/all_to_all | solution.py:404
  9.7 0.7 %copy-start.8 = (s32[128]{0:T(128)S(1)}, s32[128]{0:T(128)}, u32[]{:S(2)}) copy-start(s32[128]{0:T(128)} %rows_ref.1) | copy-start | bytes 1540
  9.7 0.7 %copy-start.9 = (f32[128]{0:T(128)S(1)}, f32[128]{0:T(128)}, u32[]{:S(2)}) copy-start(f32[128]{0:T(128)} %param.16) | copy-start | bytes 1540
  9.8 0.7 %copy-start.10 = (f32[128]{0:T(128)S(1)}, f32[128]{0:T(128)}, u32[]{:S(2)}) copy-start(f32[128]{0:T(128)} %param.17) | copy-start | bytes 1540

commit v6 on v5

--- a/solution.py
+++ b/solution.py
@@ -235,7 +235,7 @@
 def gates_kernel(
     me_ref, rows_ref, valid_ref, act_ref, grad_ref, gain_ref, bias_ref, gain_out_ref, bias_out_ref,
     wap, wag, wbp, wbg, w_gate, w_out,
-    factors, normed_t, rstd_t, gain_t, d_normed, slope, gain_out_t, bias_out_t,
+    factors, normed_t, rstd_t, gain_t, d_normed, slope, gain_out_t, bias_out_t, w_out_t,
 ):
     own, cols, _ = act_ref.shape
     hidden = wap.shape[1]
@@ -245,6 +245,7 @@
     gain_out = across(gain_out_ref[...], cols)
     gain_t[...] = gain
     gain_out_t[...] = gain_out
+    w_out_t[...] = jnp.transpose(w_out[...].astype(F32)).astype(BF16)
     bias_out_t[...] = across(bias_out_ref[...], cols)
     for r in range(own):
         act = jnp.transpose(act_ref[r].astype(F32))
@@ -302,9 +303,9 @@
     return centre * inverse, inverse
 
 
-def norm_kernel(own, tri_ref, grad_ref, slope, gain, bias, w_out, w_gate, out_ref, part_ref):
+def norm_kernel(own, tri_ref, grad_ref, slope, gain, bias, w_out_t, w_gate, out_ref, part_ref):
     devices, block, cols = tri_ref.shape
-    hidden = w_out.shape[0]
+    hidden = w_out_t.shape[1]
     normed, inverse = tri_normed(tri_ref, hidden, own)
     grad = grad_ref[...].reshape(normed.shape)
     mean_grad = fold(grad, own) / hidden
@@ -313,7 +314,7 @@
     out_ref[...] = d_tri.reshape(devices, block, cols).astype(BF16)
     parts = trade(split_channels(normed.reshape(devices, block, cols), own))
     tri_norm = jnp.concatenate([(part * gain[...] + bias[...]).astype(BF16) for part in parts], axis=1)
-    d_gate = (slope[...] * dot(w_out[...], tri_norm, 0, 0)).astype(BF16)
+    d_gate = (slope[...] * dot(w_out_t[...], tri_norm, 1, 0)).astype(BF16)
     part_ref[...] = dot(w_gate[...], d_gate, 1, 0)
 
 
@@ -330,22 +331,33 @@
         )
 
 
-def input_grad_kernel(in_ref, factors, normed_t, rstd_t, gain_t, gate_part, wap, wag, wbp, wbg, out_ref):
+def input_grad_kernel(
+    in_ref, factors, normed_t, rstd_t, gain_t, gate_part, wap, wag, wbp, wbg, out_ref, done, left
+):
     own, cols, _ = out_ref.shape
     half = in_ref.shape[1] // 2
-    total = gate_part[...]
-    for side, weights in enumerate(((wap, wag), (wbp, wbg))):
-        blocks = in_ref[:, side * half : (side + 1) * half, :].astype(F32)
-        d_edge = jnp.concatenate(trade(split_channels(blocks, own)), axis=1)
-        for at, weight in enumerate(weights):
-            total = total + dot(weight[...], (d_edge * factors[2 * side + at]).astype(BF16), 1, 0)
-    grad_hat = total * jnp.concatenate([gain_t[...]] * own, axis=1)
-    normed = normed_t[...]
-    mean_grad = jnp.mean(grad_hat, axis=0, keepdims=True)
-    mean_proj = jnp.mean(grad_hat * normed, axis=0, keepdims=True)
-    grad = rstd_t[...] * (grad_hat - mean_grad - normed * mean_proj)
+    sides = [
+        trade(split_channels(in_ref[:, side * half : (side + 1) * half, :].astype(F32), own))
+        for side in range(2)
+    ]
+    copies = []
     for r in range(own):
-        out_ref[r] = jnp.transpose(grad[:, r * cols : (r + 1) * cols]).astype(BF16)
+        lanes = pl.ds(r * cols, cols)
+        total = gate_part[:, lanes]
+        for index, weight in enumerate((wap, wag, wbp, wbg)):
+            d_in = (sides[index // 2][r] * factors[index, :, lanes]).astype(BF16)
+            total = total + dot(weight[...], d_in, 1, 0)
+        grad_hat = total * gain_t[...]
+        normed = normed_t[:, lanes]
+        mean_grad = jnp.mean(grad_hat, axis=0, keepdims=True)
+        mean_proj = jnp.mean(grad_hat * normed, axis=0, keepdims=True)
+        grad = rstd_t[:, lanes] * (grad_hat - mean_grad - normed * mean_proj)
+        done[r] = jnp.transpose(grad).astype(BF16)
+        copy = pltpu.make_async_copy(done.at[r], out_ref.at[r], left.at[r])
+        copy.start()
+        copies.append(copy)
+    for copy in copies:
+        copy.wait()
 
 
 VMEM = pl.BlockSpec(memory_space=pltpu.VMEM)
@@ -424,7 +436,7 @@
         limit=None,
     )
     edges = exchange(edges)
-    factors, normed_t, rstd_t, gain_t, d_normed, slope, gain_out_t, bias_out_t = call(
+    factors, normed_t, rstd_t, gain_t, d_normed, slope, gain_out_t, bias_out_t, w_out_t = call(
         gates_kernel,
         "gates",
         [
@@ -436,6 +448,7 @@
             ((chan, own * cols), F32),
             ((hidden, cols), F32),
             ((hidden, cols), F32),
+            ((chan, hidden), BF16),
         ],
         (me, residue_mask, valid, pair_act, out_grad, gain_in, bias_in, gain_out)
         + (bias_out, *w_edges, w_gate, w_out),
@@ -459,7 +472,7 @@
         functools.partial(norm_kernel, own),
         "norm",
         [((dap, block, cols), BF16), ((chan, own * cols), F32)],
-        (tri, d_normed, slope, gain_out_t, bias_out_t, w_out, w_gate),
+        (tri, d_normed, slope, gain_out_t, bias_out_t, w_out_t, w_gate),
         flops=2 * product,
     )
     d_tri = exchange(d_tri)
@@ -476,7 +489,9 @@
         "input_grad",
         [((own, cols, chan), BF16)],
         (d_edges, factors, normed_t, rstd_t, gain_t, gate_part, *w_edges),
+        scratch=[pltpu.VMEM((own, cols, chan), BF16), pltpu.SemaphoreType.DMA((own,))],
         flops=4 * product,
+        to=HBM,
     )
 
 

time: 55.4 us -> 55.5 us (level)
  no operation moved by 1% of the time
where the time goes in v6:
time: 55.5 us; the launch traced here: 55.2 us
  blocking collectives  33 us (59%)
  waiting for transfers between devices  8.27 us (15%)
  starting transfers between devices  7.31 us (13%)
  Pallas kernels  5.83 us (11%)
  local copies, waits for them, and re-layouts  0.63 us (1%)
    all_to_all x3, blocking collectives, exchange(): lax.all_to_all(value, 'dap', split_axis=0, concat_axis=0, axis_index_grou...  33 us
    all_to_all x1, waiting for transfers between devices, exchange(): lax.all_to_all(value, 'dap', split_axis=0, concat_axis=0, axis_index_grou...  8.27 us
    all_to_all x1, starting transfers between devices, exchange(): lax.all_to_all(value, 'dap', split_axis=0, concat_axis=0, axis_index_grou...  7.31 us
    pallas_call x6, Pallas kernels, call(): pl.pallas_call(kernel, name=name, out_shape=shapes, in_specs=[SMEM] * sca...  5.83 us
  transfers between devices with their start and end apart: 1, of which 1 were waited for; matrix products, arithmetic and copies ran while one was open for 0% of the time, Pallas kernels for 2%

profile of v6, /device:TPU:0, one launch (start us, length us, event | category | flops | bytes accessed | tf_op | source)
XLA Modules:
  0.0 55.2 jit_solution(3246965418651987277)
XLA Ops:
  0.0 2.3 %edges.1 = bf16[32,32,128]{2,1,0:T(8,128)(2,1)} custom-call(s32[1]{0:T(128)} %bitcast.me_ref, bf16[4,128,128]{2,1,0:T(8,128)(2,1)} %act_ref.1, f32[1,128]{1,0:T(1,128)} %bitcast.8, f32[1,128]{1,0:T(1,128)} %bitcast.10, s32[128]{0:T(128)} %rows_ref.1, s32[1,128]{1,0:T(1,128)} %bitcast.6, bf16[128,128]{1,0:T(8,128)(2,1)} %wap.3, bf16[128,128]{1,0:T(8,128)(2,1)} %wag.3, ...), custom_call_target="tpu_custom_call" | custom-call | flops 67108864 | bytes 526340 | tf_op jit(solution)/shard_map/edges/pallas_call | solution.py:371
  2.3 0.0 copy-start
  2.3 0.0 copy-start.1
  2.3 0.0 copy-start.2
  2.3 0.0 copy-start.3
  2.3 0.0 copy-start.4
  2.4 0.0 copy-start.5
  2.4 0.0 copy-start.6
  2.4 0.0 copy-start.7
  2.4 0.0 copy-start.11
  2.4 0.0 copy-start.12
  2.4 7.3 %all-to-all-start = ((bf16[32,32,128]{2,1,0:T(8,128)(2,1)}), bf16[32,32,128]{2,1,0:T(8,128)(2,1)S(1)}, u32[]{:S(2)}, u32[]{:S(2)}) async-start(bf16[32,32,128]{2,1,0:T(8,128)(2,1)} %edges.1), calls=%async_computation | async-start | bytes 524288 | tf_op jit(solution)/shard_map/all_to_all | solution.py:416
  9.7 0.0 copy-start.8
  9.7 0.0 copy-start.9
  9.8 0.0 copy-start.10
  9.8 0.0 copy-done
  9.8 0.0 copy-done.1
  9.8 0.0 copy-done.2
  9.8 0.0 copy-done.3
  9.8 0.0 copy-done.4
  9.8 0.0 copy-done.5
  9.8 0.0 copy-done.6
  9.8 0.0 copy-done.7
  9.8 0.0 copy-done.11
  9.9 0.0 copy-done.12
  9.9 0.5 copy-done.8
  10.4 0.0 copy-done.9
  10.4 0.0 copy-done.10
  10.4 1.2 %gates.1 = (f32[4,128,512]{2,1,0:T(8,128)S(1)}, f32[128,512]{1,0:T(8,128)S(1)}, f32[1,512]{1,0:T(1,128)S(1)}, f32[128,128]{1,0:T(8,128)S(1)}, f32[512,128]{1,0:T...) custom-call(s32[1]{0:T(128)} %bitcast.me_ref, ...), custom_call_target="tpu_custom_call" | custom-call | flops 100663296 | bytes 2528260 | tf_op jit(solution)/shard_map/gates/pallas_call | solution.py:371
  11.7 8.3 %all-to-all-done.in_ref = bf16[32,32,128]{2,1,0:T(8,128)(2,1)S(1)} async-done(((bf16[32,32,128]{2,1,0:T(8,128)(2,1)}), bf16[32,32,128]{2,1,0:T(8,128)(2,1)S(1)}, u32[]{:S(2)}, u32[]{:S(2)}) %all-to-all-start) | async-done | bytes 262176 | tf_op jit(solution)/shard_map/all_to_all | solution.py:416
  19.9 0.2 triangle.1
  20.2 10.9 %all_to_all.20.tri_ref = bf16[32,16,128]{2,1,0:T(8,128)(2,1)S(1)} all-to-all(bf16[32,16,128]{2,1,0:T(8,128)(2,1)S(1)} %get-tuple-element.20), channel_id=1, replica_groups={{0,8,16,24,1,9,17,25,2,10,18,26,3,11,19,27,4,12,20,28,5,13,21,29,6,14,2..., dimensions={0} | all-to-all | bytes 262144 | tf_op jit(solution)/shard_map/all_to_all | solution.py:416
  31.1 0.6 %norm.1 = (bf16[32,16,128]{2,1,0:T(8,128)(2,1)S(1)}, f32[128,512]{1,0:T(8,128)S(1)}) custom-call(bf16[32,16,128]{2,1,0:T(8,128)(2,1)S(1)} %all_to_all.20.tri_ref, f32[512,128]{1,0:T(8,128)S(1)} %get-tuple-element.19._.grad_ref, f32[128,512]{1,0:T(8,128)S(1)} %get-tuple-element.21.slope, f32[128,128]{1,0:T(8,128)S(1)} %get-tuple-element.22.gain, ...), custom_call_target="tpu_custom_call" | custom-call | flops 33554432 | bytes 1245184 | tf_op jit(solution)/shard_map/norm/pallas_call | solution.py:371
  31.7 10.1 %all_to_all.21.in_ref = bf16[32,16,128]{2,1,0:T(8,128)(2,1)S(1)} all-to-all(bf16[32,16,128]{2,1,0:T(8,128)(2,1)S(1)} %get-tuple-element.25), channel_id=1, replica_groups={{0,8,16,24,1,9,17,25,2,10,18,26,3,11,19,27,4,12,20,28,5,13,21,29,6,14,2..., dimensions={0} | all-to-all | bytes 262144 | tf_op jit(solution)/shard_map/all_to_all | solution.py:416
  41.8 0.2 edge_grad.1
  42.1 11.9 %all_to_all.22.in_ref = bf16[32,32,128]{2,1,0:T(8,128)(2,1)S(1)} all-to-all(bf16[32,32,128]{2,1,0:T(8,128)(2,1)S(1)} %edge_grad.1), channel_id=1, replica_groups={{0,8,16,24,1,9,17,25,2,10,18,26,3,11,19,27,4,12,20,28,5,13,21,29,6,14,2..., dimensions={0} | all-to-all | bytes 524288 | tf_op jit(solution)/shard_map/all_to_all | solution.py:416
  54.0 1.2 %input_grad.1 = bf16[4,128,128]{2,1,0:T(8,128)(2,1)} custom-call(bf16[32,32,128]{2,1,0:T(8,128)(2,1)S(1)} %all_to_all.22.in_ref, f32[4,128,512]{2,1,0:T(8,128)S(1)} %get-tuple-element.28.factors, f32[128,512]{1,0:T(8,128)S(1)} %get-tuple-element.29.normed_t, f32[1,512]{1,0:T(1,128)S(1)} %get-tuple-element.30.rstd_t, ...), custom_call_target="tpu_custom_call" | custom-call | flops 67108864 | bytes 2164736 | tf_op jit(solution)/shard_map/input_grad/pallas_call | solution.py:371
Async XLA Ops:
  2.3 7.5 %copy-start = (bf16[4,128,128]{2,1,0:T(8,128)(2,1)S(1)}, bf16[4,128,128]{2,1,0:T(8,128)(2,1)}, u32[]{:S(2)}) copy-start(bf16[4,128,128]{2,1,0:T(8,128)(2,1)} %act_ref.1) | copy-start | bytes 393220
  2.3 7.5 %copy-start.1 = (bf16[128,128]{1,0:T(8,128)(2,1)S(1)}, bf16[128,128]{1,0:T(8,128)(2,1)}, u32[]{:S(2)}) copy-start(bf16[128,128]{1,0:T(8,128)(2,1)} %wap.3) | copy-start | bytes 98308
  2.3 7.5 %copy-start.2 = (bf16[128,128]{1,0:T(8,128)(2,1)S(1)}, bf16[128,128]{1,0:T(8,128)(2,1)}, u32[]{:S(2)}) copy-start(bf16[128,128]{1,0:T(8,128)(2,1)} %wag.3) | copy-start | bytes 98308
  2.3 7.5 %copy-start.3 = (bf16[128,128]{1,0:T(8,128)(2,1)S(1)}, bf16[128,128]{1,0:T(8,128)(2,1)}, u32[]{:S(2)}) copy-start(bf16[128,128]{1,0:T(8,128)(2,1)} %wbp.3) | copy-start | bytes 98308
  2.3 7.5 %copy-start.4 = (bf16[128,128]{1,0:T(8,128)(2,1)S(1)}, bf16[128,128]{1,0:T(8,128)(2,1)}, u32[]{:S(2)}) copy-start(bf16[128,128]{1,0:T(8,128)(2,1)} %wbg.3) | copy-start | bytes 98308
  2.4 7.5 %copy-start.5 = (bf16[4,128,128]{2,1,0:T(8,128)(2,1)S(1)}, bf16[4,128,128]{2,1,0:T(8,128)(2,1)}, u32[]{:S(2)}) copy-start(bf16[4,128,128]{2,1,0:T(8,128)(2,1)} %grad_ref.1) | copy-start | bytes 393220
  2.4 7.5 %copy-start.6 = (bf16[128,128]{1,0:T(8,128)(2,1)S(1)}, bf16[128,128]{1,0:T(8,128)(2,1)}, u32[]{:S(2)}) copy-start(bf16[128,128]{1,0:T(8,128)(2,1)} %w_gate.3) | copy-start | bytes 98308
  2.4 7.5 %copy-start.7 = (bf16[128,128]{1,0:T(8,128)(2,1)S(1)}, bf16[128,128]{1,0:T(8,128)(2,1)}, u32[]{:S(2)}) copy-start(bf16[128,128]{1,0:T(8,128)(2,1)} %w_out.1) | copy-start | bytes 98308
  2.4 7.5 %copy-start.11 = (f32[128]{0:T(128)S(1)}, f32[128]{0:T(128)}, u32[]{:S(2)}) copy-start(f32[128]{0:T(128)} %param.23) | copy-start | bytes 1540
  2.4 7.5 %copy-start.12 = (f32[128]{0:T(128)S(1)}, f32[128]{0:T(128)}, u32[]{:S(2)}) copy-start(f32[128]{0:T(128)} %param.24) | copy-start | bytes 1540
  2.4 17.5 %all-to-all-start = ((bf16[32,32,128]{2,1,0:T(8,128)(2,1)}), bf16[32,32,128]{2,1,0:T(8,128)(2,1)S(1)}, u32[]{:S(2)}, u32[]{:S(2)}) async-start(bf16[32,32,128]{2,1,0:T(8,128)(2,1)} %edges.1), calls=%async_computation | async-start | bytes 524288 | tf_op jit(solution)/shard_map/all_to_all | solution.py:416
  9.7 0.7 %copy-start.8 = (s32[128]{0:T(128)S(1)}, s32[128]{0:T(128)}, u32[]{:S(2)}) copy-start(s32[128]{0:T(128)} %rows_ref.1) | copy-start | bytes 1540
  9.7 0.7 %copy-start.9 = (f32[128]{0:T(128)S(1)}, f32[128]{0:T(128)}, u32[]{:S(2)}) copy-start(f32[128]{0:T(128)} %param.16) | copy-start | bytes 1540
  9.8 0.7 %copy-start.10 = (f32[128]{0:T(128)S(1)}, f32[128]{0:T(128)}, u32[]{:S(2)}) copy-start(f32[128]{0:T(128)} %param.17) | copy-start | bytes 1540

commit v7 on v5

--- a/solution.py
+++ b/solution.py
@@ -302,7 +302,7 @@
     return centre * inverse, inverse
 
 
-def norm_kernel(own, tri_ref, grad_ref, slope, gain, bias, w_out, w_gate, out_ref, part_ref):
+def norm_kernel(own, tri_ref, grad_ref, slope, gain, bias, w_out, out_ref, gate_ref):
     devices, block, cols = tri_ref.shape
     hidden = w_out.shape[0]
     normed, inverse = tri_normed(tri_ref, hidden, own)
@@ -313,8 +313,7 @@
     out_ref[...] = d_tri.reshape(devices, block, cols).astype(BF16)
     parts = trade(split_channels(normed.reshape(devices, block, cols), own))
     tri_norm = jnp.concatenate([(part * gain[...] + bias[...]).astype(BF16) for part in parts], axis=1)
-    d_gate = (slope[...] * dot(w_out[...], tri_norm, 0, 0)).astype(BF16)
-    part_ref[...] = dot(w_gate[...], d_gate, 1, 0)
+    gate_ref[...] = (slope[...] * dot(w_out[...], tri_norm, 0, 0)).astype(BF16)
 
 
 def edge_grad_kernel(own, in_ref, a_ref, b_ref, out_ref):
@@ -330,15 +329,20 @@
         )
 
 
-def input_grad_kernel(in_ref, factors, normed_t, rstd_t, gain_t, gate_part, wap, wag, wbp, wbg, out_ref):
+def input_grad_kernel(
+    in_ref, factors, normed_t, rstd_t, gain_t, d_gate, wap, wag, wbp, wbg, w_gate, out_ref
+):
     own, cols, _ = out_ref.shape
     half = in_ref.shape[1] // 2
-    total = gate_part[...]
-    for side, weights in enumerate(((wap, wag), (wbp, wbg))):
+    grads = []
+    for side in range(2):
         blocks = in_ref[:, side * half : (side + 1) * half, :].astype(F32)
         d_edge = jnp.concatenate(trade(split_channels(blocks, own)), axis=1)
-        for at, weight in enumerate(weights):
-            total = total + dot(weight[...], (d_edge * factors[2 * side + at]).astype(BF16), 1, 0)
+        for at in range(2):
+            grads.append((d_edge * factors[2 * side + at]).astype(BF16))
+    weights = [weight[...] for weight in (wap, wag, wbp, wbg, w_gate)]
+    grads.append(d_gate[...])
+    total = dot(jnp.concatenate(weights, axis=1), jnp.concatenate(grads, axis=0), 1, 0)
     grad_hat = total * jnp.concatenate([gain_t[...]] * own, axis=1)
     normed = normed_t[...]
     mean_grad = jnp.mean(grad_hat, axis=0, keepdims=True)
@@ -455,11 +459,11 @@
         spaces=[VMEM, pl.BlockSpec(memory_space=pl.ANY)],
     )
     tri = exchange(tri)
-    d_tri, gate_part = call(
+    d_tri, d_gate = call(
         functools.partial(norm_kernel, own),
         "norm",
-        [((dap, block, cols), BF16), ((chan, own * cols), F32)],
-        (tri, d_normed, slope, gain_out_t, bias_out_t, w_out, w_gate),
+        [((dap, block, cols), BF16), ((chan, own * cols), BF16)],
+        (tri, d_normed, slope, gain_out_t, bias_out_t, w_out),
         flops=2 * product,
     )
     d_tri = exchange(d_tri)
@@ -475,7 +479,7 @@
         input_grad_kernel,
         "input_grad",
         [((own, cols, chan), BF16)],
-        (d_edges, factors, normed_t, rstd_t, gain_t, gate_part, *w_edges),
+        (d_edges, factors, normed_t, rstd_t, gain_t, d_gate, *w_edges, w_gate),
         flops=4 * product,
     )
 

time: 55.4 us -> 55.3 us (level)
  no operation moved by 1% of the time
where the time goes in v7:
time: 55.3 us; the launch traced here: 55 us
  blocking collectives  33 us (60%)
  waiting for transfers between devices  8.27 us (15%)
  starting transfers between devices  7.31 us (13%)
  Pallas kernels  5.65 us (10%)
  local copies, waits for them, and re-layouts  0.63 us (1%)
    all_to_all x3, blocking collectives, exchange(): lax.all_to_all(value, 'dap', split_axis=0, concat_axis=0, axis_index_grou...  33 us
    all_to_all x1, waiting for transfers between devices, exchange(): lax.all_to_all(value, 'dap', split_axis=0, concat_axis=0, axis_index_grou...  8.27 us
    all_to_all x1, starting transfers between devices, exchange(): lax.all_to_all(value, 'dap', split_axis=0, concat_axis=0, axis_index_grou...  7.31 us
    pallas_call x6, Pallas kernels, call(): pl.pallas_call(kernel, name=name, out_shape=shapes, in_specs=[SMEM] * sca...  5.65 us
  transfers between devices with their start and end apart: 1, of which 1 were waited for; matrix products, arithmetic and copies ran while one was open for 0% of the time, Pallas kernels for 2%

profile of v7, /device:TPU:0, one launch (start us, length us, event | category | flops | bytes accessed | tf_op | source)
XLA Modules:
  0.0 55.0 jit_solution(3551522562355719820)
XLA Ops:
  0.0 2.3 %edges.1 = bf16[32,32,128]{2,1,0:T(8,128)(2,1)} custom-call(s32[1]{0:T(128)} %bitcast.me_ref, bf16[4,128,128]{2,1,0:T(8,128)(2,1)} %act_ref.1, f32[1,128]{1,0:T(1,128)} %bitcast.8, f32[1,128]{1,0:T(1,128)} %bitcast.10, s32[128]{0:T(128)} %rows_ref.1, s32[1,128]{1,0:T(1,128)} %bitcast.6, bf16[128,128]{1,0:T(8,128)(2,1)} %wap.3, bf16[128,128]{1,0:T(8,128)(2,1)} %wag.3, ...), custom_call_target="tpu_custom_call" | custom-call | flops 67108864 | bytes 526340 | tf_op jit(solution)/shard_map/edges/pallas_call | solution.py:363
  2.3 0.0 copy-start
  2.3 0.0 copy-start.1
  2.3 0.0 copy-start.2
  2.3 0.0 copy-start.3
  2.3 0.0 copy-start.4
  2.4 0.0 copy-start.5
  2.4 0.0 copy-start.6
  2.4 0.0 copy-start.7
  2.4 0.0 copy-start.11
  2.4 0.0 copy-start.12
  2.4 7.3 %all-to-all-start = ((bf16[32,32,128]{2,1,0:T(8,128)(2,1)}), bf16[32,32,128]{2,1,0:T(8,128)(2,1)S(1)}, u32[]{:S(2)}, u32[]{:S(2)}) async-start(bf16[32,32,128]{2,1,0:T(8,128)(2,1)} %edges.1), calls=%async_computation | async-start | bytes 524288 | tf_op jit(solution)/shard_map/all_to_all | solution.py:408
  9.7 0.0 copy-start.8
  9.7 0.0 copy-start.9
  9.8 0.0 copy-start.10
  9.8 0.0 copy-done
  9.8 0.0 copy-done.1
  9.8 0.0 copy-done.2
  9.8 0.0 copy-done.3
  9.8 0.0 copy-done.4
  9.8 0.0 copy-done.5
  9.8 0.0 copy-done.6
  9.8 0.0 copy-done.7
  9.8 0.0 copy-done.11
  9.9 0.0 copy-done.12
  9.9 0.5 copy-done.8
  10.4 0.0 copy-done.9
  10.4 0.0 copy-done.10
  10.4 1.2 %gates.1 = (f32[4,128,512]{2,1,0:T(8,128)S(1)}, f32[128,512]{1,0:T(8,128)S(1)}, f32[1,512]{1,0:T(1,128)S(1)}, f32[128,128]{1,0:T(8,128)S(1)}, f32[512,128]{1,0:T...) custom-call(s32[1]{0:T(128)} %bitcast.me_ref, s32[128]{0:T(128)S(1)} %copy-done.8, ...), custom_call_target="tpu_custom_call" | custom-call | flops 100663296 | bytes 2495492 | tf_op jit(solution)/shard_map/gates/pallas_call | solution.py:363
  11.7 8.3 %all-to-all-done.in_ref = bf16[32,32,128]{2,1,0:T(8,128)(2,1)S(1)} async-done(((bf16[32,32,128]{2,1,0:T(8,128)(2,1)}), bf16[32,32,128]{2,1,0:T(8,128)(2,1)S(1)}, u32[]{:S(2)}, u32[]{:S(2)}) %all-to-all-start) | async-done | bytes 262176 | tf_op jit(solution)/shard_map/all_to_all | solution.py:408
  19.9 0.2 triangle.1
  20.2 10.9 %all_to_all.20.tri_ref = bf16[32,16,128]{2,1,0:T(8,128)(2,1)S(1)} all-to-all(bf16[32,16,128]{2,1,0:T(8,128)(2,1)S(1)} %get-tuple-element.19), channel_id=1, replica_groups={{0,8,16,24,1,9,17,25,2,10,18,26,3,11,19,27,4,12,20,28,5,13,21,29,6,14,2..., dimensions={0} | all-to-all | bytes 262144 | tf_op jit(solution)/shard_map/all_to_all | solution.py:408
  31.1 0.5 norm.1
  31.6 10.1 %all_to_all.21.in_ref = bf16[32,16,128]{2,1,0:T(8,128)(2,1)S(1)} all-to-all(bf16[32,16,128]{2,1,0:T(8,128)(2,1)S(1)} %get-tuple-element.23), channel_id=1, replica_groups={{0,8,16,24,1,9,17,25,2,10,18,26,3,11,19,27,4,12,20,28,5,13,21,29,6,14,2..., dimensions={0} | all-to-all | bytes 262144 | tf_op jit(solution)/shard_map/all_to_all | solution.py:408
  41.7 0.2 edge_grad.1
  42.0 11.9 %all_to_all.22.in_ref = bf16[32,32,128]{2,1,0:T(8,128)(2,1)S(1)} all-to-all(bf16[32,32,128]{2,1,0:T(8,128)(2,1)S(1)} %edge_grad.1), channel_id=1, replica_groups={{0,8,16,24,1,9,17,25,2,10,18,26,3,11,19,27,4,12,20,28,5,13,21,29,6,14,2..., dimensions={0} | all-to-all | bytes 524288 | tf_op jit(solution)/shard_map/all_to_all | solution.py:408
  53.9 1.2 %input_grad.1 = bf16[4,128,128]{2,1,0:T(8,128)(2,1)} custom-call(bf16[32,32,128]{2,1,0:T(8,128)(2,1)S(1)} %all_to_all.22.in_ref, f32[4,128,512]{2,1,0:T(8,128)S(1)} %get-tuple-element.26.factors, f32[128,512]{1,0:T(8,128)S(1)} %get-tuple-element.27.normed_t, f32[1,512]{1,0:T(1,128)S(1)} %get-tuple-element.28.rstd_t, ...), custom_call_target="tpu_custom_call" | custom-call | flops 67108864 | bytes 2066432 | tf_op jit(solution)/shard_map/input_grad/pallas_call | solution.py:363
Async XLA Ops:
  2.3 7.5 %copy-start = (bf16[4,128,128]{2,1,0:T(8,128)(2,1)S(1)}, bf16[4,128,128]{2,1,0:T(8,128)(2,1)}, u32[]{:S(2)}) copy-start(bf16[4,128,128]{2,1,0:T(8,128)(2,1)} %act_ref.1) | copy-start | bytes 393220
  2.3 7.5 %copy-start.1 = (bf16[128,128]{1,0:T(8,128)(2,1)S(1)}, bf16[128,128]{1,0:T(8,128)(2,1)}, u32[]{:S(2)}) copy-start(bf16[128,128]{1,0:T(8,128)(2,1)} %wap.3) | copy-start | bytes 98308
  2.3 7.5 %copy-start.2 = (bf16[128,128]{1,0:T(8,128)(2,1)S(1)}, bf16[128,128]{1,0:T(8,128)(2,1)}, u32[]{:S(2)}) copy-start(bf16[128,128]{1,0:T(8,128)(2,1)} %wag.3) | copy-start | bytes 98308
  2.3 7.5 %copy-start.3 = (bf16[128,128]{1,0:T(8,128)(2,1)S(1)}, bf16[128,128]{1,0:T(8,128)(2,1)}, u32[]{:S(2)}) copy-start(bf16[128,128]{1,0:T(8,128)(2,1)} %wbp.3) | copy-start | bytes 98308
  2.3 7.5 %copy-start.4 = (bf16[128,128]{1,0:T(8,128)(2,1)S(1)}, bf16[128,128]{1,0:T(8,128)(2,1)}, u32[]{:S(2)}) copy-start(bf16[128,128]{1,0:T(8,128)(2,1)} %wbg.3) | copy-start | bytes 98308
  2.4 7.5 %copy-start.5 = (bf16[128,128]{1,0:T(8,128)(2,1)S(1)}, bf16[128,128]{1,0:T(8,128)(2,1)}, u32[]{:S(2)}) copy-start(bf16[128,128]{1,0:T(8,128)(2,1)} %w_gate.3) | copy-start | bytes 98308
  2.4 7.5 %copy-start.6 = (bf16[4,128,128]{2,1,0:T(8,128)(2,1)S(1)}, bf16[4,128,128]{2,1,0:T(8,128)(2,1)}, u32[]{:S(2)}) copy-start(bf16[4,128,128]{2,1,0:T(8,128)(2,1)} %grad_ref.1) | copy-start | bytes 393220
  2.4 7.5 %copy-start.7 = (bf16[128,128]{1,0:T(8,128)(2,1)S(1)}, bf16[128,128]{1,0:T(8,128)(2,1)}, u32[]{:S(2)}) copy-start(bf16[128,128]{1,0:T(8,128)(2,1)} %w_out.3) | copy-start | bytes 98308
  2.4 7.5 %copy-start.11 = (f32[128]{0:T(128)S(1)}, f32[128]{0:T(128)}, u32[]{:S(2)}) copy-start(f32[128]{0:T(128)} %param.23) | copy-start | bytes 1540
  2.4 7.5 %copy-start.12 = (f32[128]{0:T(128)S(1)}, f32[128]{0:T(128)}, u32[]{:S(2)}) copy-start(f32[128]{0:T(128)} %param.24) | copy-start | bytes 1540
  2.4 17.5 %all-to-all-start = ((bf16[32,32,128]{2,1,0:T(8,128)(2,1)}), bf16[32,32,128]{2,1,0:T(8,128)(2,1)S(1)}, u32[]{:S(2)}, u32[]{:S(2)}) async-start(bf16[32,32,128]{2,1,0:T(8,128)(2,1)} %edges.1), calls=%async_computation | async-start | bytes 524288 | tf_op jit(solution)/shard_map/all_to_all | solution.py:408
  9.7 0.7 %copy-start.8 = (s32[128]{0:T(128)S(1)}, s32[128]{0:T(128)}, u32[]{:S(2)}) copy-start(s32[128]{0:T(128)} %rows_ref.1) | copy-start | bytes 1540
  9.7 0.7 %copy-start.9 = (f32[128]{0:T(128)S(1)}, f32[128]{0:T(128)}, u32[]{:S(2)}) copy-start(f32[128]{0:T(128)} %param.16) | copy-start | bytes 1540
  9.8 0.7 %copy-start.10 = (f32[128]{0:T(128)S(1)}, f32[128]{0:T(128)}, u32[]{:S(2)}) copy-start(f32[128]{0:T(128)} %param.17) | copy-start | bytes 1540

commit v8 on v7

--- a/solution.py
+++ b/solution.py
@@ -141,6 +141,12 @@
     )
 
 
+def turn(values):
+    shape = (values.shape[1], values.shape[1])
+    row, lane = (lax.broadcasted_iota(jnp.int32, shape, dim) for dim in range(2))
+    return dot(jnp.where(row == lane, 1.0, 0.0).astype(BF16), values, 1, 1)
+
+
 def across(row, count):
     return jnp.transpose(jnp.broadcast_to(row, (count, row.shape[1])))
 
@@ -204,7 +210,7 @@
     half = out_ref.shape[1] // 2
     for copy in copies[:3]:
         copy.wait()
-    act = jnp.concatenate([jnp.transpose(act_ref[r].astype(F32)) for r in range(own)], axis=1)
+    act = turn(act_ref[...].reshape(own * cols, chan))
     gain = across(gain_ref[...], cols)
     bias = across(bias_ref[...], cols)
     centre = act - jnp.mean(act, axis=0, keepdims=True)
@@ -349,7 +355,7 @@
     mean_proj = jnp.mean(grad_hat * normed, axis=0, keepdims=True)
     grad = rstd_t[...] * (grad_hat - mean_grad - normed * mean_proj)
     for r in range(own):
-        out_ref[r] = jnp.transpose(grad[:, r * cols : (r + 1) * cols]).astype(BF16)
+        out_ref[r] = turn(grad[:, r * cols : (r + 1) * cols].astype(BF16)).astype(BF16)
 
 
 VMEM = pl.BlockSpec(memory_space=pltpu.VMEM)

time: 55.3 us -> 55.5 us (level)
  no operation moved by 1% of the time
where the time goes in v8:
time: 55.5 us; the launch traced here: 55.2 us
  blocking collectives  33 us (59%)
  waiting for transfers between devices  8.28 us (15%)
  starting transfers between devices  7.3 us (13%)
  Pallas kernels  5.83 us (11%)
  local copies, waits for them, and re-layouts  0.63 us (1%)
    all_to_all x3, blocking collectives, exchange(): lax.all_to_all(value, 'dap', split_axis=0, concat_axis=0, axis_index_grou...  33 us
    all_to_all x1, waiting for transfers between devices, exchange(): lax.all_to_all(value, 'dap', split_axis=0, concat_axis=0, axis_index_grou...  8.28 us
    all_to_all x1, starting transfers between devices, exchange(): lax.all_to_all(value, 'dap', split_axis=0, concat_axis=0, axis_index_grou...  7.3 us
    pallas_call x6, Pallas kernels, call(): pl.pallas_call(kernel, name=name, out_shape=shapes, in_specs=[SMEM] * sca...  5.83 us
  transfers between devices with their start and end apart: 1, of which 1 were waited for; matrix products, arithmetic and copies ran while one was open for 0% of the time, Pallas kernels for 2%

profile of v8, /device:TPU:0, one launch (start us, length us, event | category | flops | bytes accessed | tf_op | source)
XLA Modules:
  0.0 55.2 jit_solution(425963271601887375)
XLA Ops:
  0.0 2.4 %edges.1 = bf16[32,32,128]{2,1,0:T(8,128)(2,1)} custom-call(s32[1]{0:T(128)} %bitcast.me_ref, bf16[4,128,128]{2,1,0:T(8,128)(2,1)} %act_ref.1, f32[1,128]{1,0:T(1,128)} %bitcast.8, f32[1,128]{1,0:T(1,128)} %bitcast.10, s32[128]{0:T(128)} %rows_ref.1, s32[1,128]{1,0:T(1,128)} %bitcast.6, bf16[128,128]{1,0:T(8,128)(2,1)} %wap.3, bf16[128,128]{1,0:T(8,128)(2,1)} %wag.3, ...), custom_call_target="tpu_custom_call" | custom-call | flops 67108864 | bytes 526340 | tf_op jit(solution)/shard_map/edges/pallas_call | solution.py:369
  2.4 0.0 copy-start
  2.4 0.0 copy-start.1
  2.4 0.0 copy-start.2
  2.4 0.0 copy-start.3
  2.4 0.0 copy-start.4
  2.4 0.0 copy-start.5
  2.4 0.0 copy-start.6
  2.5 0.0 copy-start.7
  2.5 0.0 copy-start.11
  2.5 0.0 copy-start.12
  2.5 7.3 %all-to-all-start = ((bf16[32,32,128]{2,1,0:T(8,128)(2,1)}), bf16[32,32,128]{2,1,0:T(8,128)(2,1)S(1)}, u32[]{:S(2)}, u32[]{:S(2)}) async-start(bf16[32,32,128]{2,1,0:T(8,128)(2,1)} %edges.1), calls=%async_computation | async-start | bytes 524288 | tf_op jit(solution)/shard_map/all_to_all | solution.py:414
  9.8 0.0 copy-start.8
  9.8 0.0 copy-start.9
  9.8 0.0 copy-start.10
  9.8 0.0 copy-done
  9.9 0.0 copy-done.1
  9.9 0.0 copy-done.2
  9.9 0.0 copy-done.3
  9.9 0.0 copy-done.4
  9.9 0.0 copy-done.5
  9.9 0.0 copy-done.6
  9.9 0.0 copy-done.7
  9.9 0.0 copy-done.11
  9.9 0.0 copy-done.12
  9.9 0.5 copy-done.8
  10.5 0.0 copy-done.9
  10.5 0.0 copy-done.10
  10.5 1.2 %gates.1 = (f32[4,128,512]{2,1,0:T(8,128)S(1)}, f32[128,512]{1,0:T(8,128)S(1)}, f32[1,512]{1,0:T(1,128)S(1)}, f32[128,128]{1,0:T(8,128)S(1)}, f32[512,128]{1,0:T...) custom-call(s32[1]{0:T(128)} %bitcast.me_ref, s32[128]{0:T(128)S(1)} %copy-done.8, ...), custom_call_target="tpu_custom_call" | custom-call | flops 100663296 | bytes 2495492 | tf_op jit(solution)/shard_map/gates/pallas_call | solution.py:369
  11.7 8.3 %all-to-all-done.in_ref = bf16[32,32,128]{2,1,0:T(8,128)(2,1)S(1)} async-done(((bf16[32,32,128]{2,1,0:T(8,128)(2,1)}), bf16[32,32,128]{2,1,0:T(8,128)(2,1)S(1)}, u32[]{:S(2)}, u32[]{:S(2)}) %all-to-all-start) | async-done | bytes 262176 | tf_op jit(solution)/shard_map/all_to_all | solution.py:414
  20.0 0.2 triangle.1
  20.2 10.9 %all_to_all.20.tri_ref = bf16[32,16,128]{2,1,0:T(8,128)(2,1)S(1)} all-to-all(bf16[32,16,128]{2,1,0:T(8,128)(2,1)S(1)} %get-tuple-element.19), channel_id=1, replica_groups={{0,8,16,24,1,9,17,25,2,10,18,26,3,11,19,27,4,12,20,28,5,13,21,29,6,14,2..., dimensions={0} | all-to-all | bytes 262144 | tf_op jit(solution)/shard_map/all_to_all | solution.py:414
  31.2 0.5 norm.1
  31.7 10.1 %all_to_all.21.in_ref = bf16[32,16,128]{2,1,0:T(8,128)(2,1)S(1)} all-to-all(bf16[32,16,128]{2,1,0:T(8,128)(2,1)S(1)} %get-tuple-element.23), channel_id=1, replica_groups={{0,8,16,24,1,9,17,25,2,10,18,26,3,11,19,27,4,12,20,28,5,13,21,29,6,14,2..., dimensions={0} | all-to-all | bytes 262144 | tf_op jit(solution)/shard_map/all_to_all | solution.py:414
  41.8 0.2 edge_grad.1
  42.0 11.9 %all_to_all.22.in_ref = bf16[32,32,128]{2,1,0:T(8,128)(2,1)S(1)} all-to-all(bf16[32,32,128]{2,1,0:T(8,128)(2,1)S(1)} %edge_grad.1), channel_id=1, replica_groups={{0,8,16,24,1,9,17,25,2,10,18,26,3,11,19,27,4,12,20,28,5,13,21,29,6,14,2..., dimensions={0} | all-to-all | bytes 524288 | tf_op jit(solution)/shard_map/all_to_all | solution.py:414
  53.9 1.3 %input_grad.1 = bf16[4,128,128]{2,1,0:T(8,128)(2,1)} custom-call(bf16[32,32,128]{2,1,0:T(8,128)(2,1)S(1)} %all_to_all.22.in_ref, f32[4,128,512]{2,1,0:T(8,128)S(1)} %get-tuple-element.26.factors, f32[128,512]{1,0:T(8,128)S(1)} %get-tuple-element.27.normed_t, f32[1,512]{1,0:T(1,128)S(1)} %get-tuple-element.28.rstd_t, ...), custom_call_target="tpu_custom_call" | custom-call | flops 67108864 | bytes 2066432 | tf_op jit(solution)/shard_map/input_grad/pallas_call | solution.py:369
Async XLA Ops:
  2.4 7.5 %copy-start = (bf16[4,128,128]{2,1,0:T(8,128)(2,1)S(1)}, bf16[4,128,128]{2,1,0:T(8,128)(2,1)}, u32[]{:S(2)}) copy-start(bf16[4,128,128]{2,1,0:T(8,128)(2,1)} %act_ref.1) | copy-start | bytes 393220
  2.4 7.5 %copy-start.1 = (bf16[128,128]{1,0:T(8,128)(2,1)S(1)}, bf16[128,128]{1,0:T(8,128)(2,1)}, u32[]{:S(2)}) copy-start(bf16[128,128]{1,0:T(8,128)(2,1)} %wap.3) | copy-start | bytes 98308
  2.4 7.5 %copy-start.2 = (bf16[128,128]{1,0:T(8,128)(2,1)S(1)}, bf16[128,128]{1,0:T(8,128)(2,1)}, u32[]{:S(2)}) copy-start(bf16[128,128]{1,0:T(8,128)(2,1)} %wag.3) | copy-start | bytes 98308
  2.4 7.5 %copy-start.3 = (bf16[128,128]{1,0:T(8,128)(2,1)S(1)}, bf16[128,128]{1,0:T(8,128)(2,1)}, u32[]{:S(2)}) copy-start(bf16[128,128]{1,0:T(8,128)(2,1)} %wbp.3) | copy-start | bytes 98308
  2.4 7.5 %copy-start.4 = (bf16[128,128]{1,0:T(8,128)(2,1)S(1)}, bf16[128,128]{1,0:T(8,128)(2,1)}, u32[]{:S(2)}) copy-start(bf16[128,128]{1,0:T(8,128)(2,1)} %wbg.3) | copy-start | bytes 98308
  2.4 7.5 %copy-start.5 = (bf16[128,128]{1,0:T(8,128)(2,1)S(1)}, bf16[128,128]{1,0:T(8,128)(2,1)}, u32[]{:S(2)}) copy-start(bf16[128,128]{1,0:T(8,128)(2,1)} %w_gate.3) | copy-start | bytes 98308
  2.4 7.5 %copy-start.6 = (bf16[4,128,128]{2,1,0:T(8,128)(2,1)S(1)}, bf16[4,128,128]{2,1,0:T(8,128)(2,1)}, u32[]{:S(2)}) copy-start(bf16[4,128,128]{2,1,0:T(8,128)(2,1)} %grad_ref.1) | copy-start | bytes 393220
  2.5 7.5 %copy-start.7 = (bf16[128,128]{1,0:T(8,128)(2,1)S(1)}, bf16[128,128]{1,0:T(8,128)(2,1)}, u32[]{:S(2)}) copy-start(bf16[128,128]{1,0:T(8,128)(2,1)} %w_out.3) | copy-start | bytes 98308
  2.5 7.5 %copy-start.11 = (f32[128]{0:T(128)S(1)}, f32[128]{0:T(128)}, u32[]{:S(2)}) copy-start(f32[128]{0:T(128)} %param.23) | copy-start | bytes 1540
  2.5 7.5 %copy-start.12 = (f32[128]{0:T(128)S(1)}, f32[128]{0:T(128)}, u32[]{:S(2)}) copy-start(f32[128]{0:T(128)} %param.24) | copy-start | bytes 1540
  2.5 17.5 %all-to-all-start = ((bf16[32,32,128]{2,1,0:T(8,128)(2,1)}), bf16[32,32,128]{2,1,0:T(8,128)(2,1)S(1)}, u32[]{:S(2)}, u32[]{:S(2)}) async-start(bf16[32,32,128]{2,1,0:T(8,128)(2,1)} %edges.1), calls=%async_computation | async-start | bytes 524288 | tf_op jit(solution)/shard_map/all_to_all | solution.py:414
  9.8 0.7 %copy-start.8 = (s32[128]{0:T(128)S(1)}, s32[128]{0:T(128)}, u32[]{:S(2)}) copy-start(s32[128]{0:T(128)} %rows_ref.1) | copy-start | bytes 1540
  9.8 0.7 %copy-start.9 = (f32[128]{0:T(128)S(1)}, f32[128]{0:T(128)}, u32[]{:S(2)}) copy-start(f32[128]{0:T(128)} %param.16) | copy-start | bytes 1540
  9.8 0.7 %copy-start.10 = (f32[128]{0:T(128)S(1)}, f32[128]{0:T(128)}, u32[]{:S(2)}) copy-start(f32[128]{0:T(128)} %param.17) | copy-start | bytes 1540

commit v9 on v7

--- a/solution.py
+++ b/solution.py
@@ -132,7 +132,6 @@
 F32 = jnp.float32
 BF16 = jnp.bfloat16
 SUBLANES = 8
-LEVELS = 4
 
 
 def dot(lhs, rhs, lhs_dim, rhs_dim):
@@ -152,16 +151,6 @@
         jnp.where(low, first, pltpu.roll(second, weight, 1)),
         jnp.where(low, pltpu.roll(first, SUBLANES - weight, 1), second),
     )
-
-
-def mesh_order(blocks):
-    count, *rest = blocks.shape
-    return jnp.swapaxes(blocks.reshape(count // LEVELS, LEVELS, *rest), 0, 1).reshape(blocks.shape)
-
-
-def list_order(blocks):
-    count, *rest = blocks.shape
-    return jnp.swapaxes(blocks.reshape(LEVELS, count // LEVELS, *rest), 0, 1).reshape(blocks.shape)
 
 
 def split_channels(blocks, own):
@@ -273,9 +262,7 @@
 def triangle_kernel(own, in_ref, _, out_ref, a_ref, b_ref):
     half = out_ref.shape[1]
     sides = [
-        split_channels(
-            mesh_order(in_ref[:, side * half : (side + 1) * half, :].astype(F32)), own
-        )
+        split_channels(in_ref[:, side * half : (side + 1) * half, :].astype(F32), own)
         for side in range(2)
     ]
     tri = []
@@ -283,7 +270,7 @@
         a_ref[c] = edge_a.astype(BF16)
         b_ref[c] = edge_b.astype(BF16)
         tri.append(dot(a_ref[c], b_ref[c], 1, 1))
-    out_ref[...] = list_order(merge_channels(tri, own)).astype(BF16)
+    out_ref[...] = merge_channels(tri, own).astype(BF16)
 
 
 def fold(values, own):
@@ -319,13 +306,13 @@
 def edge_grad_kernel(own, in_ref, a_ref, b_ref, out_ref):
     block = in_ref.shape[1]
     grads = ([], [])
-    for c, part in enumerate(split_channels(mesh_order(in_ref[...].astype(F32)), own)):
+    for c, part in enumerate(split_channels(in_ref[...].astype(F32), own)):
         d_tri = part.astype(BF16)
         grads[0].append(dot(d_tri, b_ref[c], 1, 0))
         grads[1].append(dot(d_tri, a_ref[c], 0, 0))
     for side in range(2):
         out_ref[:, side * block : (side + 1) * block, :] = (
-            list_order(merge_channels(grads[side], own)).astype(BF16)
+            merge_channels(grads[side], own).astype(BF16)
         )
 
 
@@ -402,12 +389,8 @@
     w_edges = (w_a_proj, w_a_gate, w_b_proj, w_b_gate)
     product = 2 * own * cols * chan * hidden
 
-    listed = [quarter * (dap // LEVELS) + at for at in range(dap // LEVELS) for quarter in range(LEVELS)]
-
     def exchange(value):
-        return lax.all_to_all(
-            value, "dap", split_axis=0, concat_axis=0, axis_index_groups=[listed], tiled=True
-        )
+        return lax.all_to_all(value, "dap", split_axis=0, concat_axis=0, tiled=True)
 
     first = (pair_act, gain_in, bias_in, residue_mask, valid, *w_edges)
     edges = call(

time: 55.3 us -> 55.6 us (level)
  no operation moved by 1% of the time
where the time goes in v9:
time: 55.6 us; the launch traced here: 55.3 us
  blocking collectives  32.8 us (59%)
  waiting for transfers between devices  8.68 us (16%)
  starting transfers between devices  7.31 us (13%)
  Pallas kernels  5.65 us (10%)
  local copies, waits for them, and re-layouts  0.63 us (1%)
    all_to_all x3, blocking collectives, exchange(): return lax.all_to_all(value, 'dap', split_axis=0, concat_axis=0, tiled=True)  32.8 us
    all_to_all x1, waiting for transfers between devices, exchange(): return lax.all_to_all(value, 'dap', split_axis=0, concat_axis=0, tiled=True)  8.68 us
    all_to_all x1, starting transfers between devices, exchange(): return lax.all_to_all(value, 'dap', split_axis=0, concat_axis=0, tiled=True)  7.31 us
    pallas_call x6, Pallas kernels, call(): pl.pallas_call(kernel, name=name, out_shape=shapes, in_specs=[SMEM] * sca...  5.65 us
  transfers between devices with their start and end apart: 1, of which 1 were waited for; matrix products, arithmetic and copies ran while one was open for 0% of the time, Pallas kernels for 2%

profile of v9, /device:TPU:0, one launch (start us, length us, event | category | flops | bytes accessed | tf_op | source)
XLA Modules:
  0.0 55.3 jit_solution(1448636537350740964)
XLA Ops:
  0.0 2.3 %edges.1 = bf16[32,32,128]{2,1,0:T(8,128)(2,1)} custom-call(s32[1]{0:T(128)} %bitcast.me_ref, bf16[4,128,128]{2,1,0:T(8,128)(2,1)} %act_ref.1, f32[1,128]{1,0:T(1,128)} %bitcast.8, f32[1,128]{1,0:T(1,128)} %bitcast.10, s32[128]{0:T(128)} %rows_ref.1, s32[1,128]{1,0:T(1,128)} %bitcast.6, bf16[128,128]{1,0:T(8,128)(2,1)} %wap.3, bf16[128,128]{1,0:T(8,128)(2,1)} %wag.3, ...), custom_call_target="tpu_custom_call" | custom-call | flops 67108864 | bytes 526340 | tf_op jit(solution)/shard_map/edges/pallas_call | solution.py:350
  2.3 0.0 copy-start
  2.3 0.0 copy-start.1
  2.3 0.0 copy-start.2
  2.3 0.0 copy-start.3
  2.3 0.0 copy-start.4
  2.4 0.0 copy-start.5
  2.4 0.0 copy-start.6
  2.4 0.0 copy-start.7
  2.4 0.0 copy-start.11
  2.4 0.0 copy-start.12
  2.4 7.3 %all-to-all-start = ((bf16[32,32,128]{2,1,0:T(8,128)(2,1)}), bf16[32,32,128]{2,1,0:T(8,128)(2,1)S(1)}, u32[]{:S(2)}, u32[]{:S(2)}) async-start(bf16[32,32,128]{2,1,0:T(8,128)(2,1)} %edges.1), calls=%async_computation | async-start | bytes 524288 | tf_op jit(solution)/shard_map/all_to_all | solution.py:393
  9.7 0.0 copy-start.8
  9.7 0.0 copy-start.9
  9.8 0.0 copy-start.10
  9.8 0.0 copy-done
  9.8 0.0 copy-done.1
  9.8 0.0 copy-done.2
  9.8 0.0 copy-done.3
  9.8 0.0 copy-done.4
  9.8 0.0 copy-done.5
  9.8 0.0 copy-done.6
  9.8 0.0 copy-done.7
  9.8 0.0 copy-done.11
  9.9 0.0 copy-done.12
  9.9 0.5 copy-done.8
  10.4 0.0 copy-done.9
  10.4 0.0 copy-done.10
  10.4 1.2 %gates.1 = (f32[4,128,512]{2,1,0:T(8,128)S(1)}, f32[128,512]{1,0:T(8,128)S(1)}, f32[1,512]{1,0:T(1,128)S(1)}, f32[128,128]{1,0:T(8,128)S(1)}, f32[512,128]{1,0:T...) custom-call(s32[1]{0:T(128)} %bitcast.me_ref, s32[128]{0:T(128)S(1)} %copy-done.8, ...), custom_call_target="tpu_custom_call" | custom-call | flops 100663296 | bytes 2495492 | tf_op jit(solution)/shard_map/gates/pallas_call | solution.py:350
  11.7 8.7 %all-to-all-done.in_ref = bf16[32,32,128]{2,1,0:T(8,128)(2,1)S(1)} async-done(((bf16[32,32,128]{2,1,0:T(8,128)(2,1)}), bf16[32,32,128]{2,1,0:T(8,128)(2,1)S(1)}, u32[]{:S(2)}, u32[]{:S(2)}) %all-to-all-start) | async-done | bytes 262176 | tf_op jit(solution)/shard_map/all_to_all | solution.py:393
  20.3 0.2 triangle.1
  20.6 10.4 %all_to_all.20.tri_ref = bf16[32,16,128]{2,1,0:T(8,128)(2,1)S(1)} all-to-all(bf16[32,16,128]{2,1,0:T(8,128)(2,1)S(1)} %get-tuple-element.19), channel_id=1, replica_groups=mesh['grp'=1,'dap'=32,'ch'=1] {'dap'}, dimensions={0} | all-to-all | bytes 262144 | tf_op jit(solution)/shard_map/all_to_all | solution.py:393
  31.0 0.5 norm.1
  31.5 10.0 %all_to_all.21.in_ref = bf16[32,16,128]{2,1,0:T(8,128)(2,1)S(1)} all-to-all(bf16[32,16,128]{2,1,0:T(8,128)(2,1)S(1)} %get-tuple-element.23), channel_id=1, replica_groups=mesh['grp'=1,'dap'=32,'ch'=1] {'dap'}, dimensions={0} | all-to-all | bytes 262144 | tf_op jit(solution)/shard_map/all_to_all | solution.py:393
  41.5 0.2 edge_grad.1
  41.8 12.4 %all_to_all.22.in_ref = bf16[32,32,128]{2,1,0:T(8,128)(2,1)S(1)} all-to-all(bf16[32,32,128]{2,1,0:T(8,128)(2,1)S(1)} %edge_grad.1), channel_id=1, replica_groups=mesh['grp'=1,'dap'=32,'ch'=1] {'dap'}, dimensions={0} | all-to-all | bytes 524288 | tf_op jit(solution)/shard_map/all_to_all | solution.py:393
  54.1 1.2 %input_grad.1 = bf16[4,128,128]{2,1,0:T(8,128)(2,1)} custom-call(bf16[32,32,128]{2,1,0:T(8,128)(2,1)S(1)} %all_to_all.22.in_ref, f32[4,128,512]{2,1,0:T(8,128)S(1)} %get-tuple-element.26.factors, f32[128,512]{1,0:T(8,128)S(1)} %get-tuple-element.27.normed_t, f32[1,512]{1,0:T(1,128)S(1)} %get-tuple-element.28.rstd_t, ...), custom_call_target="tpu_custom_call" | custom-call | flops 67108864 | bytes 2066432 | tf_op jit(solution)/shard_map/input_grad/pallas_call | solution.py:350
Async XLA Ops:
  2.3 7.5 %copy-start = (bf16[4,128,128]{2,1,0:T(8,128)(2,1)S(1)}, bf16[4,128,128]{2,1,0:T(8,128)(2,1)}, u32[]{:S(2)}) copy-start(bf16[4,128,128]{2,1,0:T(8,128)(2,1)} %act_ref.1) | copy-start | bytes 393220
  2.3 7.5 %copy-start.1 = (bf16[128,128]{1,0:T(8,128)(2,1)S(1)}, bf16[128,128]{1,0:T(8,128)(2,1)}, u32[]{:S(2)}) copy-start(bf16[128,128]{1,0:T(8,128)(2,1)} %wap.3) | copy-start | bytes 98308
  2.3 7.5 %copy-start.2 = (bf16[128,128]{1,0:T(8,128)(2,1)S(1)}, bf16[128,128]{1,0:T(8,128)(2,1)}, u32[]{:S(2)}) copy-start(bf16[128,128]{1,0:T(8,128)(2,1)} %wag.3) | copy-start | bytes 98308
  2.3 7.5 %copy-start.3 = (bf16[128,128]{1,0:T(8,128)(2,1)S(1)}, bf16[128,128]{1,0:T(8,128)(2,1)}, u32[]{:S(2)}) copy-start(bf16[128,128]{1,0:T(8,128)(2,1)} %wbp.3) | copy-start | bytes 98308
  2.3 7.5 %copy-start.4 = (bf16[128,128]{1,0:T(8,128)(2,1)S(1)}, bf16[128,128]{1,0:T(8,128)(2,1)}, u32[]{:S(2)}) copy-start(bf16[128,128]{1,0:T(8,128)(2,1)} %wbg.3) | copy-start | bytes 98308
  2.4 7.5 %copy-start.5 = (bf16[128,128]{1,0:T(8,128)(2,1)S(1)}, bf16[128,128]{1,0:T(8,128)(2,1)}, u32[]{:S(2)}) copy-start(bf16[128,128]{1,0:T(8,128)(2,1)} %w_gate.3) | copy-start | bytes 98308
  2.4 7.5 %copy-start.6 = (bf16[4,128,128]{2,1,0:T(8,128)(2,1)S(1)}, bf16[4,128,128]{2,1,0:T(8,128)(2,1)}, u32[]{:S(2)}) copy-start(bf16[4,128,128]{2,1,0:T(8,128)(2,1)} %grad_ref.1) | copy-start | bytes 393220
  2.4 7.5 %copy-start.7 = (bf16[128,128]{1,0:T(8,128)(2,1)S(1)}, bf16[128,128]{1,0:T(8,128)(2,1)}, u32[]{:S(2)}) copy-start(bf16[128,128]{1,0:T(8,128)(2,1)} %w_out.3) | copy-start | bytes 98308
  2.4 7.5 %copy-start.11 = (f32[128]{0:T(128)S(1)}, f32[128]{0:T(128)}, u32[]{:S(2)}) copy-start(f32[128]{0:T(128)} %param.23) | copy-start | bytes 1540
  2.4 7.5 %copy-start.12 = (f32[128]{0:T(128)S(1)}, f32[128]{0:T(128)}, u32[]{:S(2)}) copy-start(f32[128]{0:T(128)} %param.24) | copy-start | bytes 1540
  2.4 17.9 %all-to-all-start = ((bf16[32,32,128]{2,1,0:T(8,128)(2,1)}), bf16[32,32,128]{2,1,0:T(8,128)(2,1)S(1)}, u32[]{:S(2)}, u32[]{:S(2)}) async-start(bf16[32,32,128]{2,1,0:T(8,128)(2,1)} %edges.1), calls=%async_computation | async-start | bytes 524288 | tf_op jit(solution)/shard_map/all_to_all | solution.py:393
  9.7 0.7 %copy-start.8 = (s32[128]{0:T(128)S(1)}, s32[128]{0:T(128)}, u32[]{:S(2)}) copy-start(s32[128]{0:T(128)} %rows_ref.1) | copy-start | bytes 1540
  9.7 0.7 %copy-start.9 = (f32[128]{0:T(128)S(1)}, f32[128]{0:T(128)}, u32[]{:S(2)}) copy-start(f32[128]{0:T(128)} %param.16) | copy-start | bytes 1540
  9.8 0.7 %copy-start.10 = (f32[128]{0:T(128)S(1)}, f32[128]{0:T(128)}, u32[]{:S(2)}) copy-start(f32[128]{0:T(128)} %param.17) | copy-start | bytes 1540

commit v10 on v7

--- a/solution.py
+++ b/solution.py
@@ -133,6 +133,7 @@
 BF16 = jnp.bfloat16
 SUBLANES = 8
 LEVELS = 4
+CORES = 2
 
 
 def dot(lhs, rhs, lhs_dim, rhs_dim):
@@ -156,12 +157,14 @@
 
 def mesh_order(blocks):
     count, *rest = blocks.shape
-    return jnp.swapaxes(blocks.reshape(count // LEVELS, LEVELS, *rest), 0, 1).reshape(blocks.shape)
+    split = blocks.reshape(count // LEVELS // CORES, LEVELS, CORES, *rest)
+    return jnp.swapaxes(split, 0, 1).reshape(blocks.shape)
 
 
 def list_order(blocks):
     count, *rest = blocks.shape
-    return jnp.swapaxes(blocks.reshape(LEVELS, count // LEVELS, *rest), 0, 1).reshape(blocks.shape)
+    split = blocks.reshape(LEVELS, count // LEVELS // CORES, CORES, *rest)
+    return jnp.swapaxes(split, 0, 1).reshape(blocks.shape)
 
 
 def split_channels(blocks, own):
@@ -402,7 +405,13 @@
     w_edges = (w_a_proj, w_a_gate, w_b_proj, w_b_gate)
     product = 2 * own * cols * chan * hidden
 
-    listed = [quarter * (dap // LEVELS) + at for at in range(dap // LEVELS) for quarter in range(LEVELS)]
+    span = dap // LEVELS
+    listed = [
+        quarter * span + pair * CORES + core
+        for pair in range(span // CORES)
+        for quarter in range(LEVELS)
+        for core in range(CORES)
+    ]
 
     def exchange(value):
         return lax.all_to_all(

time: 55.3 us -> 55 us (level)
  no operation moved by 1% of the time
where the time goes in v10:
time: 55 us; the launch traced here: 54.8 us
  blocking collectives  32.5 us (59%)
  waiting for transfers between devices  8.46 us (15%)
  starting transfers between devices  7.31 us (13%)
  Pallas kernels  5.65 us (10%)
  local copies, waits for them, and re-layouts  0.63 us (1%)
    all_to_all x3, blocking collectives, exchange(): lax.all_to_all(value, 'dap', split_axis=0, concat_axis=0, axis_index_grou...  32.5 us
    all_to_all x1, waiting for transfers between devices, exchange(): lax.all_to_all(value, 'dap', split_axis=0, concat_axis=0, axis_index_grou...  8.46 us
    all_to_all x1, starting transfers between devices, exchange(): lax.all_to_all(value, 'dap', split_axis=0, concat_axis=0, axis_index_grou...  7.31 us
    pallas_call x6, Pallas kernels, call(): pl.pallas_call(kernel, name=name, out_shape=shapes, in_specs=[SMEM] * sca...  5.65 us
  transfers between devices with their start and end apart: 1, of which 1 were waited for; matrix products, arithmetic and copies ran while one was open for 0% of the time, Pallas kernels for 2%

profile of v10, /device:TPU:0, one launch (start us, length us, event | category | flops | bytes accessed | tf_op | source)
XLA Modules:
  0.0 54.8 jit_solution(665471214814395459)
XLA Ops:
  0.0 2.3 %edges.1 = bf16[32,32,128]{2,1,0:T(8,128)(2,1)} custom-call(s32[1]{0:T(128)} %bitcast.me_ref, bf16[4,128,128]{2,1,0:T(8,128)(2,1)} %act_ref.1, f32[1,128]{1,0:T(1,128)} %bitcast.8, f32[1,128]{1,0:T(1,128)} %bitcast.10, s32[128]{0:T(128)} %rows_ref.1, s32[1,128]{1,0:T(1,128)} %bitcast.6, bf16[128,128]{1,0:T(8,128)(2,1)} %wap.3, bf16[128,128]{1,0:T(8,128)(2,1)} %wag.3, ...), custom_call_target="tpu_custom_call" | custom-call | flops 67108864 | bytes 526340 | tf_op jit(solution)/shard_map/edges/pallas_call | solution.py:366
  2.3 0.0 copy-start
  2.3 0.0 copy-start.1
  2.3 0.0 copy-start.2
  2.3 0.0 copy-start.3
  2.3 0.0 copy-start.4
  2.4 0.0 copy-start.5
  2.4 0.0 copy-start.6
  2.4 0.0 copy-start.7
  2.4 0.0 copy-start.11
  2.4 0.0 copy-start.12
  2.4 7.3 %all-to-all-start = ((bf16[32,32,128]{2,1,0:T(8,128)(2,1)}), bf16[32,32,128]{2,1,0:T(8,128)(2,1)S(1)}, u32[]{:S(2)}, u32[]{:S(2)}) async-start(bf16[32,32,128]{2,1,0:T(8,128)(2,1)} %edges.1), calls=%async_computation | async-start | bytes 524288 | tf_op jit(solution)/shard_map/all_to_all | solution.py:417
  9.7 0.0 copy-start.8
  9.7 0.0 copy-start.9
  9.8 0.0 copy-start.10
  9.8 0.0 copy-done
  9.8 0.0 copy-done.1
  9.8 0.0 copy-done.2
  9.8 0.0 copy-done.3
  9.8 0.0 copy-done.4
  9.8 0.0 copy-done.5
  9.8 0.0 copy-done.6
  9.8 0.0 copy-done.7
  9.8 0.0 copy-done.11
  9.9 0.0 copy-done.12
  9.9 0.5 copy-done.8
  10.4 0.0 copy-done.9
  10.4 0.0 copy-done.10
  10.4 1.2 %gates.1 = (f32[4,128,512]{2,1,0:T(8,128)S(1)}, f32[128,512]{1,0:T(8,128)S(1)}, f32[1,512]{1,0:T(1,128)S(1)}, f32[128,128]{1,0:T(8,128)S(1)}, f32[512,128]{1,0:T...) custom-call(s32[1]{0:T(128)} %bitcast.me_ref, s32[128]{0:T(128)S(1)} %copy-done.8, ...), custom_call_target="tpu_custom_call" | custom-call | flops 100663296 | bytes 2495492 | tf_op jit(solution)/shard_map/gates/pallas_call | solution.py:366
  11.7 8.5 %all-to-all-done.in_ref = bf16[32,32,128]{2,1,0:T(8,128)(2,1)S(1)} async-done(((bf16[32,32,128]{2,1,0:T(8,128)(2,1)}), bf16[32,32,128]{2,1,0:T(8,128)(2,1)S(1)}, u32[]{:S(2)}, u32[]{:S(2)}) %all-to-all-start) | async-done | bytes 262176 | tf_op jit(solution)/shard_map/all_to_all | solution.py:417
  20.1 0.2 triangle.1
  20.4 10.5 %all_to_all.20.tri_ref = bf16[32,16,128]{2,1,0:T(8,128)(2,1)S(1)} all-to-all(bf16[32,16,128]{2,1,0:T(8,128)(2,1)S(1)} %get-tuple-element.19), channel_id=1, replica_groups={{0,1,8,9,16,17,24,25,2,3,10,11,18,19,26,27,4,5,12,13,20,21,28,29,6,7,14..., dimensions={0} | all-to-all | bytes 262144 | tf_op jit(solution)/shard_map/all_to_all | solution.py:417
  30.9 0.5 norm.1
  31.3 9.9 %all_to_all.21.in_ref = bf16[32,16,128]{2,1,0:T(8,128)(2,1)S(1)} all-to-all(bf16[32,16,128]{2,1,0:T(8,128)(2,1)S(1)} %get-tuple-element.23), channel_id=1, replica_groups={{0,1,8,9,16,17,24,25,2,3,10,11,18,19,26,27,4,5,12,13,20,21,28,29,6,7,14..., dimensions={0} | all-to-all | bytes 262144 | tf_op jit(solution)/shard_map/all_to_all | solution.py:417
  41.2 0.2 edge_grad.1
  41.5 12.1 %all_to_all.22.in_ref = bf16[32,32,128]{2,1,0:T(8,128)(2,1)S(1)} all-to-all(bf16[32,32,128]{2,1,0:T(8,128)(2,1)S(1)} %edge_grad.1), channel_id=1, replica_groups={{0,1,8,9,16,17,24,25,2,3,10,11,18,19,26,27,4,5,12,13,20,21,28,29,6,7,14..., dimensions={0} | all-to-all | bytes 524288 | tf_op jit(solution)/shard_map/all_to_all | solution.py:417
  53.6 1.2 %input_grad.1 = bf16[4,128,128]{2,1,0:T(8,128)(2,1)} custom-call(bf16[32,32,128]{2,1,0:T(8,128)(2,1)S(1)} %all_to_all.22.in_ref, f32[4,128,512]{2,1,0:T(8,128)S(1)} %get-tuple-element.26.factors, f32[128,512]{1,0:T(8,128)S(1)} %get-tuple-element.27.normed_t, f32[1,512]{1,0:T(1,128)S(1)} %get-tuple-element.28.rstd_t, ...), custom_call_target="tpu_custom_call" | custom-call | flops 67108864 | bytes 2066432 | tf_op jit(solution)/shard_map/input_grad/pallas_call | solution.py:366
Async XLA Ops:
  2.3 7.5 %copy-start = (bf16[4,128,128]{2,1,0:T(8,128)(2,1)S(1)}, bf16[4,128,128]{2,1,0:T(8,128)(2,1)}, u32[]{:S(2)}) copy-start(bf16[4,128,128]{2,1,0:T(8,128)(2,1)} %act_ref.1) | copy-start | bytes 393220
  2.3 7.5 %copy-start.1 = (bf16[128,128]{1,0:T(8,128)(2,1)S(1)}, bf16[128,128]{1,0:T(8,128)(2,1)}, u32[]{:S(2)}) copy-start(bf16[128,128]{1,0:T(8,128)(2,1)} %wap.3) | copy-start | bytes 98308
  2.3 7.5 %copy-start.2 = (bf16[128,128]{1,0:T(8,128)(2,1)S(1)}, bf16[128,128]{1,0:T(8,128)(2,1)}, u32[]{:S(2)}) copy-start(bf16[128,128]{1,0:T(8,128)(2,1)} %wag.3) | copy-start | bytes 98308
  2.3 7.5 %copy-start.3 = (bf16[128,128]{1,0:T(8,128)(2,1)S(1)}, bf16[128,128]{1,0:T(8,128)(2,1)}, u32[]{:S(2)}) copy-start(bf16[128,128]{1,0:T(8,128)(2,1)} %wbp.3) | copy-start | bytes 98308
  2.3 7.5 %copy-start.4 = (bf16[128,128]{1,0:T(8,128)(2,1)S(1)}, bf16[128,128]{1,0:T(8,128)(2,1)}, u32[]{:S(2)}) copy-start(bf16[128,128]{1,0:T(8,128)(2,1)} %wbg.3) | copy-start | bytes 98308
  2.4 7.5 %copy-start.5 = (bf16[128,128]{1,0:T(8,128)(2,1)S(1)}, bf16[128,128]{1,0:T(8,128)(2,1)}, u32[]{:S(2)}) copy-start(bf16[128,128]{1,0:T(8,128)(2,1)} %w_gate.3) | copy-start | bytes 98308
  2.4 7.5 %copy-start.6 = (bf16[4,128,128]{2,1,0:T(8,128)(2,1)S(1)}, bf16[4,128,128]{2,1,0:T(8,128)(2,1)}, u32[]{:S(2)}) copy-start(bf16[4,128,128]{2,1,0:T(8,128)(2,1)} %grad_ref.1) | copy-start | bytes 393220
  2.4 7.5 %copy-start.7 = (bf16[128,128]{1,0:T(8,128)(2,1)S(1)}, bf16[128,128]{1,0:T(8,128)(2,1)}, u32[]{:S(2)}) copy-start(bf16[128,128]{1,0:T(8,128)(2,1)} %w_out.3) | copy-start | bytes 98308
  2.4 7.5 %copy-start.11 = (f32[128]{0:T(128)S(1)}, f32[128]{0:T(128)}, u32[]{:S(2)}) copy-start(f32[128]{0:T(128)} %param.23) | copy-start | bytes 1540
  2.4 7.5 %copy-start.12 = (f32[128]{0:T(128)S(1)}, f32[128]{0:T(128)}, u32[]{:S(2)}) copy-start(f32[128]{0:T(128)} %param.24) | copy-start | bytes 1540
  2.4 17.7 %all-to-all-start = ((bf16[32,32,128]{2,1,0:T(8,128)(2,1)}), bf16[32,32,128]{2,1,0:T(8,128)(2,1)S(1)}, u32[]{:S(2)}, u32[]{:S(2)}) async-start(bf16[32,32,128]{2,1,0:T(8,128)(2,1)} %edges.1), calls=%async_computation | async-start | bytes 524288 | tf_op jit(solution)/shard_map/all_to_all | solution.py:417
  9.7 0.7 %copy-start.8 = (s32[128]{0:T(128)S(1)}, s32[128]{0:T(128)}, u32[]{:S(2)}) copy-start(s32[128]{0:T(128)} %rows_ref.1) | copy-start | bytes 1540
  9.7 0.7 %copy-start.9 = (f32[128]{0:T(128)S(1)}, f32[128]{0:T(128)}, u32[]{:S(2)}) copy-start(f32[128]{0:T(128)} %param.16) | copy-start | bytes 1540
  9.8 0.7 %copy-start.10 = (f32[128]{0:T(128)S(1)}, f32[128]{0:T(128)}, u32[]{:S(2)}) copy-start(f32[128]{0:T(128)} %param.17) | copy-start | bytes 1540

commit v11 on v10

--- a/solution.py
+++ b/solution.py
@@ -155,16 +155,20 @@
     )
 
 
+def falling(blocks):
+    return jnp.concatenate([blocks[at : at + 1] for at in reversed(range(LEVELS))], axis=0)
+
+
 def mesh_order(blocks):
     count, *rest = blocks.shape
     split = blocks.reshape(count // LEVELS // CORES, LEVELS, CORES, *rest)
-    return jnp.swapaxes(split, 0, 1).reshape(blocks.shape)
+    return falling(jnp.swapaxes(split, 0, 1)).reshape(blocks.shape)
 
 
 def list_order(blocks):
     count, *rest = blocks.shape
     split = blocks.reshape(LEVELS, count // LEVELS // CORES, CORES, *rest)
-    return jnp.swapaxes(split, 0, 1).reshape(blocks.shape)
+    return jnp.swapaxes(falling(split), 0, 1).reshape(blocks.shape)
 
 
 def split_channels(blocks, own):
@@ -409,7 +413,7 @@
     listed = [
         quarter * span + pair * CORES + core
         for pair in range(span // CORES)
-        for quarter in range(LEVELS)
+        for quarter in reversed(range(LEVELS))
         for core in range(CORES)
     ]
 

time: 55 us -> 54.6 us (level); the launches traced: 54.8 us -> 53.8 us
  waiting for transfers between devices: 8.46 us -> 7.85 us
    all_to_all x1, waiting for transfers between devices: 8.46 us -> 7.85 us  [exchange(): lax.all_to_all(value, 'dap', split_axis=0, concat_axis=0, axis_index_grou...]
where the time goes in v11:
time: 54.6 us; the launch traced here: 53.8 us
  blocking collectives  32.1 us (59%)
  waiting for transfers between devices  7.85 us (14%)
  starting transfers between devices  7.31 us (13%)
  Pallas kernels  5.65 us (10%)
  local copies, waits for them, and re-layouts  0.63 us (1%)
    all_to_all x3, blocking collectives, exchange(): lax.all_to_all(value, 'dap', split_axis=0, concat_axis=0, axis_index_grou...  32.1 us
    all_to_all x1, waiting for transfers between devices, exchange(): lax.all_to_all(value, 'dap', split_axis=0, concat_axis=0, axis_index_grou...  7.85 us
    all_to_all x1, starting transfers between devices, exchange(): lax.all_to_all(value, 'dap', split_axis=0, concat_axis=0, axis_index_grou...  7.31 us
    pallas_call x6, Pallas kernels, call(): pl.pallas_call(kernel, name=name, out_shape=shapes, in_specs=[SMEM] * sca...  5.65 us
  transfers between devices with their start and end apart: 1, of which 1 were waited for; matrix products, arithmetic and copies ran while one was open for 0% of the time, Pallas kernels for 2%

profile of v11, /device:TPU:0, one launch (start us, length us, event | category | flops | bytes accessed | tf_op | source)
XLA Modules:
  0.0 53.8 jit_solution(14637352244795767143)
XLA Ops:
  0.0 2.3 %edges.1 = bf16[32,32,128]{2,1,0:T(8,128)(2,1)} custom-call(s32[1]{0:T(128)} %bitcast.me_ref, bf16[4,128,128]{2,1,0:T(8,128)(2,1)} %act_ref.1, f32[1,128]{1,0:T(1,128)} %bitcast.8, f32[1,128]{1,0:T(1,128)} %bitcast.10, s32[128]{0:T(128)} %rows_ref.1, s32[1,128]{1,0:T(1,128)} %bitcast.6, bf16[128,128]{1,0:T(8,128)(2,1)} %wap.3, bf16[128,128]{1,0:T(8,128)(2,1)} %wag.3, ...), custom_call_target="tpu_custom_call" | custom-call | flops 67108864 | bytes 526340 | tf_op jit(solution)/shard_map/edges/pallas_call | solution.py:370
  2.3 0.0 copy-start
  2.3 0.0 copy-start.1
  2.3 0.0 copy-start.2
  2.3 0.0 copy-start.3
  2.3 0.0 copy-start.4
  2.4 0.0 copy-start.5
  2.4 0.0 copy-start.6
  2.4 0.0 copy-start.7
  2.4 0.0 copy-start.11
  2.4 0.0 copy-start.12
  2.4 7.3 %all-to-all-start = ((bf16[32,32,128]{2,1,0:T(8,128)(2,1)}), bf16[32,32,128]{2,1,0:T(8,128)(2,1)S(1)}, u32[]{:S(2)}, u32[]{:S(2)}) async-start(bf16[32,32,128]{2,1,0:T(8,128)(2,1)} %edges.1), calls=%async_computation | async-start | bytes 524288 | tf_op jit(solution)/shard_map/all_to_all | solution.py:421
  9.7 0.0 copy-start.8
  9.7 0.0 copy-start.9
  9.8 0.0 copy-start.10
  9.8 0.0 copy-done
  9.8 0.0 copy-done.1
  9.8 0.0 copy-done.2
  9.8 0.0 copy-done.3
  9.8 0.0 copy-done.4
  9.8 0.0 copy-done.5
  9.8 0.0 copy-done.6
  9.8 0.0 copy-done.7
  9.8 0.0 copy-done.11
  9.9 0.0 copy-done.12
  9.9 0.5 copy-done.8
  10.4 0.0 copy-done.9
  10.4 0.0 copy-done.10
  10.4 1.2 %gates.1 = (f32[4,128,512]{2,1,0:T(8,128)S(1)}, f32[128,512]{1,0:T(8,128)S(1)}, f32[1,512]{1,0:T(1,128)S(1)}, f32[128,128]{1,0:T(8,128)S(1)}, f32[512,128]{1,0:T...) custom-call(s32[1]{0:T(128)} %bitcast.me_ref, s32[128]{0:T(128)S(1)} %copy-done.8, ...), custom_call_target="tpu_custom_call" | custom-call | flops 100663296 | bytes 2495492 | tf_op jit(solution)/shard_map/gates/pallas_call | solution.py:370
  11.7 7.9 %all-to-all-done.in_ref = bf16[32,32,128]{2,1,0:T(8,128)(2,1)S(1)} async-done(((bf16[32,32,128]{2,1,0:T(8,128)(2,1)}), bf16[32,32,128]{2,1,0:T(8,128)(2,1)S(1)}, u32[]{:S(2)}, u32[]{:S(2)}) %all-to-all-start) | async-done | bytes 262176 | tf_op jit(solution)/shard_map/all_to_all | solution.py:421
  19.5 0.2 triangle.1
  19.7 10.7 %all_to_all.20.tri_ref = bf16[32,16,128]{2,1,0:T(8,128)(2,1)S(1)} all-to-all(bf16[32,16,128]{2,1,0:T(8,128)(2,1)S(1)} %get-tuple-element.19), channel_id=1, replica_groups={{24,25,16,17,8,9,0,1,26,27,18,19,10,11,2,3,28,29,20,21,12,13,4,5,30,31,..., dimensions={0} | all-to-all | bytes 262144 | tf_op jit(solution)/shard_map/all_to_all | solution.py:421
  30.4 0.5 norm.1
  30.9 9.8 %all_to_all.21.in_ref = bf16[32,16,128]{2,1,0:T(8,128)(2,1)S(1)} all-to-all(bf16[32,16,128]{2,1,0:T(8,128)(2,1)S(1)} %get-tuple-element.23), channel_id=1, replica_groups={{24,25,16,17,8,9,0,1,26,27,18,19,10,11,2,3,28,29,20,21,12,13,4,5,30,31,..., dimensions={0} | all-to-all | bytes 262144 | tf_op jit(solution)/shard_map/all_to_all | solution.py:421
  40.7 0.2 edge_grad.1
  41.0 11.6 %all_to_all.22.in_ref = bf16[32,32,128]{2,1,0:T(8,128)(2,1)S(1)} all-to-all(bf16[32,32,128]{2,1,0:T(8,128)(2,1)S(1)} %edge_grad.1), channel_id=1, replica_groups={{24,25,16,17,8,9,0,1,26,27,18,19,10,11,2,3,28,29,20,21,12,13,4,5,30,31,..., dimensions={0} | all-to-all | bytes 524288 | tf_op jit(solution)/shard_map/all_to_all | solution.py:421
  52.6 1.2 %input_grad.1 = bf16[4,128,128]{2,1,0:T(8,128)(2,1)} custom-call(bf16[32,32,128]{2,1,0:T(8,128)(2,1)S(1)} %all_to_all.22.in_ref, f32[4,128,512]{2,1,0:T(8,128)S(1)} %get-tuple-element.26.factors, f32[128,512]{1,0:T(8,128)S(1)} %get-tuple-element.27.normed_t, f32[1,512]{1,0:T(1,128)S(1)} %get-tuple-element.28.rstd_t, ...), custom_call_target="tpu_custom_call" | custom-call | flops 67108864 | bytes 2066432 | tf_op jit(solution)/shard_map/input_grad/pallas_call | solution.py:370
Async XLA Ops:
  2.3 7.5 %copy-start = (bf16[4,128,128]{2,1,0:T(8,128)(2,1)S(1)}, bf16[4,128,128]{2,1,0:T(8,128)(2,1)}, u32[]{:S(2)}) copy-start(bf16[4,128,128]{2,1,0:T(8,128)(2,1)} %act_ref.1) | copy-start | bytes 393220
  2.3 7.5 %copy-start.1 = (bf16[128,128]{1,0:T(8,128)(2,1)S(1)}, bf16[128,128]{1,0:T(8,128)(2,1)}, u32[]{:S(2)}) copy-start(bf16[128,128]{1,0:T(8,128)(2,1)} %wap.3) | copy-start | bytes 98308
  2.3 7.5 %copy-start.2 = (bf16[128,128]{1,0:T(8,128)(2,1)S(1)}, bf16[128,128]{1,0:T(8,128)(2,1)}, u32[]{:S(2)}) copy-start(bf16[128,128]{1,0:T(8,128)(2,1)} %wag.3) | copy-start | bytes 98308
  2.3 7.5 %copy-start.3 = (bf16[128,128]{1,0:T(8,128)(2,1)S(1)}, bf16[128,128]{1,0:T(8,128)(2,1)}, u32[]{:S(2)}) copy-start(bf16[128,128]{1,0:T(8,128)(2,1)} %wbp.3) | copy-start | bytes 98308
  2.3 7.5 %copy-start.4 = (bf16[128,128]{1,0:T(8,128)(2,1)S(1)}, bf16[128,128]{1,0:T(8,128)(2,1)}, u32[]{:S(2)}) copy-start(bf16[128,128]{1,0:T(8,128)(2,1)} %wbg.3) | copy-start | bytes 98308
  2.4 7.5 %copy-start.5 = (bf16[128,128]{1,0:T(8,128)(2,1)S(1)}, bf16[128,128]{1,0:T(8,128)(2,1)}, u32[]{:S(2)}) copy-start(bf16[128,128]{1,0:T(8,128)(2,1)} %w_gate.3) | copy-start | bytes 98308
  2.4 7.5 %copy-start.6 = (bf16[4,128,128]{2,1,0:T(8,128)(2,1)S(1)}, bf16[4,128,128]{2,1,0:T(8,128)(2,1)}, u32[]{:S(2)}) copy-start(bf16[4,128,128]{2,1,0:T(8,128)(2,1)} %grad_ref.1) | copy-start | bytes 393220
  2.4 7.5 %copy-start.7 = (bf16[128,128]{1,0:T(8,128)(2,1)S(1)}, bf16[128,128]{1,0:T(8,128)(2,1)}, u32[]{:S(2)}) copy-start(bf16[128,128]{1,0:T(8,128)(2,1)} %w_out.3) | copy-start | bytes 98308
  2.4 7.5 %copy-start.11 = (f32[128]{0:T(128)S(1)}, f32[128]{0:T(128)}, u32[]{:S(2)}) copy-start(f32[128]{0:T(128)} %param.23) | copy-start | bytes 1540
  2.4 7.5 %copy-start.12 = (f32[128]{0:T(128)S(1)}, f32[128]{0:T(128)}, u32[]{:S(2)}) copy-start(f32[128]{0:T(128)} %param.24) | copy-start | bytes 1540
  2.4 17.1 %all-to-all-start = ((bf16[32,32,128]{2,1,0:T(8,128)(2,1)}), bf16[32,32,128]{2,1,0:T(8,128)(2,1)S(1)}, u32[]{:S(2)}, u32[]{:S(2)}) async-start(bf16[32,32,128]{2,1,0:T(8,128)(2,1)} %edges.1), calls=%async_computation | async-start | bytes 524288 | tf_op jit(solution)/shard_map/all_to_all | solution.py:421
  9.7 0.7 %copy-start.8 = (s32[128]{0:T(128)S(1)}, s32[128]{0:T(128)}, u32[]{:S(2)}) copy-start(s32[128]{0:T(128)} %rows_ref.1) | copy-start | bytes 1540
  9.7 0.7 %copy-start.9 = (f32[128]{0:T(128)S(1)}, f32[128]{0:T(128)}, u32[]{:S(2)}) copy-start(f32[128]{0:T(128)} %param.16) | copy-start | bytes 1540
  9.8 0.7 %copy-start.10 = (f32[128]{0:T(128)S(1)}, f32[128]{0:T(128)}, u32[]{:S(2)}) copy-start(f32[128]{0:T(128)} %param.17) | copy-start | bytes 1540

commit v12 on v11

--- a/solution.py
+++ b/solution.py
@@ -156,19 +156,19 @@
 
 
 def falling(blocks):
-    return jnp.concatenate([blocks[at : at + 1] for at in reversed(range(LEVELS))], axis=0)
+    return jnp.concatenate([blocks[at : at + 1] for at in reversed(range(blocks.shape[0]))], axis=0)
 
 
 def mesh_order(blocks):
     count, *rest = blocks.shape
     split = blocks.reshape(count // LEVELS // CORES, LEVELS, CORES, *rest)
-    return falling(jnp.swapaxes(split, 0, 1)).reshape(blocks.shape)
+    return falling(jnp.swapaxes(falling(split), 0, 1)).reshape(blocks.shape)
 
 
 def list_order(blocks):
     count, *rest = blocks.shape
     split = blocks.reshape(LEVELS, count // LEVELS // CORES, CORES, *rest)
-    return jnp.swapaxes(falling(split), 0, 1).reshape(blocks.shape)
+    return falling(jnp.swapaxes(falling(split), 0, 1)).reshape(blocks.shape)
 
 
 def split_channels(blocks, own):
@@ -412,7 +412,7 @@
     span = dap // LEVELS
     listed = [
         quarter * span + pair * CORES + core
-        for pair in range(span // CORES)
+        for pair in reversed(range(span // CORES))
         for quarter in reversed(range(LEVELS))
         for core in range(CORES)
     ]

time: 54.6 us -> 54.1 us (level); the launches traced: 53.8 us -> 53.9 us
  no operation moved by 1% of the time
where the time goes in v12:
time: 54.1 us; the launch traced here: 53.9 us
  blocking collectives  32.1 us (59%)
  waiting for transfers between devices  7.92 us (15%)
  starting transfers between devices  7.31 us (14%)
  Pallas kernels  5.65 us (10%)
  local copies, waits for them, and re-layouts  0.63 us (1%)
    all_to_all x3, blocking collectives, exchange(): lax.all_to_all(value, 'dap', split_axis=0, concat_axis=0, axis_index_grou...  32.1 us
    all_to_all x1, waiting for transfers between devices, exchange(): lax.all_to_all(value, 'dap', split_axis=0, concat_axis=0, axis_index_grou...  7.92 us
    all_to_all x1, starting transfers between devices, exchange(): lax.all_to_all(value, 'dap', split_axis=0, concat_axis=0, axis_index_grou...  7.31 us
    pallas_call x6, Pallas kernels, call(): pl.pallas_call(kernel, name=name, out_shape=shapes, in_specs=[SMEM] * sca...  5.65 us
  transfers between devices with their start and end apart: 1, of which 1 were waited for; matrix products, arithmetic and copies ran while one was open for 0% of the time, Pallas kernels for 2%

profile of v12, /device:TPU:0, one launch (start us, length us, event | category | flops | bytes accessed | tf_op | source)
XLA Modules:
  0.0 53.9 jit_solution(16573769028847479104)
XLA Ops:
  0.0 2.3 %edges.1 = bf16[32,32,128]{2,1,0:T(8,128)(2,1)} custom-call(s32[1]{0:T(128)} %bitcast.me_ref, bf16[4,128,128]{2,1,0:T(8,128)(2,1)} %act_ref.1, f32[1,128]{1,0:T(1,128)} %bitcast.8, f32[1,128]{1,0:T(1,128)} %bitcast.10, s32[128]{0:T(128)} %rows_ref.1, s32[1,128]{1,0:T(1,128)} %bitcast.6, bf16[128,128]{1,0:T(8,128)(2,1)} %wap.3, bf16[128,128]{1,0:T(8,128)(2,1)} %wag.3, ...), custom_call_target="tpu_custom_call" | custom-call | flops 67108864 | bytes 526340 | tf_op jit(solution)/shard_map/edges/pallas_call | solution.py:370
  2.3 0.0 copy-start
  2.3 0.0 copy-start.1
  2.3 0.0 copy-start.2
  2.3 0.0 copy-start.3
  2.3 0.0 copy-start.4
  2.4 0.0 copy-start.5
  2.4 0.0 copy-start.6
  2.4 0.0 copy-start.7
  2.4 0.0 copy-start.11
  2.4 0.0 copy-start.12
  2.4 7.3 %all-to-all-start = ((bf16[32,32,128]{2,1,0:T(8,128)(2,1)}), bf16[32,32,128]{2,1,0:T(8,128)(2,1)S(1)}, u32[]{:S(2)}, u32[]{:S(2)}) async-start(bf16[32,32,128]{2,1,0:T(8,128)(2,1)} %edges.1), calls=%async_computation | async-start | bytes 524288 | tf_op jit(solution)/shard_map/all_to_all | solution.py:421
  9.7 0.0 copy-start.8
  9.7 0.0 copy-start.9
  9.8 0.0 copy-start.10
  9.8 0.0 copy-done
  9.8 0.0 copy-done.1
  9.8 0.0 copy-done.2
  9.8 0.0 copy-done.3
  9.8 0.0 copy-done.4
  9.8 0.0 copy-done.5
  9.8 0.0 copy-done.6
  9.8 0.0 copy-done.7
  9.8 0.0 copy-done.11
  9.9 0.0 copy-done.12
  9.9 0.5 copy-done.8
  10.4 0.0 copy-done.9
  10.4 0.0 copy-done.10
  10.4 1.2 %gates.1 = (f32[4,128,512]{2,1,0:T(8,128)S(1)}, f32[128,512]{1,0:T(8,128)S(1)}, f32[1,512]{1,0:T(1,128)S(1)}, f32[128,128]{1,0:T(8,128)S(1)}, f32[512,128]{1,0:T...) custom-call(s32[1]{0:T(128)} %bitcast.me_ref, s32[128]{0:T(128)S(1)} %copy-done.8, ...), custom_call_target="tpu_custom_call" | custom-call | flops 100663296 | bytes 2495492 | tf_op jit(solution)/shard_map/gates/pallas_call | solution.py:370
  11.7 7.9 %all-to-all-done.in_ref = bf16[32,32,128]{2,1,0:T(8,128)(2,1)S(1)} async-done(((bf16[32,32,128]{2,1,0:T(8,128)(2,1)}), bf16[32,32,128]{2,1,0:T(8,128)(2,1)S(1)}, u32[]{:S(2)}, u32[]{:S(2)}) %all-to-all-start) | async-done | bytes 262176 | tf_op jit(solution)/shard_map/all_to_all | solution.py:421
  19.6 0.2 triangle.1
  19.8 10.5 %all_to_all.20.tri_ref = bf16[32,16,128]{2,1,0:T(8,128)(2,1)S(1)} all-to-all(bf16[32,16,128]{2,1,0:T(8,128)(2,1)S(1)} %get-tuple-element.19), channel_id=1, replica_groups={{30,31,22,23,14,15,6,7,28,29,20,21,12,13,4,5,26,27,18,19,10,11,2,3,24,2..., dimensions={0} | all-to-all | bytes 262144 | tf_op jit(solution)/shard_map/all_to_all | solution.py:421
  30.4 0.5 norm.1
  30.8 9.8 %all_to_all.21.in_ref = bf16[32,16,128]{2,1,0:T(8,128)(2,1)S(1)} all-to-all(bf16[32,16,128]{2,1,0:T(8,128)(2,1)S(1)} %get-tuple-element.23), channel_id=1, replica_groups={{30,31,22,23,14,15,6,7,28,29,20,21,12,13,4,5,26,27,18,19,10,11,2,3,24,2..., dimensions={0} | all-to-all | bytes 262144 | tf_op jit(solution)/shard_map/all_to_all | solution.py:421
  40.6 0.2 edge_grad.1
  40.9 11.8 %all_to_all.22.in_ref = bf16[32,32,128]{2,1,0:T(8,128)(2,1)S(1)} all-to-all(bf16[32,32,128]{2,1,0:T(8,128)(2,1)S(1)} %edge_grad.1), channel_id=1, replica_groups={{30,31,22,23,14,15,6,7,28,29,20,21,12,13,4,5,26,27,18,19,10,11,2,3,24,2..., dimensions={0} | all-to-all | bytes 524288 | tf_op jit(solution)/shard_map/all_to_all | solution.py:421
  52.7 1.2 %input_grad.1 = bf16[4,128,128]{2,1,0:T(8,128)(2,1)} custom-call(bf16[32,32,128]{2,1,0:T(8,128)(2,1)S(1)} %all_to_all.22.in_ref, f32[4,128,512]{2,1,0:T(8,128)S(1)} %get-tuple-element.26.factors, f32[128,512]{1,0:T(8,128)S(1)} %get-tuple-element.27.normed_t, f32[1,512]{1,0:T(1,128)S(1)} %get-tuple-element.28.rstd_t, ...), custom_call_target="tpu_custom_call" | custom-call | flops 67108864 | bytes 2066432 | tf_op jit(solution)/shard_map/input_grad/pallas_call | solution.py:370
Async XLA Ops:
  2.3 7.5 %copy-start = (bf16[4,128,128]{2,1,0:T(8,128)(2,1)S(1)}, bf16[4,128,128]{2,1,0:T(8,128)(2,1)}, u32[]{:S(2)}) copy-start(bf16[4,128,128]{2,1,0:T(8,128)(2,1)} %act_ref.1) | copy-start | bytes 393220
  2.3 7.5 %copy-start.1 = (bf16[128,128]{1,0:T(8,128)(2,1)S(1)}, bf16[128,128]{1,0:T(8,128)(2,1)}, u32[]{:S(2)}) copy-start(bf16[128,128]{1,0:T(8,128)(2,1)} %wap.3) | copy-start | bytes 98308
  2.3 7.5 %copy-start.2 = (bf16[128,128]{1,0:T(8,128)(2,1)S(1)}, bf16[128,128]{1,0:T(8,128)(2,1)}, u32[]{:S(2)}) copy-start(bf16[128,128]{1,0:T(8,128)(2,1)} %wag.3) | copy-start | bytes 98308
  2.3 7.5 %copy-start.3 = (bf16[128,128]{1,0:T(8,128)(2,1)S(1)}, bf16[128,128]{1,0:T(8,128)(2,1)}, u32[]{:S(2)}) copy-start(bf16[128,128]{1,0:T(8,128)(2,1)} %wbp.3) | copy-start | bytes 98308
  2.3 7.5 %copy-start.4 = (bf16[128,128]{1,0:T(8,128)(2,1)S(1)}, bf16[128,128]{1,0:T(8,128)(2,1)}, u32[]{:S(2)}) copy-start(bf16[128,128]{1,0:T(8,128)(2,1)} %wbg.3) | copy-start | bytes 98308
  2.4 7.5 %copy-start.5 = (bf16[128,128]{1,0:T(8,128)(2,1)S(1)}, bf16[128,128]{1,0:T(8,128)(2,1)}, u32[]{:S(2)}) copy-start(bf16[128,128]{1,0:T(8,128)(2,1)} %w_gate.3) | copy-start | bytes 98308
  2.4 7.5 %copy-start.6 = (bf16[4,128,128]{2,1,0:T(8,128)(2,1)S(1)}, bf16[4,128,128]{2,1,0:T(8,128)(2,1)}, u32[]{:S(2)}) copy-start(bf16[4,128,128]{2,1,0:T(8,128)(2,1)} %grad_ref.1) | copy-start | bytes 393220
  2.4 7.5 %copy-start.7 = (bf16[128,128]{1,0:T(8,128)(2,1)S(1)}, bf16[128,128]{1,0:T(8,128)(2,1)}, u32[]{:S(2)}) copy-start(bf16[128,128]{1,0:T(8,128)(2,1)} %w_out.3) | copy-start | bytes 98308
  2.4 7.5 %copy-start.11 = (f32[128]{0:T(128)S(1)}, f32[128]{0:T(128)}, u32[]{:S(2)}) copy-start(f32[128]{0:T(128)} %param.23) | copy-start | bytes 1540
  2.4 7.5 %copy-start.12 = (f32[128]{0:T(128)S(1)}, f32[128]{0:T(128)}, u32[]{:S(2)}) copy-start(f32[128]{0:T(128)} %param.24) | copy-start | bytes 1540
  2.4 17.2 %all-to-all-start = ((bf16[32,32,128]{2,1,0:T(8,128)(2,1)}), bf16[32,32,128]{2,1,0:T(8,128)(2,1)S(1)}, u32[]{:S(2)}, u32[]{:S(2)}) async-start(bf16[32,32,128]{2,1,0:T(8,128)(2,1)} %edges.1), calls=%async_computation | async-start | bytes 524288 | tf_op jit(solution)/shard_map/all_to_all | solution.py:421
  9.7 0.7 %copy-start.8 = (s32[128]{0:T(128)S(1)}, s32[128]{0:T(128)}, u32[]{:S(2)}) copy-start(s32[128]{0:T(128)} %rows_ref.1) | copy-start | bytes 1540
  9.7 0.7 %copy-start.9 = (f32[128]{0:T(128)S(1)}, f32[128]{0:T(128)}, u32[]{:S(2)}) copy-start(f32[128]{0:T(128)} %param.16) | copy-start | bytes 1540
  9.8 0.7 %copy-start.10 = (f32[128]{0:T(128)S(1)}, f32[128]{0:T(128)}, u32[]{:S(2)}) copy-start(f32[128]{0:T(128)} %param.17) | copy-start | bytes 1540

commit v13 on v12

--- a/solution.py
+++ b/solution.py
@@ -161,14 +161,14 @@
 
 def mesh_order(blocks):
     count, *rest = blocks.shape
-    split = blocks.reshape(count // LEVELS // CORES, LEVELS, CORES, *rest)
-    return falling(jnp.swapaxes(falling(split), 0, 1)).reshape(blocks.shape)
+    split = falling(blocks).reshape(count // LEVELS // CORES, LEVELS, CORES, *rest)
+    return jnp.swapaxes(split, 0, 1).reshape(blocks.shape)
 
 
 def list_order(blocks):
     count, *rest = blocks.shape
     split = blocks.reshape(LEVELS, count // LEVELS // CORES, CORES, *rest)
-    return falling(jnp.swapaxes(falling(split), 0, 1)).reshape(blocks.shape)
+    return falling(jnp.swapaxes(split, 0, 1).reshape(blocks.shape))
 
 
 def split_channels(blocks, own):
@@ -414,7 +414,7 @@
         quarter * span + pair * CORES + core
         for pair in reversed(range(span // CORES))
         for quarter in reversed(range(LEVELS))
-        for core in range(CORES)
+        for core in reversed(range(CORES))
     ]
 
     def exchange(value):

time: 54.1 us -> 55.3 us (1.022)
  waiting for transfers between devices: 7.92 us -> 8.94 us
    all_to_all x1, waiting for transfers between devices: 7.92 us -> 8.94 us  [exchange(): lax.all_to_all(value, 'dap', split_axis=0, concat_axis=0, axis_index_grou...]
where the time goes in v13:
time: 55.3 us; the launch traced here: 55 us
  blocking collectives  32.3 us (58%)
  waiting for transfers between devices  8.94 us (16%)
  starting transfers between devices  7.31 us (13%)
  Pallas kernels  5.65 us (10%)
  local copies, waits for them, and re-layouts  0.63 us (1%)
    all_to_all x3, blocking collectives, exchange(): lax.all_to_all(value, 'dap', split_axis=0, concat_axis=0, axis_index_grou...  32.3 us
    all_to_all x1, waiting for transfers between devices, exchange(): lax.all_to_all(value, 'dap', split_axis=0, concat_axis=0, axis_index_grou...  8.94 us
    all_to_all x1, starting transfers between devices, exchange(): lax.all_to_all(value, 'dap', split_axis=0, concat_axis=0, axis_index_grou...  7.31 us
    pallas_call x6, Pallas kernels, call(): pl.pallas_call(kernel, name=name, out_shape=shapes, in_specs=[SMEM] * sca...  5.65 us
  transfers between devices with their start and end apart: 1, of which 1 were waited for; matrix products, arithmetic and copies ran while one was open for 0% of the time, Pallas kernels for 2%

profile of v13, /device:TPU:0, one launch (start us, length us, event | category | flops | bytes accessed | tf_op | source)
XLA Modules:
  0.0 55.0 jit_solution(1103867264894949951)
XLA Ops:
  0.0 2.3 %edges.1 = bf16[32,32,128]{2,1,0:T(8,128)(2,1)} custom-call(s32[1]{0:T(128)} %bitcast.me_ref, bf16[4,128,128]{2,1,0:T(8,128)(2,1)} %act_ref.1, f32[1,128]{1,0:T(1,128)} %bitcast.8, f32[1,128]{1,0:T(1,128)} %bitcast.10, s32[128]{0:T(128)} %rows_ref.1, s32[1,128]{1,0:T(1,128)} %bitcast.6, bf16[128,128]{1,0:T(8,128)(2,1)} %wap.3, bf16[128,128]{1,0:T(8,128)(2,1)} %wag.3, ...), custom_call_target="tpu_custom_call" | custom-call | flops 67108864 | bytes 526340 | tf_op jit(solution)/shard_map/edges/pallas_call | solution.py:370
  2.3 0.0 copy-start
  2.3 0.0 copy-start.1
  2.3 0.0 copy-start.2
  2.3 0.0 copy-start.3
  2.3 0.0 copy-start.4
  2.4 0.0 copy-start.5
  2.4 0.0 copy-start.6
  2.4 0.0 copy-start.7
  2.4 0.0 copy-start.11
  2.4 0.0 copy-start.12
  2.4 7.3 %all-to-all-start = ((bf16[32,32,128]{2,1,0:T(8,128)(2,1)}), bf16[32,32,128]{2,1,0:T(8,128)(2,1)S(1)}, u32[]{:S(2)}, u32[]{:S(2)}) async-start(bf16[32,32,128]{2,1,0:T(8,128)(2,1)} %edges.1), calls=%async_computation | async-start | bytes 524288 | tf_op jit(solution)/shard_map/all_to_all | solution.py:421
  9.7 0.0 copy-start.8
  9.7 0.0 copy-start.9
  9.8 0.0 copy-start.10
  9.8 0.0 copy-done
  9.8 0.0 copy-done.1
  9.8 0.0 copy-done.2
  9.8 0.0 copy-done.3
  9.8 0.0 copy-done.4
  9.8 0.0 copy-done.5
  9.8 0.0 copy-done.6
  9.8 0.0 copy-done.7
  9.8 0.0 copy-done.11
  9.9 0.0 copy-done.12
  9.9 0.5 copy-done.8
  10.4 0.0 copy-done.9
  10.4 0.0 copy-done.10
  10.4 1.2 %gates.1 = (f32[4,128,512]{2,1,0:T(8,128)S(1)}, f32[128,512]{1,0:T(8,128)S(1)}, f32[1,512]{1,0:T(1,128)S(1)}, f32[128,128]{1,0:T(8,128)S(1)}, f32[512,128]{1,0:T...) custom-call(s32[1]{0:T(128)} %bitcast.me_ref, s32[128]{0:T(128)S(1)} %copy-done.8, ...), custom_call_target="tpu_custom_call" | custom-call | flops 100663296 | bytes 2495492 | tf_op jit(solution)/shard_map/gates/pallas_call | solution.py:370
  11.7 8.9 %all-to-all-done.in_ref = bf16[32,32,128]{2,1,0:T(8,128)(2,1)S(1)} async-done(((bf16[32,32,128]{2,1,0:T(8,128)(2,1)}), bf16[32,32,128]{2,1,0:T(8,128)(2,1)S(1)}, u32[]{:S(2)}, u32[]{:S(2)}) %all-to-all-start) | async-done | bytes 262176 | tf_op jit(solution)/shard_map/all_to_all | solution.py:421
  20.6 0.2 triangle.1
  20.8 9.8 %all_to_all.20.tri_ref = bf16[32,16,128]{2,1,0:T(8,128)(2,1)S(1)} all-to-all(bf16[32,16,128]{2,1,0:T(8,128)(2,1)S(1)} %get-tuple-element.19), channel_id=1, replica_groups={{31,30,23,22,15,14,7,6,29,28,21,20,13,12,5,4,27,26,19,18,11,10,3,2,25,2..., dimensions={0} | all-to-all | bytes 262144 | tf_op jit(solution)/shard_map/all_to_all | solution.py:421
  30.7 0.5 norm.1
  31.2 9.8 %all_to_all.21.in_ref = bf16[32,16,128]{2,1,0:T(8,128)(2,1)S(1)} all-to-all(bf16[32,16,128]{2,1,0:T(8,128)(2,1)S(1)} %get-tuple-element.23), channel_id=1, replica_groups={{31,30,23,22,15,14,7,6,29,28,21,20,13,12,5,4,27,26,19,18,11,10,3,2,25,2..., dimensions={0} | all-to-all | bytes 262144 | tf_op jit(solution)/shard_map/all_to_all | solution.py:421
  41.0 0.2 edge_grad.1
  41.2 12.6 %all_to_all.22.in_ref = bf16[32,32,128]{2,1,0:T(8,128)(2,1)S(1)} all-to-all(bf16[32,32,128]{2,1,0:T(8,128)(2,1)S(1)} %edge_grad.1), channel_id=1, replica_groups={{31,30,23,22,15,14,7,6,29,28,21,20,13,12,5,4,27,26,19,18,11,10,3,2,25,2..., dimensions={0} | all-to-all | bytes 524288 | tf_op jit(solution)/shard_map/all_to_all | solution.py:421
  53.8 1.2 %input_grad.1 = bf16[4,128,128]{2,1,0:T(8,128)(2,1)} custom-call(bf16[32,32,128]{2,1,0:T(8,128)(2,1)S(1)} %all_to_all.22.in_ref, f32[4,128,512]{2,1,0:T(8,128)S(1)} %get-tuple-element.26.factors, f32[128,512]{1,0:T(8,128)S(1)} %get-tuple-element.27.normed_t, f32[1,512]{1,0:T(1,128)S(1)} %get-tuple-element.28.rstd_t, ...), custom_call_target="tpu_custom_call" | custom-call | flops 67108864 | bytes 2066432 | tf_op jit(solution)/shard_map/input_grad/pallas_call | solution.py:370
Async XLA Ops:
  2.3 7.5 %copy-start = (bf16[4,128,128]{2,1,0:T(8,128)(2,1)S(1)}, bf16[4,128,128]{2,1,0:T(8,128)(2,1)}, u32[]{:S(2)}) copy-start(bf16[4,128,128]{2,1,0:T(8,128)(2,1)} %act_ref.1) | copy-start | bytes 393220
  2.3 7.5 %copy-start.1 = (bf16[128,128]{1,0:T(8,128)(2,1)S(1)}, bf16[128,128]{1,0:T(8,128)(2,1)}, u32[]{:S(2)}) copy-start(bf16[128,128]{1,0:T(8,128)(2,1)} %wap.3) | copy-start | bytes 98308
  2.3 7.5 %copy-start.2 = (bf16[128,128]{1,0:T(8,128)(2,1)S(1)}, bf16[128,128]{1,0:T(8,128)(2,1)}, u32[]{:S(2)}) copy-start(bf16[128,128]{1,0:T(8,128)(2,1)} %wag.3) | copy-start | bytes 98308
  2.3 7.5 %copy-start.3 = (bf16[128,128]{1,0:T(8,128)(2,1)S(1)}, bf16[128,128]{1,0:T(8,128)(2,1)}, u32[]{:S(2)}) copy-start(bf16[128,128]{1,0:T(8,128)(2,1)} %wbp.3) | copy-start | bytes 98308
  2.3 7.5 %copy-start.4 = (bf16[128,128]{1,0:T(8,128)(2,1)S(1)}, bf16[128,128]{1,0:T(8,128)(2,1)}, u32[]{:S(2)}) copy-start(bf16[128,128]{1,0:T(8,128)(2,1)} %wbg.3) | copy-start | bytes 98308
  2.4 7.5 %copy-start.5 = (bf16[128,128]{1,0:T(8,128)(2,1)S(1)}, bf16[128,128]{1,0:T(8,128)(2,1)}, u32[]{:S(2)}) copy-start(bf16[128,128]{1,0:T(8,128)(2,1)} %w_gate.3) | copy-start | bytes 98308
  2.4 7.5 %copy-start.6 = (bf16[4,128,128]{2,1,0:T(8,128)(2,1)S(1)}, bf16[4,128,128]{2,1,0:T(8,128)(2,1)}, u32[]{:S(2)}) copy-start(bf16[4,128,128]{2,1,0:T(8,128)(2,1)} %grad_ref.1) | copy-start | bytes 393220
  2.4 7.5 %copy-start.7 = (bf16[128,128]{1,0:T(8,128)(2,1)S(1)}, bf16[128,128]{1,0:T(8,128)(2,1)}, u32[]{:S(2)}) copy-start(bf16[128,128]{1,0:T(8,128)(2,1)} %w_out.3) | copy-start | bytes 98308
  2.4 7.5 %copy-start.11 = (f32[128]{0:T(128)S(1)}, f32[128]{0:T(128)}, u32[]{:S(2)}) copy-start(f32[128]{0:T(128)} %param.23) | copy-start | bytes 1540
  2.4 7.5 %copy-start.12 = (f32[128]{0:T(128)S(1)}, f32[128]{0:T(128)}, u32[]{:S(2)}) copy-start(f32[128]{0:T(128)} %param.24) | copy-start | bytes 1540
  2.4 18.2 %all-to-all-start = ((bf16[32,32,128]{2,1,0:T(8,128)(2,1)}), bf16[32,32,128]{2,1,0:T(8,128)(2,1)S(1)}, u32[]{:S(2)}, u32[]{:S(2)}) async-start(bf16[32,32,128]{2,1,0:T(8,128)(2,1)} %edges.1), calls=%async_computation | async-start | bytes 524288 | tf_op jit(solution)/shard_map/all_to_all | solution.py:421
  9.7 0.7 %copy-start.8 = (s32[128]{0:T(128)S(1)}, s32[128]{0:T(128)}, u32[]{:S(2)}) copy-start(s32[128]{0:T(128)} %rows_ref.1) | copy-start | bytes 1540
  9.7 0.7 %copy-start.9 = (f32[128]{0:T(128)S(1)}, f32[128]{0:T(128)}, u32[]{:S(2)}) copy-start(f32[128]{0:T(128)} %param.16) | copy-start | bytes 1540
  9.8 0.7 %copy-start.10 = (f32[128]{0:T(128)S(1)}, f32[128]{0:T(128)}, u32[]{:S(2)}) copy-start(f32[128]{0:T(128)} %param.17) | copy-start | bytes 1540

commit v14 on v12

--- a/solution.py
+++ b/solution.py
@@ -162,13 +162,13 @@
 def mesh_order(blocks):
     count, *rest = blocks.shape
     split = blocks.reshape(count // LEVELS // CORES, LEVELS, CORES, *rest)
-    return falling(jnp.swapaxes(falling(split), 0, 1)).reshape(blocks.shape)
+    return jnp.swapaxes(falling(split), 0, 1).reshape(blocks.shape)
 
 
 def list_order(blocks):
     count, *rest = blocks.shape
     split = blocks.reshape(LEVELS, count // LEVELS // CORES, CORES, *rest)
-    return falling(jnp.swapaxes(falling(split), 0, 1)).reshape(blocks.shape)
+    return falling(jnp.swapaxes(split, 0, 1)).reshape(blocks.shape)
 
 
 def split_channels(blocks, own):
@@ -413,7 +413,7 @@
     listed = [
         quarter * span + pair * CORES + core
         for pair in reversed(range(span // CORES))
-        for quarter in reversed(range(LEVELS))
+        for quarter in range(LEVELS)
         for core in range(CORES)
     ]
 

time: 54.1 us -> 55.8 us (1.031)
  blocking collectives: 32.1 us -> 33 us
    all_to_all x3, blocking collectives: 32.1 us -> 33 us  [exchange(): lax.all_to_all(value, 'dap', split_axis=0, concat_axis=0, axis_index_grou...]
where the time goes in v14:
time: 55.8 us; the launch traced here: 55.3 us
  blocking collectives  33 us (59%)
  waiting for transfers between devices  8.42 us (15%)
  starting transfers between devices  7.31 us (13%)
  Pallas kernels  5.65 us (10%)
  local copies, waits for them, and re-layouts  0.63 us (1%)
    all_to_all x3, blocking collectives, exchange(): lax.all_to_all(value, 'dap', split_axis=0, concat_axis=0, axis_index_grou...  33 us
    all_to_all x1, waiting for transfers between devices, exchange(): lax.all_to_all(value, 'dap', split_axis=0, concat_axis=0, axis_index_grou...  8.42 us
    all_to_all x1, starting transfers between devices, exchange(): lax.all_to_all(value, 'dap', split_axis=0, concat_axis=0, axis_index_grou...  7.31 us
    pallas_call x6, Pallas kernels, call(): pl.pallas_call(kernel, name=name, out_shape=shapes, in_specs=[SMEM] * sca...  5.65 us
  transfers between devices with their start and end apart: 1, of which 1 were waited for; matrix products, arithmetic and copies ran while one was open for 0% of the time, Pallas kernels for 2%

profile of v14, /device:TPU:0, one launch (start us, length us, event | category | flops | bytes accessed | tf_op | source)
XLA Modules:
  0.0 55.3 jit_solution(9482906841409954117)
XLA Ops:
  0.0 2.3 %edges.1 = bf16[32,32,128]{2,1,0:T(8,128)(2,1)} custom-call(s32[1]{0:T(128)} %bitcast.me_ref, bf16[4,128,128]{2,1,0:T(8,128)(2,1)} %act_ref.1, f32[1,128]{1,0:T(1,128)} %bitcast.8, f32[1,128]{1,0:T(1,128)} %bitcast.10, s32[128]{0:T(128)} %rows_ref.1, s32[1,128]{1,0:T(1,128)} %bitcast.6, bf16[128,128]{1,0:T(8,128)(2,1)} %wap.3, bf16[128,128]{1,0:T(8,128)(2,1)} %wag.3, ...), custom_call_target="tpu_custom_call" | custom-call | flops 67108864 | bytes 526340 | tf_op jit(solution)/shard_map/edges/pallas_call | solution.py:370
  2.3 0.0 copy-start
  2.3 0.0 copy-start.1
  2.3 0.0 copy-start.2
  2.3 0.0 copy-start.3
  2.3 0.0 copy-start.4
  2.4 0.0 copy-start.5
  2.4 0.0 copy-start.6
  2.4 0.0 copy-start.7
  2.4 0.0 copy-start.11
  2.4 0.0 copy-start.12
  2.4 7.3 %all-to-all-start = ((bf16[32,32,128]{2,1,0:T(8,128)(2,1)}), bf16[32,32,128]{2,1,0:T(8,128)(2,1)S(1)}, u32[]{:S(2)}, u32[]{:S(2)}) async-start(bf16[32,32,128]{2,1,0:T(8,128)(2,1)} %edges.1), calls=%async_computation | async-start | bytes 524288 | tf_op jit(solution)/shard_map/all_to_all | solution.py:421
  9.7 0.0 copy-start.8
  9.7 0.0 copy-start.9
  9.8 0.0 copy-start.10
  9.8 0.0 copy-done
  9.8 0.0 copy-done.1
  9.8 0.0 copy-done.2
  9.8 0.0 copy-done.3
  9.8 0.0 copy-done.4
  9.8 0.0 copy-done.5
  9.8 0.0 copy-done.6
  9.8 0.0 copy-done.7
  9.8 0.0 copy-done.11
  9.9 0.0 copy-done.12
  9.9 0.5 copy-done.8
  10.4 0.0 copy-done.9
  10.4 0.0 copy-done.10
  10.4 1.2 %gates.1 = (f32[4,128,512]{2,1,0:T(8,128)S(1)}, f32[128,512]{1,0:T(8,128)S(1)}, f32[1,512]{1,0:T(1,128)S(1)}, f32[128,128]{1,0:T(8,128)S(1)}, f32[512,128]{1,0:T...) custom-call(s32[1]{0:T(128)} %bitcast.me_ref, s32[128]{0:T(128)S(1)} %copy-done.8, ...), custom_call_target="tpu_custom_call" | custom-call | flops 100663296 | bytes 2495492 | tf_op jit(solution)/shard_map/gates/pallas_call | solution.py:370
  11.7 8.4 %all-to-all-done.in_ref = bf16[32,32,128]{2,1,0:T(8,128)(2,1)S(1)} async-done(((bf16[32,32,128]{2,1,0:T(8,128)(2,1)}), bf16[32,32,128]{2,1,0:T(8,128)(2,1)S(1)}, u32[]{:S(2)}, u32[]{:S(2)}) %all-to-all-start) | async-done | bytes 262176 | tf_op jit(solution)/shard_map/all_to_all | solution.py:421
  20.1 0.2 triangle.1
  20.3 10.8 %all_to_all.20.tri_ref = bf16[32,16,128]{2,1,0:T(8,128)(2,1)S(1)} all-to-all(bf16[32,16,128]{2,1,0:T(8,128)(2,1)S(1)} %get-tuple-element.19), channel_id=1, replica_groups={{6,7,14,15,22,23,30,31,4,5,12,13,20,21,28,29,2,3,10,11,18,19,26,27,0,1,..., dimensions={0} | all-to-all | bytes 262144 | tf_op jit(solution)/shard_map/all_to_all | solution.py:421
  31.1 0.5 norm.1
  31.6 10.2 %all_to_all.21.in_ref = bf16[32,16,128]{2,1,0:T(8,128)(2,1)S(1)} all-to-all(bf16[32,16,128]{2,1,0:T(8,128)(2,1)S(1)} %get-tuple-element.23), channel_id=1, replica_groups={{6,7,14,15,22,23,30,31,4,5,12,13,20,21,28,29,2,3,10,11,18,19,26,27,0,1,..., dimensions={0} | all-to-all | bytes 262144 | tf_op jit(solution)/shard_map/all_to_all | solution.py:421
  41.8 0.2 edge_grad.1
  42.0 12.1 %all_to_all.22.in_ref = bf16[32,32,128]{2,1,0:T(8,128)(2,1)S(1)} all-to-all(bf16[32,32,128]{2,1,0:T(8,128)(2,1)S(1)} %edge_grad.1), channel_id=1, replica_groups={{6,7,14,15,22,23,30,31,4,5,12,13,20,21,28,29,2,3,10,11,18,19,26,27,0,1,..., dimensions={0} | all-to-all | bytes 524288 | tf_op jit(solution)/shard_map/all_to_all | solution.py:421
  54.1 1.2 %input_grad.1 = bf16[4,128,128]{2,1,0:T(8,128)(2,1)} custom-call(bf16[32,32,128]{2,1,0:T(8,128)(2,1)S(1)} %all_to_all.22.in_ref, f32[4,128,512]{2,1,0:T(8,128)S(1)} %get-tuple-element.26.factors, f32[128,512]{1,0:T(8,128)S(1)} %get-tuple-element.27.normed_t, f32[1,512]{1,0:T(1,128)S(1)} %get-tuple-element.28.rstd_t, ...), custom_call_target="tpu_custom_call" | custom-call | flops 67108864 | bytes 2066432 | tf_op jit(solution)/shard_map/input_grad/pallas_call | solution.py:370
Async XLA Ops:
  2.3 7.5 %copy-start = (bf16[4,128,128]{2,1,0:T(8,128)(2,1)S(1)}, bf16[4,128,128]{2,1,0:T(8,128)(2,1)}, u32[]{:S(2)}) copy-start(bf16[4,128,128]{2,1,0:T(8,128)(2,1)} %act_ref.1) | copy-start | bytes 393220
  2.3 7.5 %copy-start.1 = (bf16[128,128]{1,0:T(8,128)(2,1)S(1)}, bf16[128,128]{1,0:T(8,128)(2,1)}, u32[]{:S(2)}) copy-start(bf16[128,128]{1,0:T(8,128)(2,1)} %wap.3) | copy-start | bytes 98308
  2.3 7.5 %copy-start.2 = (bf16[128,128]{1,0:T(8,128)(2,1)S(1)}, bf16[128,128]{1,0:T(8,128)(2,1)}, u32[]{:S(2)}) copy-start(bf16[128,128]{1,0:T(8,128)(2,1)} %wag.3) | copy-start | bytes 98308
  2.3 7.5 %copy-start.3 = (bf16[128,128]{1,0:T(8,128)(2,1)S(1)}, bf16[128,128]{1,0:T(8,128)(2,1)}, u32[]{:S(2)}) copy-start(bf16[128,128]{1,0:T(8,128)(2,1)} %wbp.3) | copy-start | bytes 98308
  2.3 7.5 %copy-start.4 = (bf16[128,128]{1,0:T(8,128)(2,1)S(1)}, bf16[128,128]{1,0:T(8,128)(2,1)}, u32[]{:S(2)}) copy-start(bf16[128,128]{1,0:T(8,128)(2,1)} %wbg.3) | copy-start | bytes 98308
  2.4 7.5 %copy-start.5 = (bf16[128,128]{1,0:T(8,128)(2,1)S(1)}, bf16[128,128]{1,0:T(8,128)(2,1)}, u32[]{:S(2)}) copy-start(bf16[128,128]{1,0:T(8,128)(2,1)} %w_gate.3) | copy-start | bytes 98308
  2.4 7.5 %copy-start.6 = (bf16[4,128,128]{2,1,0:T(8,128)(2,1)S(1)}, bf16[4,128,128]{2,1,0:T(8,128)(2,1)}, u32[]{:S(2)}) copy-start(bf16[4,128,128]{2,1,0:T(8,128)(2,1)} %grad_ref.1) | copy-start | bytes 393220
  2.4 7.5 %copy-start.7 = (bf16[128,128]{1,0:T(8,128)(2,1)S(1)}, bf16[128,128]{1,0:T(8,128)(2,1)}, u32[]{:S(2)}) copy-start(bf16[128,128]{1,0:T(8,128)(2,1)} %w_out.3) | copy-start | bytes 98308
  2.4 7.5 %copy-start.11 = (f32[128]{0:T(128)S(1)}, f32[128]{0:T(128)}, u32[]{:S(2)}) copy-start(f32[128]{0:T(128)} %param.23) | copy-start | bytes 1540
  2.4 7.5 %copy-start.12 = (f32[128]{0:T(128)S(1)}, f32[128]{0:T(128)}, u32[]{:S(2)}) copy-start(f32[128]{0:T(128)} %param.24) | copy-start | bytes 1540
  2.4 17.7 %all-to-all-start = ((bf16[32,32,128]{2,1,0:T(8,128)(2,1)}), bf16[32,32,128]{2,1,0:T(8,128)(2,1)S(1)}, u32[]{:S(2)}, u32[]{:S(2)}) async-start(bf16[32,32,128]{2,1,0:T(8,128)(2,1)} %edges.1), calls=%async_computation | async-start | bytes 524288 | tf_op jit(solution)/shard_map/all_to_all | solution.py:421
  9.7 0.7 %copy-start.8 = (s32[128]{0:T(128)S(1)}, s32[128]{0:T(128)}, u32[]{:S(2)}) copy-start(s32[128]{0:T(128)} %rows_ref.1) | copy-start | bytes 1540
  9.7 0.7 %copy-start.9 = (f32[128]{0:T(128)S(1)}, f32[128]{0:T(128)}, u32[]{:S(2)}) copy-start(f32[128]{0:T(128)} %param.16) | copy-start | bytes 1540
  9.8 0.7 %copy-start.10 = (f32[128]{0:T(128)S(1)}, f32[128]{0:T(128)}, u32[]{:S(2)}) copy-start(f32[128]{0:T(128)} %param.17) | copy-start | bytes 1540
